TPU v7x, 256 devices: a whole 4x4x8 slice. The times are simulated.
256 devices in a mesh: cfg: 2 (over z_lo), ta: 4 (over y), ha: 4 (over x), wa: 8 (over z_hi, core).
Axes of the slice: x: 4, y: 4, z: 8 (z_hi: 4, z_lo: 2; z = z_hi * 2 + z_lo), core: 2. Of those that a mesh axis runs over, the one named last changes fastest.
Arguments:
- video_query: bfloat16 [2, 24, 32, 64, 1536], P('cfg', 'ta', 'ha', 'wa'), may hold values from -13.5 to 13.5
- video_key: bfloat16 [2, 24, 32, 64, 1536], P('cfg', 'ta', 'ha', 'wa'), may hold values from -13.5 to 13.5
- video_value: bfloat16 [2, 24, 32, 64, 1536], P('cfg', 'ta', 'ha', 'wa'), may hold values from -6 to 6
- text_query: bfloat16 [2, 128, 1536], P('cfg'), may hold values from -13.5 to 13.5
- text_key: bfloat16 [2, 128, 1536], P('cfg', ('ta', 'ha', 'wa')), may hold values from -9.5625 to 9.5625
- text_value: bfloat16 [2, 128, 1536], P('cfg', ('ta', 'ha', 'wa')), may hold values from -6 to 6
- text_count: int32 [2], P('cfg'), may hold values from 1 to 128, as said below
- head_windows: int32 [12, 3], replicated, may hold values from 1 to 3, as said below
- hidden_state: bfloat16 [2, 24, 32, 64, 3072], P('cfg', 'ta', 'ha', 'wa'), may hold values from -6 to 6
- out_weight: bfloat16 [1536, 3072], P('cfg'), may hold values from -0.15625 to 0.15625
- final_weight: bfloat16 [3072, 64], replicated, may hold values from -0.109375 to 0.109375
- modulation: float32 [2, 3, 3072], P('cfg'), may hold values from -4 to 4
- guidance: float32 [1], replicated, may hold values from 1.5 to 3
Outputs:
- patches: float32 [24, 32, 4096], P('ta', ('ha', 'cfg'), 'wa')
- text_attended: bfloat16 [2, 128, 1536], P('cfg')
Inputs may be any that keep to these rules, and one draw needn't show every extreme that they name: `text_count`: branch 0 uses all 128 text positions; branch 1 uses at most 32. `head_windows`: every entry is 1 or 3; the columns are time, rows and columns. Exactly 3 heads have a 3 in some column, the others 1 in all three; some head has 3 in all three.
All inputs are finite; a program needn't handle non-finite values.
Results may differ from a plain program's by a relative error of at most 0.0034.
Values may be sent and summed in bfloat16 or wider, within the bound.
No kernel may reach another device: no remote copies, remote signals or barrier semaphores. Data moves between devices by JAX's collectives and lax.ppermute only.
A program may use at most 320 MiB of HBM per device.

v0:
```python
import math

import jax
import jax.numpy as jnp
from jax import lax
from jax.sharding import PartitionSpec as P

TILE_T = 6


def padded(cells, sides, width):
    for axis, dim in sides:
        count = lax.axis_size(axis)
        ends = count - 1
        head = lax.slice_in_dim(cells, 0, width, axis=dim)
        tail = lax.slice_in_dim(cells, cells.shape[dim] - width, cells.shape[dim], axis=dim)
        cells = jnp.concatenate(
            [
                lax.ppermute(tail, axis, [(i, (i + 1) % count) for i in range(ends)]),
                cells,
                lax.ppermute(head, axis, [((i + 1) % count, i) for i in range(ends)]),
            ],
            axis=dim,
        )
    return cells


def joint_attention(query, keys, values, keep, text_keys, text_values, text_valid, scale):
    region_scores = (
        jnp.einsum("nqd,nkd->nqk", query, keys, preferred_element_type=jnp.float32) * scale
    )
    text_scores = (
        jnp.einsum("nqd,ld->nql", query, text_keys, preferred_element_type=jnp.float32) * scale
    )
    region_held = jnp.where(keep[:, None, :], region_scores, -jnp.inf)
    text_held = jnp.where(text_valid, text_scores, -jnp.inf)
    peak = jnp.maximum(
        jnp.max(region_held, axis=-1, keepdims=True), jnp.max(text_held, axis=-1, keepdims=True)
    )
    region_weights = jnp.exp(region_held - peak)
    text_weights = jnp.exp(text_held - peak)
    total = jnp.sum(region_weights, axis=-1, keepdims=True) + jnp.sum(
        text_weights, axis=-1, keepdims=True
    )
    mixed = jnp.einsum(
        "nqk,nkd->nqd",
        region_weights.astype(jnp.bfloat16),
        values,
        preferred_element_type=jnp.float32,
    )
    mixed = mixed + jnp.einsum(
        "nql,ld->nqd",
        text_weights.astype(jnp.bfloat16),
        text_values,
        preferred_element_type=jnp.float32,
    )
    return mixed / total


def local(
    video_query,
    video_key,
    video_value,
    text_query,
    text_key,
    text_value,
    text_count,
    head_windows,
    hidden_state,
    out_weight,
    final_weight,
    modulation,
    guidance,
):
    frames, rows, cols, width = video_query.shape[1:]
    heads = head_windows.shape[0]
    depth = width // heads
    blocks = frames // TILE_T
    tile_tokens = TILE_T * rows * cols
    tokens = frames * rows * cols
    scale = 1.0 / math.sqrt(depth)
    wide_count = heads // 4
    is_wide = (jnp.max(head_windows, axis=1) > 1).astype(jnp.int32)
    chosen = jnp.argsort(-is_wide, stable=True)[:wide_count]
    text_pair = jnp.concatenate((text_key[0], text_value[0]), axis=-1)
    text_all = lax.all_gather(text_pair, ("ta", "ha", "wa"), axis=0, tiled=True)
    text_len = text_all.shape[0]
    text_all = text_all.reshape(text_len, 2, heads, depth)
    text_keys = text_all[:, 0]
    text_values = text_all[:, 1]
    text_valid = jnp.arange(text_len) < text_count[0]
    key_heads = video_key[0].reshape(frames, rows, cols, heads, depth)
    value_heads = video_value[0].reshape(frames, rows, cols, heads, depth)
    queries = video_query[0].reshape(blocks, tile_tokens, heads, depth)
    own_keys = key_heads.reshape(blocks, tile_tokens, heads, depth)
    own_values = value_heads.reshape(blocks, tile_tokens, heads, depth)
    whole_tile = jnp.ones((blocks, tile_tokens), jnp.bool_)
    local_heads = jax.vmap(joint_attention, in_axes=(2, 2, 2, None, 1, 1, None, None))(
        queries, own_keys, own_values, whole_tile, text_keys, text_values, text_valid, scale
    )
    offsets = jnp.arange(3) - 1
    time_at = lax.axis_index("ta") * blocks + jnp.arange(blocks)[:, None] + offsets[None, :]
    time_in = (time_at >= 0) & (time_at < lax.axis_size("ta") * blocks)
    row_at = lax.axis_index("ha") + offsets
    row_in = (row_at >= 0) & (row_at < lax.axis_size("ha"))
    col_at = lax.axis_index("wa") + offsets
    col_in = (col_at >= 0) & (col_at < lax.axis_size("wa"))

    def wide_attention(extended, head):
        stacked = jnp.stack(
            [extended[time_step * TILE_T : time_step * TILE_T + frames] for time_step in range(3)]
        )
        region = (
            stacked.reshape(3, blocks, TILE_T, 3, rows, 3, cols, 2 * depth)
            .transpose(1, 0, 3, 5, 2, 4, 6, 7)
            .reshape(blocks, 27 * tile_tokens, 2 * depth)
        )
        window = lax.dynamic_index_in_dim(head_windows, head, 0, keepdims=False)
        reach = jnp.abs(offsets)[None, :] <= (window // 2)[:, None]
        time_ok = time_in & reach[0][None, :]
        row_ok = row_in & reach[1]
        col_ok = col_in & reach[2]
        tile_ok = (
            time_ok[:, :, None, None] & row_ok[None, None, :, None] & col_ok[None, None, None, :]
        )
        keep = jnp.repeat(tile_ok.reshape(blocks, 27), tile_tokens, axis=1)
        query = lax.dynamic_index_in_dim(queries, head, 2, keepdims=False)
        text_key_head = lax.dynamic_index_in_dim(text_keys, head, 1, keepdims=False)
        text_value_head = lax.dynamic_index_in_dim(text_values, head, 1, keepdims=False)
        return joint_attention(
            query,
            region[..., :depth],
            region[..., depth:],
            keep,
            text_key_head,
            text_value_head,
            text_valid,
            scale,
        )

    def head_pass(head):
        pair = jnp.concatenate(
            (
                lax.dynamic_index_in_dim(key_heads, head, 3, keepdims=False),
                lax.dynamic_index_in_dim(value_heads, head, 3, keepdims=False),
            ),
            axis=-1,
        )
        timed = padded(pair, (("ta", 0),), TILE_T)
        extended = padded(timed, (("ha", 1), ("wa", 2)), rows)
        return wide_attention(extended, head)

    wide_out = lax.map(head_pass, chosen)
    every_head = local_heads.at[chosen].set(wide_out)
    attended = every_head.transpose(1, 2, 0, 3).reshape(tokens, width).astype(jnp.bfloat16)
    text_queries = text_query[0].reshape(text_len, heads, depth)
    tile_scores = (
        jnp.einsum("lhd,nkhd->nhlk", text_queries, own_keys, preferred_element_type=jnp.float32)
        * scale
    )
    tile_peak = jnp.max(tile_scores, axis=-1)
    tile_weights = jnp.exp(tile_scores - tile_peak[..., None])
    tile_total = jnp.sum(tile_weights, axis=-1)
    tile_sum = jnp.einsum(
        "nhlk,nkhd->nhld",
        tile_weights.astype(jnp.bfloat16),
        own_values,
        preferred_element_type=jnp.float32,
    )
    own_top = jnp.max(tile_peak, axis=0)
    factor = jnp.exp(tile_peak - own_top)
    part = (
        own_top,
        jnp.sum(tile_total * factor, axis=0),
        jnp.sum(tile_sum * factor[..., None], axis=0),
    )
    cross_scores = (
        jnp.einsum("lhd,khd->hlk", text_queries, text_keys, preferred_element_type=jnp.float32)
        * scale
    )
    cross_held = jnp.where(text_valid, cross_scores, -jnp.inf)
    cross_peak = jnp.max(cross_held, axis=-1)
    cross_weights = jnp.exp(cross_held - cross_peak[..., None])
    cross_total = jnp.sum(cross_weights, axis=-1)
    cross_sum = jnp.einsum(
        "hlk,khd->hld",
        cross_weights.astype(jnp.bfloat16),
        text_values,
        preferred_element_type=jnp.float32,
    )
    top_all = jnp.maximum(lax.pmax(part[0], ("ta", "ha", "wa")), cross_peak)
    rescale = jnp.exp(part[0] - top_all)
    total_rows, sum_rows = (
        lax.psum_scatter(part[1] * rescale, ("ta", "ha", "wa"), scatter_dimension=1, tiled=True),
        lax.psum_scatter(
            part[2] * rescale[..., None], ("ta", "ha", "wa"), scatter_dimension=1, tiled=True
        ),
    )
    row_count = total_rows.shape[1]
    first_row = lax.axis_index(("ta", "ha", "wa")) * row_count
    top_rows = lax.dynamic_slice_in_dim(top_all, first_row, row_count, 1)
    cross_factor = jnp.exp(lax.dynamic_slice_in_dim(cross_peak, first_row, row_count, 1) - top_rows)
    total_rows = total_rows + cross_factor * lax.dynamic_slice_in_dim(
        cross_total, first_row, row_count, 1
    )
    sum_rows = sum_rows + cross_factor[..., None] * lax.dynamic_slice_in_dim(
        cross_sum, first_row, row_count, 1
    )
    finished = (
        (sum_rows / total_rows[..., None])
        .transpose(1, 0, 2)
        .reshape(row_count, width)
        .astype(jnp.bfloat16)
    )
    text_out = lax.all_gather(finished, ("ta", "ha", "wa"), axis=0, tiled=True)
    model_width = out_weight.shape[1]
    projected = jnp.dot(
        attended,
        lax.all_gather(out_weight, "cfg", axis=0, tiled=True),
        preferred_element_type=jnp.float32,
    )
    updated = (
        hidden_state[0].reshape(tokens, model_width).astype(jnp.float32)
        + modulation[0, 0] * projected
    )
    mean = jnp.mean(updated, axis=-1, keepdims=True)
    centered = updated - mean
    variance = jnp.mean(centered * centered, axis=-1, keepdims=True)
    normed = centered * lax.rsqrt(variance + 1e-06) * (1.0 + modulation[0, 2]) + modulation[0, 1]
    branch_out = jnp.dot(
        normed.astype(jnp.bfloat16), final_weight, preferred_element_type=jnp.float32
    )
    channels = final_weight.shape[1]
    branches = lax.axis_size("cfg")
    halves = branch_out.reshape(frames, branches, rows // branches, cols * channels)
    paired = lax.all_to_all(halves, "cfg", split_axis=1, concat_axis=1, tiled=True)
    conditional = paired[:, 0]
    unconditional = paired[:, 1]
    guided = unconditional + guidance[0] * (conditional - unconditional)
    return (guided, text_out[None])


def solution(mesh):
    in_specs = (
        P("cfg", "ta", "ha", "wa", None),
        P("cfg", "ta", "ha", "wa", None),
        P("cfg", "ta", "ha", "wa", None),
        P("cfg", None, None),
        P("cfg", ("ta", "ha", "wa"), None),
        P("cfg", ("ta", "ha", "wa"), None),
        P("cfg"),
        P(),
        P("cfg", "ta", "ha", "wa", None),
        P("cfg", None),
        P(),
        P("cfg", None, None),
        P(),
    )
    out_specs = (P("ta", ("ha", "cfg"), "wa"), P("cfg", None, None))
    return jax.shard_map(local, mesh=mesh, in_specs=in_specs, out_specs=out_specs, check_vma=False)
```

profile of v0, /device:TPU:1, one launch (start us, length us, event | category | flops | bytes accessed | tf_op | source)
XLA Modules:
  0.0 2206.8 jit_solution(4390434408608700228)
XLA Ops:
  8.9 201.1 %all-gather = bf16[128,1,3072]{2,1,0:T(2,128)(2,1)S(1)} all-gather(bf16[1,1,3072]{2,1,0:T(2,128)(2,1)S(1)} %maximum_bitcast_fusion), channel_id=1, replica_groups=mesh['cfg'=2,'ta'=4,'ha'=4,'wa'=8] {'ta','ha','wa'}, dimensions={0}, use_global_device_ids=true | all-gather | bytes 792576 | tf_op jit(solution)/shard_map/all_gather | solution.py:86
  219.3 347.2 %pmax.7 = f32[12,128]{1,0:T(8,128)} all-reduce(f32[12,128]{1,0:T(8,128)S(1)} %get-tuple-element.340), channel_id=1, replica_groups=mesh['cfg'=2,'ta'=4,'ha'=4,'wa'=8] {'ta','ha','wa'}, use_global_device_ids=true, to_apply=%region_16.17 | all-reduce | flops 1536 | bytes 12288 | tf_op jit(solution)/shard_map/pmax | solution.py:191
  595.8 677.4 %all-reduce.1 = f32[12,128]{0,1:T(8,128)} all-reduce(f32[12,128]{0,1:T(8,128)} %copy.150), channel_id=3, replica_groups=mesh['cfg'=2,'ta'=4,'ha'=4,'wa'=8] {'ta','ha','wa'}, use_global_device_ids=true, to_apply=%region_20.21.clone | all-reduce | flops 1536 | bytes 12288
  1292.4 276.3 %while.13 = (s32[]{:T(128)}, f32[3,1,384,128]{3,2,1,0:T(8,128)}, s32[3]{0:T(128)S(1)}, s32[12,3]{1,0:T(8,128)S(1)}, bf16[1,384,12,128]{3,1,2,0:T(8,128)(2,1)}, /...) while((s32[]{:T(128)}, f32[3,1,384,128]{3,2,1,0:T(8,128)}, ...), condition=%wide.region_11.12_spmd.clone, body=%wide.region_6.11_spmd.clone.sunk | while | flops 2153053696 | bytes 125374176 | solution.py:153
  1316.3 12.8 collective-permute-start.4
  1335.3 16.4 collective-permute-done.4
  1351.7 7.3 pad_maximum_fusion.13
  1360.8 7.9 fusion.126
  1368.7 7.8 fusion.129
  1376.5 7.2 fusion.128
  1412.4 10.3 collective-permute-start.5
  1427.0 22.7 %collective-permute-done.4 = bf16[18,24,8,256]{3,2,1,0:T(8,128)(2,1)} collective-permute-done((bf16[18,24,8,256]{3,2,1,0:T(8,128)(2,1)S(1)}, bf16[18,24,8,256]{3,2,1,0:T(8,128)(2,1)}, u32[]{:S(2)}, u32[]{:S(2)}) %collective-permute-start.4) | collective-permute-done | bytes 1769504 | tf_op jit(solution)/shard_map/while/body/eval_jaxpr/ppermute | solution.py:21
  1449.7 7.3 pad_maximum_fusion.13
  1458.8 7.9 fusion.126
  1466.7 7.8 fusion.129
  1474.5 7.2 fusion.128
  1519.6 14.8 collective-permute-done.4
  1535.0 7.3 pad_maximum_fusion.13
  1544.1 7.9 fusion.126
  1552.0 7.8 fusion.129
  1559.8 7.2 fusion.128
  1579.0 407.9 %all-reduce.4.cloned.1.call-done = f32[12,128,128]{2,1,0:T(8,128)} async-done(((f32[12,128,128]{2,1,0:T(8,128)}), f32[12,128,128]{2,1,0:T(8,128)}) %all-reduce.4.cloned.1.call-update) | async-done | bytes 786448
  1988.4 9.0 fusion.101
  2003.0 194.9 %all-gather.1 = bf16[128,1,1536]{2,1,0:T(2,128)(2,1)S(1)} all-gather(bf16[1,1,1536]{2,1,0:T(2,128)(2,1)S(1)} %convert_bitcast_fusion.1), channel_id=1, replica_groups=mesh['cfg'=2,'ta'=4,'ha'=4,'wa'=8] {'ta','ha','wa'}, dimensions={0}, use_global_device_ids=true | all-gather | bytes 396288 | tf_op jit(solution)/shard_map/all_gather | solution.py:215
  (248 shorter events, 178.3 us)
Async XLA Ops:
  8.0 1990.0 %copy-start = (bf16[3072,64]{0,1:T(8,128)(2,1)S(1)}, bf16[3072,64]{0,1:T(8,128)(2,1)}, u32[]{:S(2)}) copy-start(bf16[3072,64]{0,1:T(8,128)(2,1)} %param.25) | copy-start | bytes 1179652
  8.0 1978.8 %all-reduce.4.cloned.1.call-start = ((), (), s32[]{:S(2)}) async-start(), calls=%async_computation.2 | async-start | bytes 1572864
  211.7 1078.2 %copy-start.6 = (bf16[128,1,3072]{0,2,1:T(8,128)(2,1)}, bf16[128,1,3072]{0,2,1:T(8,128)(2,1)S(1)}, u32[]{:S(2)}) copy-start(bf16[128,1,3072]{0,2,1:T(8,128)(2,1)S(1)} %copy.129) | copy-start | bytes 2359300
  578.2 1410.2 %all-gather.4.cloned.1.call-start = ((), (), s32[]{:S(2)}) async-start(), calls=%async_computation.1 | async-start | bytes 14155776 | tf_op jit(solution)/shard_map/all_gather | solution.py:219
  595.1 687.0 %copy-start.24 = (s32[12,3]{0,1:T(4,128)S(1)}, s32[12,3]{0,1:T(4,128)}, u32[]{:S(2)}) copy-start(s32[12,3]{0,1:T(4,128)} %param.22) | copy-start | bytes 436
  1296.0 6.4 collective-permute-start
  1297.3 6.6 collective-permute-start.1
  1303.9 11.0 collective-permute-start.2
  1305.2 10.9 collective-permute-start.3
  1316.3 35.4 %collective-permute-start.4 = (bf16[18,24,8,256]{3,2,1,0:T(8,128)(2,1)S(1)}, bf16[18,24,8,256]{3,2,1,0:T(8,128)(2,1)}, u32[]{:S(2)}, u32[]{:S(2)}) collective-permute-start(bf16[18,24,8,256]{3,2,1,0:T(8,128)(2,1)S(1)} %pad_maximum_fusion.12), channel_id=1, source_target_pairs={{1,0},{2,1},{3,2},{4,3},{5,4},{6,5},{7,6},{9,8},{10,9},{11,10},{12... | collective-permute-start | bytes 5308424 | tf_op jit(solution)/shard_map/while/body/eval_jaxpr/ppermute | solution.py:21
  1329.1 22.6 %collective-permute-start.5 = (bf16[18,24,8,256]{3,2,1,0:T(8,128)(2,1)S(1)}, bf16[18,24,8,256]{3,2,1,0:T(8,128)(2,1)}, u32[]{:S(2)}, u32[]{:S(2)}) collective-permute-start(bf16[18,24,8,256]{3,2,1,0:T(8,128)(2,1)S(1)} %pad_maximum_fusion.12), channel_id=1, source_target_pairs={{0,1},{1,2},{2,3},{3,4},{4,5},{5,6},{6,7},{8,9},{9,10},{10,11},{11... | collective-permute-start | bytes 5308424 | tf_op jit(solution)/shard_map/while/body/eval_jaxpr/ppermute | solution.py:19
  1389.0 6.8 collective-permute-start
  1390.3 7.0 collective-permute-start.1
  1397.3 11.4 collective-permute-start.2
  1398.6 11.6 collective-permute-start.3
  1410.5 39.2 %collective-permute-start.4 = (bf16[18,24,8,256]{3,2,1,0:T(8,128)(2,1)S(1)}, bf16[18,24,8,256]{3,2,1,0:T(8,128)(2,1)}, u32[]{:S(2)}, u32[]{:S(2)}) collective-permute-start(bf16[18,24,8,256]{3,2,1,0:T(8,128)(2,1)S(1)} %pad_maximum_fusion.12), channel_id=1, source_target_pairs={{1,0},{2,1},{3,2},{4,3},{5,4},{6,5},{7,6},{9,8},{10,9},{11,10},{12... | collective-permute-start | bytes 5308424 | tf_op jit(solution)/shard_map/while/body/eval_jaxpr/ppermute | solution.py:21
  1412.4 37.3 %collective-permute-start.5 = (bf16[18,24,8,256]{3,2,1,0:T(8,128)(2,1)S(1)}, bf16[18,24,8,256]{3,2,1,0:T(8,128)(2,1)}, u32[]{:S(2)}, u32[]{:S(2)}) collective-permute-start(bf16[18,24,8,256]{3,2,1,0:T(8,128)(2,1)S(1)} %pad_maximum_fusion.12), channel_id=1, source_target_pairs={{0,1},{1,2},{2,3},{3,4},{4,5},{5,6},{6,7},{8,9},{9,10},{10,11},{11... | collective-permute-start | bytes 5308424 | tf_op jit(solution)/shard_map/while/body/eval_jaxpr/ppermute | solution.py:19
  1487.0 7.2 collective-permute-start
  1488.3 7.5 collective-permute-start.1
  1495.9 11.3 collective-permute-start.2
  1497.2 11.5 collective-permute-start.3
  1508.9 25.5 %collective-permute-start.4 = (bf16[18,24,8,256]{3,2,1,0:T(8,128)(2,1)S(1)}, bf16[18,24,8,256]{3,2,1,0:T(8,128)(2,1)}, u32[]{:S(2)}, u32[]{:S(2)}) collective-permute-start(bf16[18,24,8,256]{3,2,1,0:T(8,128)(2,1)S(1)} %pad_maximum_fusion.12), channel_id=1, source_target_pairs={{1,0},{2,1},{3,2},{4,3},{5,4},{6,5},{7,6},{9,8},{10,9},{11,10},{12... | collective-permute-start | bytes 5308424 | tf_op jit(solution)/shard_map/while/body/eval_jaxpr/ppermute | solution.py:21
  1510.9 24.1 %collective-permute-start.5 = (bf16[18,24,8,256]{3,2,1,0:T(8,128)(2,1)S(1)}, bf16[18,24,8,256]{3,2,1,0:T(8,128)(2,1)}, u32[]{:S(2)}, u32[]{:S(2)}) collective-permute-start(bf16[18,24,8,256]{3,2,1,0:T(8,128)(2,1)S(1)} %pad_maximum_fusion.12), channel_id=1, source_target_pairs={{0,1},{1,2},{2,3},{3,4},{4,5},{5,6},{6,7},{8,9},{9,10},{10,11},{11... | collective-permute-start | bytes 5308424 | tf_op jit(solution)/shard_map/while/body/eval_jaxpr/ppermute | solution.py:19
  1999.7 199.0 %all-to-all-start = ((f32[6,2,4,512]{3,2,0,1:T(4,128)}), f32[6,2,4,512]{3,2,0,1:T(4,128)S(1)}, u32[]{:S(2)}, u32[]{:S(2)}) async-start(f32[6,2,4,512]{3,2,0,1:T(4,128)} %copy.142), calls=%async_computation | async-start | bytes 196608 | tf_op jit(solution)/shard_map/all_to_all | solution.py:236
  (40 other events, 1561.2 us)
Sparse Core Ops, SparseCore 0:
  578.3 1408.4 all-reduce.3
Sparse Core Ops, SparseCore 1:
  580.5 116.7 all-gather.3
where the time goes:
time: 2210 us
  blocking collectives  1420 us (64%)
  waiting for transfers between devices  491 us (22%)
  matrix products  84.4 us (4%)
  starting transfers between devices  71.5 us (3%)
  other arithmetic  68 us (3%)
  local copies, waits for them, and re-layouts  47.6 us (2%)
    unnamed x1, blocking collectives  677 us
    unnamed x3, waiting for transfers between devices  408 us
    pmax x1, blocking collectives, local(): top_all = jnp.maximum(lax.pmax(part[0], ('ta', 'ha', 'wa')), cross_peak)  347 us
    all_gather x1, blocking collectives, local(): text_all = lax.all_gather(text_pair, ('ta', 'ha', 'wa'), axis=0, tiled=True)  201 us
    all_gather x1, blocking collectives, local(): text_out = lax.all_gather(finished, ('ta', 'ha', 'wa'), axis=0, tiled=True)  195 us
    ppermute x9, waiting for transfers between devices, padded(): lax.ppermute(head, axis, [((i + 1) % count, i) for i in range(ends)])  73.6 us
  transfers between devices with their start and end apart: 21, of which 17 were waited for; matrix products, arithmetic and copies ran while one was open for 8% of the time, Pallas kernels for 0%

commit v1 on v0

v1 whole, which is shorter than its diff:
```python
import functools
import math

import jax
import jax.numpy as jnp
from jax import lax
from jax.experimental import pallas as pl
from jax.experimental.pallas import tpu as pltpu
from jax.sharding import Mesh
from jax.sharding import PartitionSpec as P

DEPTH = 128
WIDE = 3
NEVER = -(2.0**100)
CHIPS = ("ta", "ha", "zh")
PLACES = 9
LOG2E = math.log2(math.e)
SCALE = LOG2E / math.sqrt(DEPTH)
MIB = 1024 * 1024

VMEM = pl.BlockSpec(memory_space=pltpu.VMEM)
SMEM = pl.BlockSpec(memory_space=pltpu.SMEM)
HBM = pl.BlockSpec(memory_space=pl.ANY)


def call(body, out_shape, in_specs, out_specs, scratch, flops, moved, *operands):
    return pl.pallas_call(
        body,
        grid=(1,),
        out_shape=out_shape,
        in_specs=in_specs,
        out_specs=out_specs,
        scratch_shapes=scratch,
        compiler_params=pltpu.CompilerParams(vmem_limit_bytes=56 * MIB),
        cost_estimate=pl.CostEstimate(flops=flops, bytes_accessed=moved, transcendentals=0),
    )(*operands)


def lanes(head):
    return pl.ds(pl.multiple_of(head * DEPTH, DEPTH), DEPTH)


def wide_heads(windows):
    found = jnp.int32(0)
    ids = [jnp.int32(0)] * WIDE
    for head in range(windows.shape[1]):
        wide = (windows[0, head] > 1) | (windows[1, head] > 1) | (windows[2, head] > 1)
        for at in range(WIDE):
            ids[at] = jnp.where(wide & (found == at), head, ids[at])
        found = found + wide.astype(jnp.int32)
    return ids


def outer(a, b):
    return lax.dot_general(a, b, (((1,), (1,)), ((), ())), preferred_element_type=jnp.float32)


def inner(a, b):
    return jnp.dot(a, b, preferred_element_type=jnp.float32)


def low(x):
    return x.astype(jnp.bfloat16)


def high(x):
    return x.astype(jnp.float32)


def pack_body(windows, query, key, value, pairs, queries, held, sems):
    ids = wide_heads(windows)
    copies = []
    for at in range(WIDE):
        copies.append(pltpu.make_async_copy(key.at[:, lanes(ids[at])], pairs.at[at], sems.at[at]))
        copies.append(
            pltpu.make_async_copy(
                value.at[:, lanes(ids[at])], pairs.at[WIDE + at], sems.at[WIDE + at]
            )
        )
    asked = [
        pltpu.make_async_copy(query.at[:, lanes(ids[at])], held.at[at], sems.at[2 * WIDE + at])
        for at in range(WIDE)
    ]
    for copy in copies + asked:
        copy.start()
    for at in range(WIDE):
        asked[at].wait()
        queries[at] = held[at].T
    for copy in copies:
        copy.wait()


def quarter_body(weight, after, out, sem):
    rows = out.shape[0]
    first = pl.multiple_of(lax.axis_index("co") * rows, rows)
    copy = pltpu.make_async_copy(weight.at[pl.ds(first, rows), :], out, sem)
    copy.start()
    copy.wait()


def text_partial(query, key, value, rows, head, before, rounded):
    cols = slice(head * DEPTH, (head + 1) * DEPTH)
    scores = outer(query[rows, cols], key[:, cols]) * SCALE
    peak = jnp.max(scores, axis=1, keepdims=True)
    if before is not None:
        peak = jnp.maximum(peak, before[0])
    weights = jnp.exp2(scores - peak)
    total = jnp.sum(weights, axis=1, keepdims=True)
    mixed = inner(low(weights), value[:, cols])
    if before is not None:
        factor = jnp.exp2(before[0] - peak)
        total = total + before[1] * factor
        mixed = mixed + before[2] * factor
    if rounded:
        top = high(low(peak))
        factor = jnp.exp2(peak - top)
        peak, total, mixed = top, total * factor, mixed * factor
    return peak, total, mixed


def text_far_body(query, key, value, sums, stats):
    half = sums.shape[0]
    rows = pl.ds(pl.multiple_of((1 - lax.axis_index("co")) * half, half), half)
    lane = lax.broadcasted_iota(jnp.int32, stats.shape, 1)
    held = jnp.zeros(stats.shape, jnp.float32)
    heads = query.shape[1] // DEPTH
    for head in range(heads):
        peak, total, mixed = text_partial(query, key, value, rows, head, None, False)
        sums[:, head * DEPTH : (head + 1) * DEPTH] = mixed
        held = jnp.where(lane == head, peak, jnp.where(lane == 16 + head, total, held))
    stats[...] = held


def text_own_body(query, key, value, sums, stats, text_key, text_value, out):
    half = sums.shape[0]
    width = query.shape[1]
    heads = width // DEPTH
    rows = pl.ds(pl.multiple_of(lax.axis_index("co") * half, half), half)
    lane = lax.broadcasted_iota(jnp.int32, stats.shape, 1)
    held = jnp.zeros(stats.shape, jnp.float32)
    for head in range(heads):
        cols = slice(head * DEPTH, (head + 1) * DEPTH)
        before = (stats[:, head : head + 1], stats[:, 16 + head : 17 + head], sums[:, cols])
        peak, total, mixed = text_partial(query, key, value, rows, head, before, True)
        coarse = low(mixed)
        out[:, cols] = coarse
        out[:, width + head * DEPTH : width + (head + 1) * DEPTH] = low(mixed - high(coarse))
        big = high(low(total))
        held = jnp.where(lane == head, peak, held)
        held = jnp.where(lane == 16 + head, big, held)
        held = jnp.where(lane == 32 + head, total - big, held)
    out[:, 2 * width : 3 * width] = low(jnp.broadcast_to(high(text_key[...]), (half, width)))
    out[:, 3 * width : 4 * width] = low(jnp.broadcast_to(high(text_value[...]), (half, width)))
    out[:, 4 * width :] = low(held)


def text_masks(count, rows, cols):
    place = 2 * lax.broadcasted_iota(jnp.int32, (rows, cols), 0)
    core = lax.axis_index("co")
    return place + core < count, place + 1 - core < count


def narrow_body(windows, count, query, key, value, tk0, tv0, tk1, tv1, out, ids):
    heads = windows.shape[1]
    found = jnp.int32(0)
    for head in range(heads):
        wide = (windows[0, head] > 1) | (windows[1, head] > 1) | (windows[2, head] > 1)
        ids[jnp.where(wide, heads, found)] = head
        found = found + 1 - wide.astype(jnp.int32)
    tokens = query.shape[0]
    near, far = text_masks(count[0], tk0.shape[0], tokens)

    def step(group, carry):
        for at in range(3):
            cols = lanes(ids[group * 3 + at])
            asked = query[:, cols].T
            scores = inner(key[:, cols], asked) * SCALE
            first = jnp.where(near, inner(tk0[:, cols], asked) * SCALE, NEVER)
            second = jnp.where(far, inner(tk1[:, cols], asked) * SCALE, NEVER)
            peak = jnp.maximum(
                jnp.max(scores, axis=0, keepdims=True),
                jnp.max(jnp.maximum(first, second), axis=0, keepdims=True),
            )
            scores = jnp.exp2(scores - peak)
            first = jnp.exp2(first - peak)
            second = jnp.exp2(second - peak)
            total = jnp.sum(scores, axis=0, keepdims=True) + jnp.sum(
                first + second, axis=0, keepdims=True
            )
            mixed = (
                inner(value[:, cols].T, low(scores))
                + inner(tv0[:, cols].T, low(first))
                + inner(tv1[:, cols].T, low(second))
            )
            out[:, cols] = low((mixed / total).T)
        return carry

    lax.fori_loop(0, (heads - WIDE) // 3, step, 0)


def place_ok(windows, head, at, needs_time):
    row_at, zone, core = lax.axis_index("ha"), lax.axis_index("zh"), lax.axis_index("co")
    a, c = at // 3, at % 3
    rows = windows[1, head] > 1
    cols = windows[2, head] > 1
    row_in = (a == 0) | (
        rows & (((a == 1) & (row_at > 0)) | ((a == 2) & (row_at < lax.axis_size("ha") - 1)))
    )
    outer_in = jnp.where(core == 0, zone > 0, zone < lax.axis_size("zh") - 1)
    col_in = (c == 0) | (cols & ((c == 2) | outer_in))
    ok = row_in & col_in
    if needs_time:
        ok = ok & (windows[0, head] > 1)
    return ok


def wide_tiles(windows, ids, sources, keys, values, sems, needs_time):
    own, left, right, inside = sources
    for at in range(WIDE):
        for place in range(PLACES):
            a, c = divmod(place, 3)
            source = inside.at[a] if c == 2 else (own, left, right)[a].at[c]
            slot = at * PLACES + place

            @pl.when(place_ok(windows, ids[at], jnp.int32(place), needs_time))
            def _(source=source, slot=slot, at=at):
                pltpu.make_async_copy(source.at[at], keys.at[slot], sems.at[slot, 0]).start()
                pltpu.make_async_copy(source.at[WIDE + at], values.at[slot], sems.at[slot, 1]).start()


def wide_head(windows, ids, at, sources, keys, values, sems, needs_time, asked, peak, total, mixed):
    own = sources[0]

    def step(place, carry):
        @pl.when(place_ok(windows, ids[at], place, needs_time))
        def _():
            slot = at * PLACES + place
            pltpu.make_async_copy(own.at[0, 0], keys.at[slot], sems.at[slot, 0]).wait()
            pltpu.make_async_copy(own.at[0, 0], values.at[slot], sems.at[slot, 1]).wait()
            key = keys[slot]
            value = values[slot].T
            for part, query in enumerate(asked):
                scores = inner(key, query) * SCALE
                top = jnp.maximum(peak[part], jnp.max(scores, axis=0, keepdims=True))
                factor = jnp.exp2(peak[part] - top)
                weights = jnp.exp2(scores - top)
                total[part] = total[part] * factor + jnp.sum(weights, axis=0, keepdims=True)
                mixed[part] = mixed[part] * factor + inner(value, low(weights))
                peak[part] = top

        return carry

    lax.fori_loop(0, PLACES, step, 0)


def wide_lent_body(
    windows, own, left, right, inside, before, after, out0, out1, keys, values, peak, total, mixed, sems
):
    ids = wide_heads(windows)
    sources = (own, left, right, inside)
    wide_tiles(windows, ids, sources, keys, values, sems, True)
    for at in range(WIDE):
        peak[...] = jnp.full(peak.shape, NEVER, jnp.float32)
        total[...] = jnp.zeros(total.shape, jnp.float32)
        mixed[...] = jnp.zeros(mixed.shape, jnp.float32)
        asked = (before[at], after[at])
        wide_head(windows, ids, at, sources, keys, values, sems, True, asked, peak, total, mixed)
        for part, out in enumerate((out0, out1)):
            top = high(low(peak[part]))
            factor = jnp.exp2(peak[part] - top)
            sums = total[part] * factor
            big = high(low(sums))
            row = lax.broadcasted_iota(jnp.int32, (16, sums.shape[1]), 0)
            held = jnp.where(row == 0, top, jnp.where(row == 1, big, sums - big))
            out[at, :DEPTH] = low(mixed[part] * factor)
            out[at, DEPTH:] = low(held)


def wide_own_body(
    windows, count, own, left, right, inside, queries, tk0, tv0, tk1, tv1,
    sums, stats, keys, values, peak, total, mixed, sems,
):
    ids = wide_heads(windows)
    sources = (own, left, right, inside)
    wide_tiles(windows, ids, sources, keys, values, sems, False)
    near, far = text_masks(count[0], tk0.shape[0], queries.shape[2])
    for at in range(WIDE):
        cols = lanes(ids[at])
        asked = queries[at]
        first = jnp.where(near, inner(tk0[:, cols], asked) * SCALE, NEVER)
        second = jnp.where(far, inner(tk1[:, cols], asked) * SCALE, NEVER)
        top = jnp.max(jnp.maximum(first, second), axis=0, keepdims=True)
        first = jnp.exp2(first - top)
        second = jnp.exp2(second - top)
        peak[0] = top
        total[0] = jnp.sum(first + second, axis=0, keepdims=True)
        mixed[0] = inner(tv0[:, cols].T, low(first)) + inner(tv1[:, cols].T, low(second))
        wide_head(windows, ids, at, sources, keys, values, sems, False, (asked,), peak, total, mixed)
        row = lax.broadcasted_iota(jnp.int32, stats.shape[1:], 0)
        stats[at] = jnp.where(row == 0, peak[0], total[0])
        sums[at] = mixed[0]


def text_merge_body(query, count, got, tk1, tv1, out):
    width = query.shape[1]
    core = lax.axis_index("co")
    chip = (
        lax.axis_index("ta") * lax.axis_size("ha") + lax.axis_index("ha")
    ) * lax.axis_size("zh") + lax.axis_index("zh")
    sources = got.shape[0]
    at = core * sources + chip
    block = high(query[pl.ds(pl.multiple_of(at // 16 * 16, 16), 16), :])
    row = lax.broadcasted_iota(jnp.int32, block.shape, 0)
    asked = jnp.sum(jnp.where(row == at % 16, block, 0.0), axis=0, keepdims=True)
    near, far = text_masks(count[0], sources, 1)
    stats = high(got[:, 4 * width :])
    for head in range(width // DEPTH):
        cols = slice(head * DEPTH, (head + 1) * DEPTH)

        def part(block, head=head):
            return high(got[:, block * width + head * DEPTH : block * width + (head + 1) * DEPTH])

        peak = stats[:, head : head + 1]
        total = stats[:, 16 + head : 17 + head] + stats[:, 32 + head : 33 + head]
        mine = asked[:, cols]
        first = jnp.sum(part(2) * mine, axis=1, keepdims=True) * SCALE
        second = jnp.sum(high(tk1[:, cols]) * mine, axis=1, keepdims=True) * SCALE
        first = jnp.where(near, first, NEVER)
        second = jnp.where(far, second, NEVER)
        top = jnp.max(jnp.maximum(peak, jnp.maximum(first, second)), axis=0, keepdims=True)
        factor = jnp.exp2(peak - top)
        first = jnp.exp2(first - top)
        second = jnp.exp2(second - top)
        whole = jnp.sum(factor * total + first + second, axis=0, keepdims=True)
        mixed = jnp.sum(
            factor * (part(0) + part(1)) + first * part(3) + second * high(tv1[:, cols]),
            axis=0,
            keepdims=True,
        )
        out[:, cols] = low(jnp.broadcast_to(mixed / whole, (sources, DEPTH)))


def final_body(
    windows, sums, stats, back0, back1, narrow, w_own, w_mine, w_other, hidden, modulation, final, out,
    attended, weight, updated, sems, *, parts,
):
    ids = wide_heads(windows)
    branch, core = lax.axis_index("cfg"), lax.axis_index("co")
    half, model = w_own.shape
    part_cols = model // parts
    copies = []
    for part in range(parts):
        cols = pl.ds(part * part_cols, part_cols)
        for at, (source, row) in enumerate(
            (
                (w_own, branch * half),
                (w_mine, (1 - branch) * half + core * (half // 2)),
                (w_other, (1 - branch) * half + (1 - core) * (half // 2)),
            )
        ):
            rows = pl.ds(pl.multiple_of(row, half // 2), source.shape[0])
            copies.append(
                pltpu.make_async_copy(
                    source.at[:, cols], weight.at[rows, cols], sems.at[part, at]
                )
            )
    for copy in copies:
        copy.start()
    attended[...] = narrow[...]
    time_at = lax.axis_index("ta")
    inside = (time_at > 0, time_at < lax.axis_size("ta") - 1)
    for at in range(WIDE):
        peaks = [stats[at, 0:1]]
        totals = [stats[at, 1:2]]
        for back, ok in zip((back0, back1), inside):
            rows = high(back[at, DEPTH:])
            peaks.append(jnp.where(ok, rows[0:1], NEVER))
            totals.append(jnp.where(ok, rows[1:2] + rows[2:3], 0.0))
        top = jnp.maximum(peaks[0], jnp.maximum(peaks[1], peaks[2]))
        factors = [jnp.exp2(peak - top) for peak in peaks]
        total = sum(factor * whole for factor, whole in zip(factors, totals))
        mixed = (
            sums[at] * factors[0]
            + high(back0[at, :DEPTH]) * factors[1]
            + high(back1[at, :DEPTH]) * factors[2]
        )
        attended[:, lanes(ids[at])] = low((mixed / total).T)
    tokens = attended.shape[0]
    running = jnp.zeros((tokens, 1), jnp.float32)
    for part in range(parts):
        cols = slice(part * part_cols, (part + 1) * part_cols)
        for copy in copies[3 * part : 3 * part + 3]:
            copy.wait()
        projected = inner(attended[...], weight[:, cols])
        fresh = high(hidden[:, cols]) + modulation[0, :, cols] * projected
        updated[:, cols] = fresh
        running = running + jnp.sum(fresh, axis=1, keepdims=True)
    mean = running / model
    spread = jnp.zeros((tokens, 1), jnp.float32)
    for part in range(parts):
        cols = slice(part * part_cols, (part + 1) * part_cols)
        centered = updated[:, cols] - mean
        spread = spread + jnp.sum(centered * centered, axis=1, keepdims=True)
    factor = lax.rsqrt(spread / model + 1e-06)
    result = jnp.zeros(out.shape, jnp.float32)
    for part in range(parts):
        cols = slice(part * part_cols, (part + 1) * part_cols)
        normed = (updated[:, cols] - mean) * factor * (1.0 + modulation[2, :, cols])
        normed = normed + modulation[1, :, cols]
        result = result + outer(low(normed), final[:, cols])
    out[...] = result


def shift(x, axis, step):
    size = lax.axis_size(axis)
    return lax.ppermute(x, axis, [(i, i + step) for i in range(size) if 0 <= i + step < size])


def swap_core(x):
    return lax.ppermute(x, "co", [(0, 1), (1, 0)])


def local(
    video_query, video_key, video_value, text_query, text_key, text_value, text_count, head_windows,
    hidden_state, out_weight, final_weight, modulation, guidance,
):
    frames, rows, cols, width = video_query.shape[1:]
    tokens = frames * rows * cols
    heads = head_windows.shape[0]
    text_len = text_query.shape[1]
    half_text = text_len // 2
    model = out_weight.shape[1]
    half_width = out_weight.shape[0]
    bf16, f32 = jnp.bfloat16, jnp.float32
    shape = jax.ShapeDtypeStruct
    query = video_query.reshape(tokens, width)
    key = video_key.reshape(tokens, width)
    value = video_value.reshape(tokens, width)
    text_query = text_query[0]
    windows = head_windows.T
    core = lax.axis_index("co")
    branch = lax.axis_index("cfg")
    zones = lax.axis_size("zh")

    pairs, queries = call(
        pack_body,
        (shape((2 * WIDE, tokens, DEPTH), bf16), shape((WIDE, DEPTH, tokens), bf16)),
        [SMEM, HBM, HBM, HBM],
        (VMEM, VMEM),
        [pltpu.VMEM((WIDE, tokens, DEPTH), bf16), pltpu.SemaphoreType.DMA((3 * WIDE,))],
        0, 4 * 1024 * 1024,
        windows, query, key, value,
    )
    beside = [(2 * z + 1, 2 * z + 2) for z in range(zones - 1)]
    beside = beside + [(b, a) for a, b in beside]
    next_pairs = lax.ppermute(pairs, ("zh", "co"), beside)
    from_before = shift(queries, "ta", 1)
    from_after = shift(queries, "ta", -1)

    def at(branch_at, zone, core_at):
        return (branch_at * zones + zone) * 2 + core_at

    weight_pairs = []
    for z in range(zones):
        weight_pairs.append((at(0, z, 0), at(1, z, 0)))
        weight_pairs.append((at(0, (z + 1) % zones, 1), at(1, z, 1)))
    weight_pairs = weight_pairs + [(b, a) for a, b in weight_pairs]
    quarter = call(
        quarter_body,
        shape((half_width // 2, model), bf16),
        [HBM, HBM], VMEM, [pltpu.SemaphoreType.DMA], 0, 2 * half_width * model,
        out_weight, next_pairs,
    )
    w_mine = lax.ppermute(quarter, ("cfg", "zh", "co"), weight_pairs)

    text_flops = 2 * 2 * half_text * tokens * width
    text_bytes = 2 * 2 * tokens * width
    far_sums, far_stats = call(
        text_far_body,
        (shape((half_text, width), f32), shape((half_text, DEPTH), f32)),
        [VMEM] * 3, (VMEM, VMEM), [], text_flops, text_bytes,
        text_query, key, value,
    )
    payload = call(
        text_own_body,
        shape((half_text, 4 * width + DEPTH), bf16),
        [VMEM] * 7, VMEM, [], text_flops, text_bytes,
        text_query, key, value, swap_core(far_sums), swap_core(far_stats), text_key[0], text_value[0],
    )
    got = lax.all_to_all(payload, CHIPS, 0, 0, tiled=True)

    own = jnp.stack((pairs, next_pairs))
    left = shift(own, "ha", 1)
    right = shift(own, "ha", -1)
    inside = swap_core(jnp.stack((pairs, left[0], right[0])))
    w_other = swap_core(w_mine)

    got_other = swap_core(got)

    def text_block(index):
        return pl.BlockSpec((half_text, width), lambda step: (0, index))

    text_specs = [text_block(2), text_block(3), text_block(2), text_block(3)]
    narrow = call(
        narrow_body,
        shape((tokens, width), bf16),
        [SMEM, SMEM, VMEM, VMEM, VMEM] + text_specs, VMEM,
        [pltpu.SMEM((heads + 1,), jnp.int32)],
        4 * (heads - WIDE) * tokens * (tokens + text_len) * DEPTH, 5 * tokens * width * 2,
        windows, text_count, query, key, value, got, got, got_other, got_other,
    )

    def wide_scratch(parts):
        return [
            pltpu.VMEM((WIDE * PLACES, tokens, DEPTH), bf16),
            pltpu.VMEM((WIDE * PLACES, tokens, DEPTH), bf16),
            pltpu.VMEM((parts, 1, tokens), f32),
            pltpu.VMEM((parts, 1, tokens), f32),
            pltpu.VMEM((parts, DEPTH, tokens), f32),
            pltpu.SemaphoreType.DMA((WIDE * PLACES, 2)),
        ]

    tile_flops = 4 * tokens * tokens * DEPTH
    lent = shape((WIDE, DEPTH + 16, tokens), bf16)
    to_before, to_after = call(
        wide_lent_body,
        (lent, lent),
        [SMEM, HBM, HBM, HBM, HBM, VMEM, VMEM], (VMEM, VMEM),
        wide_scratch(2), 2 * WIDE * PLACES * tile_flops, 6 * MIB,
        windows, own, left, right, inside, from_before, from_after,
    )
    back_after = shift(to_before, "ta", -1)
    back_before = shift(to_after, "ta", 1)
    sums, stats = call(
        wide_own_body,
        (shape((WIDE, DEPTH, tokens), f32), shape((WIDE, 8, tokens), f32)),
        [SMEM, SMEM, HBM, HBM, HBM, HBM, VMEM] + text_specs, (VMEM, VMEM),
        wide_scratch(1), WIDE * PLACES * tile_flops, 6 * MIB,
        windows, text_count, own, left, right, inside, queries, got, got, got_other, got_other,
    )

    finished = call(
        text_merge_body,
        shape((half_text, width), bf16),
        [VMEM, SMEM, VMEM] + text_specs[2:], VMEM, [], 0, 2 * MIB,
        text_query, text_count, got, got_other, got_other,
    )
    text_mine = lax.all_to_all(finished, CHIPS, 0, 0, tiled=True)
    text_other = swap_core(text_mine)
    text_out = jnp.where(
        core == 0,
        jnp.concatenate((text_mine, text_other)),
        jnp.concatenate((text_other, text_mine)),
    )

    parts = 6
    branch_out = call(
        functools.partial(final_body, parts=parts),
        shape((tokens, final_weight.shape[1]), f32),
        [SMEM, VMEM, VMEM, VMEM, VMEM, VMEM, HBM, HBM, HBM, VMEM, VMEM, VMEM], VMEM,
        [
            pltpu.VMEM((tokens, width), bf16),
            pltpu.VMEM((width, model), bf16),
            pltpu.VMEM((tokens, model), f32),
            pltpu.SemaphoreType.DMA((parts, 3)),
        ],
        2 * tokens * width * model, 16 * MIB,
        windows, sums, stats, back_before, back_after, narrow, out_weight, w_mine, w_other,
        hidden_state.reshape(tokens, model), modulation.transpose(1, 0, 2), final_weight.T,
    )
    half_rows = rows // 2
    grid = branch_out.reshape(frames, rows, cols * final_weight.shape[1])
    kept = lax.dynamic_slice_in_dim(grid, branch * half_rows, half_rows, 1)
    sent = lax.dynamic_slice_in_dim(grid, (1 - branch) * half_rows, half_rows, 1)
    received = lax.ppermute(sent, "cfg", [(0, 1), (1, 0)])
    conditional = jnp.where(branch == 0, kept, received)
    unconditional = jnp.where(branch == 0, received, kept)
    guided = unconditional + guidance[0] * (conditional - unconditional)
    return (guided, text_out[None])


def solution(mesh):
    devices = mesh.devices.reshape(mesh.devices.shape[:3] + (mesh.devices.shape[3] // 2, 2))
    split = Mesh(devices, ("cfg", "ta", "ha", "zh", "co"))
    wa = ("zh", "co")
    everyone = ("ta", "ha", "zh", "co")
    video = P("cfg", "ta", "ha", wa, None)
    in_specs = (
        video, video, video,
        P("cfg", None, None),
        P("cfg", everyone, None),
        P("cfg", everyone, None),
        P("cfg"),
        P(),
        video,
        P("cfg", None),
        P(),
        P("cfg", None, None),
        P(),
    )
    out_specs = (P("ta", ("ha", "cfg"), wa), P("cfg", None, None))
    return jax.shard_map(local, mesh=split, in_specs=in_specs, out_specs=out_specs, check_vma=False)
```

time: 2210 us -> 186 us (0.08)
  the two profiles are of different devices: /device:TPU:1 before, /device:TPU:74 now
where the time goes in v1:
time: 186 us; the launch traced here: 190 us
  Pallas kernels  80.4 us (43%)
  starting transfers between devices  55.3 us (30%)
  waiting for transfers between devices  31.3 us (17%)
  local copies, waits for them, and re-layouts  12.3 us (7%)
  other arithmetic  8.03 us (4%)
  between operations  2.3 us (1%)
    pallas_call x9, Pallas kernels, call(): pl.pallas_call(body, grid=(1,), out_shape=out_shape, in_specs=in_specs, o...  80.4 us
    ppermute x6, starting transfers between devices, shift(): lax.ppermute(x, axis, [(i, i + step) for i in range(size) if 0 <= i + ste...  17.9 us
    all_to_all x1, starting transfers between devices, local(): text_mine = lax.all_to_all(finished, CHIPS, 0, 0, tiled=True)  14.6 us
    ppermute x1, waiting for transfers between devices, local(): next_pairs = lax.ppermute(pairs, ('zh', 'co'), beside)  14.6 us
    all_to_all x1, starting transfers between devices, local(): got = lax.all_to_all(payload, CHIPS, 0, 0, tiled=True)  14.2 us
    all_to_all x1, waiting for transfers between devices, local(): got = lax.all_to_all(payload, CHIPS, 0, 0, tiled=True)  13.4 us
    unnamed x32, local copies, waits for them, and re-layouts  8.52 us
    ppermute x1, starting transfers between devices, local(): w_mine = lax.ppermute(quarter, ('cfg', 'zh', 'co'), weight_pairs)  3.79 us
  transfers between devices with their start and end apart: 17, of which 4 were waited for; matrix products, arithmetic and copies ran while one was open for 8% of the time, Pallas kernels for 39%

profile of v1, /device:TPU:74, one launch (start us, length us, event | category | flops | bytes accessed | tf_op | source)
XLA Modules:
  0.0 189.6 jit_solution(14400574420143420935)
XLA Ops:
  0.6 3.2 %shard_map.140 = (bf16[6,384,128]{2,1,0:T(8,128)(2,1)}, bf16[3,128,384]{2,1,0:T(8,128)(2,1)}) custom-call(s32[3,12]{1,0:T(4,128)} %bitcast.55, bf16[384,1536]{1,0:T(8,128)(2,1)} %bitcast.39, bf16[384,1536]{1,0:T(8,128)(2,1)} %bitcast.31, bf16[384,1536]{1,0:T(8,128)(2,1)} %bitcast.35), custom_call_target="tpu_custom_call" | custom-call | bytes 4194304 | tf_op jit(solution)/shard_map/pallas_call | solution.py:27
  3.9 2.1 %collective-permute-start = (bf16[6,384,128]{2,1,0:T(8,128)(2,1)}, bf16[6,384,128]{2,1,0:T(8,128)(2,1)S(1)}, u32[]{:S(2)}, u32[]{:S(2)}) collective-permute-start(bf16[6,384,128]{2,1,0:T(8,128)(2,1)} %get-tuple-element.10), channel_id=1, source_target_pairs={{1,2},{3,4},{5,6},{2,1},{4,3},{6,5},{9,10},{11,12},{13,14},{10,9},... | collective-permute-start | bytes 1769480 | tf_op jit(solution)/shard_map/ppermute | solution.py:456
  5.9 14.6 %collective-permute-done.after = bf16[6,384,128]{2,1,0:T(8,128)(2,1)S(1)} collective-permute-done((bf16[6,384,128]{2,1,0:T(8,128)(2,1)}, bf16[6,384,128]{2,1,0:T(8,128)(2,1)S(1)}, u32[]{:S(2)}, u32[]{:S(2)}) %collective-permute-start) | collective-permute-done | bytes 589856 | tf_op jit(solution)/shard_map/ppermute | solution.py:456
  21.3 3.1 %shard_map.146 = bf16[384,3072]{1,0:T(8,128)(2,1)} custom-call(bf16[768,3072]{1,0:T(8,128)(2,1)} %w_own.1, bf16[6,384,128]{2,1,0:T(8,128)(2,1)} %copy-done.5), custom_call_target="tpu_custom_call" | custom-call | bytes 4718592 | tf_op jit(solution)/shard_map/pallas_call | solution.py:27
  24.5 3.8 %collective-permute-start.11 = (bf16[384,3072]{1,0:T(8,128)(2,1)}, bf16[384,3072]{1,0:T(8,128)(2,1)}, u32[]{:S(2)}, u32[]{:S(2)}) collective-permute-start(bf16[384,3072]{1,0:T(8,128)(2,1)} %shard_map.146), channel_id=1, source_target_pairs={{0,128},{3,129},{2,130},{5,131},{4,132},{7,133},{6,134},{1,135},{1... | collective-permute-start | bytes 7077896 | tf_op jit(solution)/shard_map/ppermute | solution.py:474
  29.4 2.4 %collective-permute-start.2 = (bf16[2,6,384,128]{3,2,1,0:T(8,128)(2,1)S(1)}, bf16[2,6,384,128]{3,2,1,0:T(8,128)(2,1)}, u32[]{:S(2)}, u32[]{:S(2)}) collective-permute-start(bf16[2,6,384,128]{3,2,1,0:T(8,128)(2,1)S(1)} %pad_maximum_fusion.1.own), channel_id=1, source_target_pairs={{8,0},{16,8},{24,16},{9,1},{17,9},{25,17},{10,2},{18,10},{26,18},{... | collective-permute-start | bytes 3538952 | tf_op jit(solution)/shard_map/ppermute | solution.py:416
  31.9 3.4 %collective-permute-start.1 = (bf16[2,6,384,128]{3,2,1,0:T(8,128)(2,1)S(1)}, bf16[2,6,384,128]{3,2,1,0:T(8,128)(2,1)}, u32[]{:S(2)}, u32[]{:S(2)}) collective-permute-start(bf16[2,6,384,128]{3,2,1,0:T(8,128)(2,1)S(1)} %pad_maximum_fusion.1.own), channel_id=1, source_target_pairs={{0,8},{8,16},{16,24},{1,9},{9,17},{17,25},{2,10},{10,18},{18,26},{... | collective-permute-start | bytes 3538952 | tf_op jit(solution)/shard_map/ppermute | solution.py:416
  35.3 5.6 %shard_map.141 = (f32[64,1536]{1,0:T(8,128)}, f32[64,128]{1,0:T(8,128)}) custom-call(bf16[128,1536]{1,0:T(8,128)(2,1)} %bitcast.41, bf16[384,1536]{1,0:T(8,128)(2,1)} %bitcast.32, bf16[384,1536]{1,0:T(8,128)(2,1)} %bitcast.36), custom_call_target="tpu_custom_call" | custom-call | flops 150994944 | bytes 2359296 | tf_op jit(solution)/shard_map/pallas_call | solution.py:27
  43.7 7.1 %shard_map.142 = bf16[64,6272]{1,0:T(8,128)(2,1)} custom-call(bf16[128,1536]{1,0:T(8,128)(2,1)} %bitcast.42, bf16[384,1536]{1,0:T(8,128)(2,1)} %bitcast.33, bf16[384,1536]{1,0:T(8,128)(2,1)} %bitcast.37, f32[64,1536]{1,0:T(8,128)} %copy-done.6, f32[64,128]{1,0:T(8,128)} %copy-done.10, bf16[1,1536]{1,0:T(2,128)(2,1)} %bitcast.60, bf16[1,1536]{1,0:T(2,128)(2,1)} %bitcast.61), custom_call_target="tpu_custom_call" | custom-call | flops 150994944 | bytes 2359296 | tf_op jit(solution)/shard_map/pallas_call | solution.py:27
  51.2 2.3 %reduce = bf16[64,6272]{1,0:T(8,128)(2,1)S(1)} reduce(bf16[64,1,6272]{2,0,1:T(8,128)(2,1)} %bitcast.44, bf16[]{:T(256)} %broadcast.7), dimensions={1}, to_apply=%copy.17.reduce_sub_computation | reduce | bytes 1605634 | tf_op jit(solution)/shard_map/all_to_all | solution.py:490
  53.5 1.7 reshape.85
  55.2 14.2 %all-to-all-start = ((bf16[64,2,3136]{2,1,0:T(2,128)(2,1)}), bf16[64,2,3136]{2,1,0:T(2,128)(2,1)S(1)}, u32[]{:S(2)}, u32[]{:S(2)}) async-start(bf16[64,2,3136]{2,1,0:T(2,128)(2,1)} %reshape.85), calls=%async_computation | async-start | bytes 1638400 | tf_op jit(solution)/shard_map/all_to_all | solution.py:490
  73.7 13.4 %all-to-all-done = bf16[64,2,3136]{2,1,0:T(2,128)(2,1)S(1)} async-done(((bf16[64,2,3136]{2,1,0:T(2,128)(2,1)}), bf16[64,2,3136]{2,1,0:T(2,128)(2,1)S(1)}, u32[]{:S(2)}, u32[]{:S(2)}) %all-to-all-start) | async-done | bytes 802848 | tf_op jit(solution)/shard_map/all_to_all | solution.py:490
  89.1 3.4 %collective-permute-start.7 = (bf16[3,128,384]{2,1,0:T(8,128)(2,1)S(1)}, bf16[3,128,384]{2,1,0:T(8,128)(2,1)S(1)}, u32[]{:S(2)}, u32[]{:S(2)}) collective-permute-start(bf16[3,128,384]{2,1,0:T(8,128)(2,1)S(1)} %copy-done.9), channel_id=1, source_target_pairs={{0,32},{32,64},{64,96},{1,33},{33,65},{65,97},{2,34},{34,66},{66,9... | collective-permute-start | bytes 884744 | tf_op jit(solution)/shard_map/ppermute | solution.py:416
  92.5 2.7 %collective-permute-start.8 = (bf16[3,128,384]{2,1,0:T(8,128)(2,1)S(1)}, bf16[3,128,384]{2,1,0:T(8,128)(2,1)S(1)}, u32[]{:S(2)}, u32[]{:S(2)}) collective-permute-start(bf16[3,128,384]{2,1,0:T(8,128)(2,1)S(1)} %copy-done.9), channel_id=1, source_target_pairs={{32,0},{64,32},{96,64},{33,1},{65,33},{97,65},{34,2},{66,34},{98,6... | collective-permute-start | bytes 884744 | tf_op jit(solution)/shard_map/ppermute | solution.py:416
  96.9 3.8 %shard_map.148 = bf16[64,1536]{1,0:T(8,128)(2,1)} custom-call(bf16[128,1536]{1,0:T(8,128)(2,1)} %bitcast.43, s32[1]{0:T(128)S(6)} %copy.29.count, bf16[64,6272]{1,0:T(8,128)(2,1)} %bitcast.26, bf16[64,6272]{1,0:T(8,128)(2,1)} %copy-done.1, bf16[64,6272]{1,0:T(8,128)(2,1)} %copy-done.1), custom_call_target="tpu_custom_call" | custom-call | bytes 2097152 | tf_op jit(solution)/shard_map/pallas_call | solution.py:27
  103.1 14.6 %all-to-all-start.1 = ((bf16[64,2,768]{2,1,0:T(2,128)(2,1)}), bf16[64,2,768]{2,1,0:T(2,128)(2,1)S(1)}, u32[]{:S(2)}, u32[]{:S(2)}) async-start(bf16[64,2,768]{2,1,0:T(2,128)(2,1)} %reshape.87), calls=%async_computation.1 | async-start | bytes 393216 | tf_op jit(solution)/shard_map/all_to_all | solution.py:548
  118.5 20.3 %shard_map.144 = (bf16[3,144,384]{2,1,0:T(8,128)(2,1)}, bf16[3,144,384]{2,1,0:T(8,128)(2,1)}) custom-call(s32[3,12]{1,0:T(4,128)} %bitcast.56, bf16[2,6,384,128]{3,2,1,0:T(8,128)(2,1)} %copy-done.2, bf16[2,6,384,128]{3,2,1,0:T(8,128)(2,1)} %collective-permute-done.1.left, bf16[2,6,384,128]{3,2,1,0:T(8,128)(2,1)} %collective-permute-done.2.right, ...), custom_call_target="tpu_custom_call" | custom-call | flops 4076863488 | bytes 6291456 | tf_op jit(solution)/shard_map/pallas_call | solution.py:27
  138.8 3.5 %collective-permute-start.9 = (bf16[3,144,384]{2,1,0:T(8,128)(2,1)}, bf16[3,144,384]{2,1,0:T(8,128)(2,1)S(1)}, u32[]{:S(2)}, u32[]{:S(2)}) collective-permute-start(bf16[3,144,384]{2,1,0:T(8,128)(2,1)} %get-tuple-element.16), channel_id=1, source_target_pairs={{0,32},{32,64},{64,96},{1,33},{33,65},{65,97},{2,34},{34,66},{66,9... | collective-permute-start | bytes 995336 | tf_op jit(solution)/shard_map/ppermute | solution.py:416
  142.3 2.4 %collective-permute-start.10 = (bf16[3,144,384]{2,1,0:T(8,128)(2,1)}, bf16[3,144,384]{2,1,0:T(8,128)(2,1)S(1)}, u32[]{:S(2)}, u32[]{:S(2)}) collective-permute-start(bf16[3,144,384]{2,1,0:T(8,128)(2,1)} %get-tuple-element.17), channel_id=1, source_target_pairs={{32,0},{64,32},{96,64},{33,1},{65,33},{97,65},{34,2},{66,34},{98,6... | collective-permute-start | bytes 995336 | tf_op jit(solution)/shard_map/ppermute | solution.py:416
  145.4 8.3 %shard_map.145.narrow = bf16[384,1536]{1,0:T(8,128)(2,1)} custom-call(s32[3,12]{1,0:T(4,128)} %bitcast.57, s32[1]{0:T(128)S(6)} %copy.29.count, bf16[384,1536]{1,0:T(8,128)(2,1)} %bitcast.40, bf16[384,1536]{1,0:T(8,128)(2,1)} %bitcast.34, bf16[384,1536]{1,0:T(8,128)(2,1)} %bitcast.38, bf16[64,6272]{1,0:T(8,128)(2,1)} %bitcast.27, bf16[64,6272]{1,0:T(8,128)(2,1)} %bitcast.28, ...), custom_call_target="tpu_custom_call" | custom-call | flops 905969664 | bytes 5898240 | tf_op jit(solution)/shard_map/pallas_call | solution.py:27
  154.0 16.4 %shard_map.143 = (f32[3,128,384]{2,1,0:T(8,128)}, f32[3,8,384]{2,1,0:T(8,128)}) custom-call(s32[3,12]{1,0:T(4,128)} %bitcast.58, s32[1]{0:T(128)S(6)} %copy.29.count, bf16[2,6,384,128]{3,2,1,0:T(8,128)(2,1)} %copy-done.2, bf16[2,6,384,128]{3,2,1,0:T(8,128)(2,1)} %collective-permute-done.1.left, bf16[2,6,384,128]{3,2,1,0:T(8,128)(2,1)} %collective-permute-done.2.right, ...), custom_call_target="tpu_custom_call" | custom-call | flops 2038431744 | bytes 6291456 | tf_op jit(solution)/shard_map/pallas_call | solution.py:27
  171.2 12.5 %shard_map.147 = f32[384,64]{1,0:T(8,128)} custom-call(s32[3,12]{1,0:T(4,128)} %bitcast.59, f32[3,128,384]{2,1,0:T(8,128)} %get-tuple-element.14.sums, f32[3,8,384]{2,1,0:T(8,128)} %get-tuple-element.15.stats, bf16[3,144,384]{2,1,0:T(8,128)(2,1)} %copy-done.7, bf16[3,144,384]{2,1,0:T(8,128)(2,1)} %copy-done.8, bf16[384,1536]{1,0:T(8,128)(2,1)} %shard_map.145.narrow, ...), custom_call_target="tpu_custom_call" | custom-call | flops 3623878656 | bytes 16777216 | tf_op jit(solution)/shard_map/pallas_call | solution.py:27
  187.1 1.9 collective-permute-done.13
  (62 shorter events, 20.7 us)
Async XLA Ops:
  3.9 24.4 %copy-start.3 = (bf16[6,384,128]{2,1,0:T(8,128)(2,1)S(1)}, bf16[6,384,128]{2,1,0:T(8,128)(2,1)}, u32[]{:S(2)}) copy-start(bf16[6,384,128]{2,1,0:T(8,128)(2,1)} %get-tuple-element.10) | copy-start | bytes 1769476
  3.9 16.6 %collective-permute-start = (bf16[6,384,128]{2,1,0:T(8,128)(2,1)}, bf16[6,384,128]{2,1,0:T(8,128)(2,1)S(1)}, u32[]{:S(2)}, u32[]{:S(2)}) collective-permute-start(bf16[6,384,128]{2,1,0:T(8,128)(2,1)} %get-tuple-element.10), channel_id=1, source_target_pairs={{1,2},{3,4},{5,6},{2,1},{4,3},{6,5},{9,10},{11,12},{13,14},{10,9},... | collective-permute-start | bytes 1769480 | tf_op jit(solution)/shard_map/ppermute | solution.py:456
  20.5 0.8 copy-start.5
  24.5 48.8 %collective-permute-start.11 = (bf16[384,3072]{1,0:T(8,128)(2,1)}, bf16[384,3072]{1,0:T(8,128)(2,1)}, u32[]{:S(2)}, u32[]{:S(2)}) collective-permute-start(bf16[384,3072]{1,0:T(8,128)(2,1)} %shard_map.146), channel_id=1, source_target_pairs={{0,128},{3,129},{2,130},{5,131},{4,132},{7,133},{6,134},{1,135},{1... | collective-permute-start | bytes 7077896 | tf_op jit(solution)/shard_map/ppermute | solution.py:474
  29.4 21.3 %copy-start.2 = (bf16[2,6,384,128]{3,2,1,0:T(8,128)(2,1)}, bf16[2,6,384,128]{3,2,1,0:T(8,128)(2,1)S(1)}, u32[]{:S(2)}) copy-start(bf16[2,6,384,128]{3,2,1,0:T(8,128)(2,1)S(1)} %pad_maximum_fusion.1.own) | copy-start | bytes 3538948
  29.4 40.0 %collective-permute-start.2 = (bf16[2,6,384,128]{3,2,1,0:T(8,128)(2,1)S(1)}, bf16[2,6,384,128]{3,2,1,0:T(8,128)(2,1)}, u32[]{:S(2)}, u32[]{:S(2)}) collective-permute-start(bf16[2,6,384,128]{3,2,1,0:T(8,128)(2,1)S(1)} %pad_maximum_fusion.1.own), channel_id=1, source_target_pairs={{8,0},{16,8},{24,16},{9,1},{17,9},{25,17},{10,2},{18,10},{26,18},{... | collective-permute-start | bytes 3538952 | tf_op jit(solution)/shard_map/ppermute | solution.py:416
  31.9 38.7 %collective-permute-start.1 = (bf16[2,6,384,128]{3,2,1,0:T(8,128)(2,1)S(1)}, bf16[2,6,384,128]{3,2,1,0:T(8,128)(2,1)}, u32[]{:S(2)}, u32[]{:S(2)}) collective-permute-start(bf16[2,6,384,128]{3,2,1,0:T(8,128)(2,1)S(1)} %pad_maximum_fusion.1.own), channel_id=1, source_target_pairs={{0,8},{8,16},{16,24},{1,9},{9,17},{17,25},{2,10},{10,18},{18,26},{... | collective-permute-start | bytes 3538952 | tf_op jit(solution)/shard_map/ppermute | solution.py:416
  40.9 2.0 %collective-permute-start.4 = (f32[64,1536]{1,0:T(8,128)}, f32[64,1536]{1,0:T(8,128)S(1)}, u32[]{:S(2)}, u32[]{:S(2)}) collective-permute-start(f32[64,1536]{1,0:T(8,128)} %get-tuple-element.12), channel_id=1, source_target_pairs={{0,1},{1,0},{2,3},{3,2},{4,5},{5,4},{6,7},{7,6},{8,9},{9,8},{10,11... | collective-permute-start | bytes 1179656 | tf_op jit(solution)/shard_map/ppermute | solution.py:420
  40.9 2.0 %collective-permute-start.5 = (f32[64,128]{1,0:T(8,128)}, f32[64,128]{1,0:T(8,128)S(1)}, u32[]{:S(2)}, u32[]{:S(2)}) collective-permute-start(f32[64,128]{1,0:T(8,128)} %get-tuple-element.13), channel_id=1, source_target_pairs={{0,1},{1,0},{2,3},{3,2},{4,5},{5,4},{6,7},{7,6},{8,9},{9,8},{10,11... | collective-permute-start | bytes 98312 | tf_op jit(solution)/shard_map/ppermute | solution.py:420
  55.2 31.9 %all-to-all-start = ((bf16[64,2,3136]{2,1,0:T(2,128)(2,1)}), bf16[64,2,3136]{2,1,0:T(2,128)(2,1)S(1)}, u32[]{:S(2)}, u32[]{:S(2)}) async-start(bf16[64,2,3136]{2,1,0:T(2,128)(2,1)} %reshape.85), calls=%async_computation | async-start | bytes 1638400 | tf_op jit(solution)/shard_map/all_to_all | solution.py:490
  69.4 2.3 %copy-start.4 = (bf16[6,384,128]{2,1,0:T(8,128)(2,1)S(1)}, bf16[6,384,128]{2,1,0:T(8,128)(2,1)}, u32[]{:S(2)}) copy-start(bf16[6,384,128]{2,1,0:T(8,128)(2,1)} %get-tuple-element.10) | copy-start | bytes 1769476
  73.2 44.5 %collective-permute-start.3 = (bf16[3,6,384,128]{3,2,1,0:T(8,128)(2,1)}, bf16[3,6,384,128]{3,2,1,0:T(8,128)(2,1)}, u32[]{:S(2)}, u32[]{:S(2)}) collective-permute-start(bf16[3,6,384,128]{3,2,1,0:T(8,128)(2,1)} %pad_maximum_fusion), channel_id=1, source_target_pairs={{0,1},{1,0},{2,3},{3,2},{4,5},{5,4},{6,7},{7,6},{8,9},{9,8},{10,11... | collective-permute-start | bytes 5308424 | tf_op jit(solution)/shard_map/ppermute | solution.py:420
  73.2 97.2 %collective-permute-start.12 = (bf16[384,3072]{1,0:T(8,128)(2,1)}, bf16[384,3072]{1,0:T(8,128)(2,1)}, u32[]{:S(2)}, u32[]{:S(2)}) collective-permute-start(bf16[384,3072]{1,0:T(8,128)(2,1)} %collective-permute-done.11.w_mine), channel_id=1, source_target_pairs={{0,1},{1,0},{2,3},{3,2},{4,5},{5,4},{6,7},{7,6},{8,9},{9,8},{10,11... | collective-permute-start | bytes 7077896 | tf_op jit(solution)/shard_map/ppermute | solution.py:420
  88.1 1.0 copy-start.9
  88.2 7.7 %copy-start = (bf16[64,1,6272]{2,0,1:T(8,128)(2,1)}, bf16[64,1,6272]{2,0,1:T(8,128)(2,1)S(1)}, u32[]{:S(2)}) copy-start(bf16[64,1,6272]{2,0,1:T(8,128)(2,1)S(1)} %copy.25) | copy-start | bytes 2408452
  88.2 7.7 %collective-permute-start.6 = (bf16[64,6272]{1,0:T(8,128)(2,1)S(1)}, bf16[64,6272]{1,0:T(8,128)(2,1)S(1)}, u32[]{:S(2)}, u32[]{:S(2)}) collective-permute-start(bf16[64,6272]{1,0:T(8,128)(2,1)S(1)} %bitcast.25), channel_id=1, source_target_pairs={{0,1},{1,0},{2,3},{3,2},{4,5},{5,4},{6,7},{7,6},{8,9},{9,8},{10,11... | collective-permute-start | bytes 2408456 | tf_op jit(solution)/shard_map/ppermute | solution.py:420
  89.1 28.6 %collective-permute-start.7 = (bf16[3,128,384]{2,1,0:T(8,128)(2,1)S(1)}, bf16[3,128,384]{2,1,0:T(8,128)(2,1)S(1)}, u32[]{:S(2)}, u32[]{:S(2)}) collective-permute-start(bf16[3,128,384]{2,1,0:T(8,128)(2,1)S(1)} %copy-done.9), channel_id=1, source_target_pairs={{0,32},{32,64},{64,96},{1,33},{33,65},{65,97},{2,34},{34,66},{66,9... | collective-permute-start | bytes 884744 | tf_op jit(solution)/shard_map/ppermute | solution.py:416
  92.5 25.2 %collective-permute-start.8 = (bf16[3,128,384]{2,1,0:T(8,128)(2,1)S(1)}, bf16[3,128,384]{2,1,0:T(8,128)(2,1)S(1)}, u32[]{:S(2)}, u32[]{:S(2)}) collective-permute-start(bf16[3,128,384]{2,1,0:T(8,128)(2,1)S(1)} %copy-done.9), channel_id=1, source_target_pairs={{32,0},{64,32},{96,64},{33,1},{65,33},{97,65},{34,2},{66,34},{98,6... | collective-permute-start | bytes 884744 | tf_op jit(solution)/shard_map/ppermute | solution.py:416
  95.9 0.9 copy-start.1
  103.1 50.6 %all-to-all-start.1 = ((bf16[64,2,768]{2,1,0:T(2,128)(2,1)}), bf16[64,2,768]{2,1,0:T(2,128)(2,1)S(1)}, u32[]{:S(2)}, u32[]{:S(2)}) async-start(bf16[64,2,768]{2,1,0:T(2,128)(2,1)} %reshape.87), calls=%async_computation.1 | async-start | bytes 393216 | tf_op jit(solution)/shard_map/all_to_all | solution.py:548
  138.8 31.6 %collective-permute-start.9 = (bf16[3,144,384]{2,1,0:T(8,128)(2,1)}, bf16[3,144,384]{2,1,0:T(8,128)(2,1)S(1)}, u32[]{:S(2)}, u32[]{:S(2)}) collective-permute-start(bf16[3,144,384]{2,1,0:T(8,128)(2,1)} %get-tuple-element.16), channel_id=1, source_target_pairs={{0,32},{32,64},{64,96},{1,33},{33,65},{65,97},{2,34},{34,66},{66,9... | collective-permute-start | bytes 995336 | tf_op jit(solution)/shard_map/ppermute | solution.py:416
  142.3 28.1 %collective-permute-start.10 = (bf16[3,144,384]{2,1,0:T(8,128)(2,1)}, bf16[3,144,384]{2,1,0:T(8,128)(2,1)S(1)}, u32[]{:S(2)}, u32[]{:S(2)}) collective-permute-start(bf16[3,144,384]{2,1,0:T(8,128)(2,1)} %get-tuple-element.17), channel_id=1, source_target_pairs={{32,0},{64,32},{96,64},{33,1},{65,33},{97,65},{34,2},{66,34},{98,6... | collective-permute-start | bytes 995336 | tf_op jit(solution)/shard_map/ppermute | solution.py:416
  153.9 32.4 %collective-permute-start.14 = (bf16[64,1536]{1,0:T(8,128)(2,1)S(1)}, bf16[64,1536]{1,0:T(8,128)(2,1)S(1)}, u32[]{:S(2)}, u32[]{:S(2)}) collective-permute-start(bf16[64,1536]{1,0:T(8,128)(2,1)S(1)} %bitcast.50), channel_id=1, source_target_pairs={{0,1},{1,0},{2,3},{3,2},{4,5},{5,4},{6,7},{7,6},{8,9},{9,8},{10,11... | collective-permute-start | bytes 589832 | tf_op jit(solution)/shard_map/ppermute | solution.py:420
  184.8 4.2 %collective-permute-start.13 = (f32[6,4,512]{2,1,0:T(4,128)S(1)}, f32[6,4,512]{2,1,0:T(4,128)S(1)}, u32[]{:S(2)}, u32[]{:S(2)}) collective-permute-start(f32[6,4,512]{2,1,0:T(4,128)S(1)} %constant_dynamic-slice_fusion), channel_id=1, source_target_pairs={{0,128},{128,0},{1,129},{129,1},{2,130},{130,2},{3,131},{131,3},{4... | collective-permute-start | bytes 147464 | tf_op jit(solution)/shard_map/ppermute | solution.py:575
  (6 other events, 4.4 us)

commit v2 on v1

v2 whole, which is shorter than its diff:
```python
import functools
import math

import jax
import jax.numpy as jnp
from jax import lax
from jax.experimental import pallas as pl
from jax.experimental.pallas import tpu as pltpu
from jax.sharding import Mesh
from jax.sharding import PartitionSpec as P

DEPTH = 128
WIDE = 3
NEVER = -(2.0**100)
CHIPS = ("ta", "ha", "zh")
SLOTS = 40
ENDS = 16
LOG2E = math.log2(math.e)
SCALE = LOG2E / math.sqrt(DEPTH)
MIB = 1024 * 1024

VMEM = pl.BlockSpec(memory_space=pltpu.VMEM)
SMEM = pl.BlockSpec(memory_space=pltpu.SMEM)
HBM = pl.BlockSpec(memory_space=pl.ANY)


def call(body, out_shape, in_specs, out_specs, scratch, vmem, flops, moved, *operands):
    return pl.pallas_call(
        body,
        grid=(1,),
        out_shape=out_shape,
        in_specs=in_specs,
        out_specs=out_specs,
        scratch_shapes=scratch,
        compiler_params=pltpu.CompilerParams(vmem_limit_bytes=64 * MIB - 65536),
        cost_estimate=pl.CostEstimate(flops=flops, bytes_accessed=moved, transcendentals=0),
    )(*operands)


def lanes(head):
    return pl.ds(pl.multiple_of(head * DEPTH, DEPTH), DEPTH)


def wide_heads(windows):
    found = jnp.int32(0)
    ids = [jnp.int32(0)] * WIDE
    for head in range(windows.shape[1]):
        wide = (windows[0, head] > 1) | (windows[1, head] > 1) | (windows[2, head] > 1)
        for at in range(WIDE):
            ids[at] = jnp.where(wide & (found == at), head, ids[at])
        found = found + wide.astype(jnp.int32)
    return ids


def outer(a, b):
    return lax.dot_general(a, b, (((1,), (1,)), ((), ())), preferred_element_type=jnp.float32)


def inner(a, b):
    return jnp.dot(a, b, preferred_element_type=jnp.float32)


def low(x):
    return x.astype(jnp.bfloat16)


def high(x):
    return x.astype(jnp.float32)


def slot(index):
    return pl.ds(index, 64, stride=SLOTS), slice(None)


def after_body(*refs):
    pass


def after(x, *others):
    return pl.pallas_call(
        after_body,
        out_shape=jax.ShapeDtypeStruct(x.shape, x.dtype),
        in_specs=[HBM] * (1 + len(others)),
        out_specs=HBM,
        input_output_aliases={0: 0},
    )(x, *others)


def pack_body(windows, query, key, value, pairs, queries, held, sems):
    ids = wide_heads(windows)
    tokens = query.shape[0]
    copies = []
    for at in range(WIDE):
        cols = lanes(ids[at])
        copies.append(pltpu.make_async_copy(query.at[:, cols], held.at[at], sems.at[at]))
        copies.append(
            pltpu.make_async_copy(value.at[:, cols], held.at[WIDE + at], sems.at[WIDE + at])
        )
        copies.append(pltpu.make_async_copy(key.at[:, cols], pairs.at[at], sems.at[2 * WIDE + at]))
    for copy in copies:
        copy.start()
    for copy in copies:
        copy.wait()
    for at in range(WIDE):
        queries[at] = held[at].T
        for row in range(0, tokens, DEPTH):
            pairs[WIDE + at, row : row + DEPTH] = held[WIDE + at, row : row + DEPTH].T


def quarter_body(weight, after, out, held, sems):
    rows = out.shape[0]
    first = lax.axis_index("co") * rows
    chunk = rows // 4
    loads = []
    stores = []
    for at in range(4):
        source = pl.ds(pl.multiple_of(first + at * chunk, chunk), chunk)
        here = pl.ds(at * chunk, chunk)
        loads.append(pltpu.make_async_copy(weight.at[source, :], held.at[here], sems.at[0, at]))
        stores.append(pltpu.make_async_copy(held.at[here], out.at[here], sems.at[1, at]))
    for load in loads:
        load.start()
    for load, store in zip(loads, stores):
        load.wait()
        store.start()
    for store in stores:
        store.wait()


def text_video_body(query, key, value, after, own_sums, far_sums, own_stats, far_stats, held):
    half = own_sums.shape[0]
    core = lax.axis_index("co")
    own_rows = pl.ds(pl.multiple_of(core * half, half), half)
    far_rows = pl.ds(pl.multiple_of((1 - core) * half, half), half)
    held[...] = jnp.zeros(held.shape, jnp.float32)
    for head in range(query.shape[1] // DEPTH):
        cols = slice(head * DEPTH, (head + 1) * DEPTH)
        asked = jnp.concatenate((query[own_rows, cols], query[far_rows, cols]), axis=0).T
        scores = inner(key[:, cols], asked) * SCALE
        peak = jnp.max(scores, axis=0, keepdims=True)
        weights = jnp.exp2(scores - peak)
        held[head : head + 1] = peak
        held[16 + head : 17 + head] = jnp.sum(weights, axis=0, keepdims=True)
        mixed = inner(low(weights).T, value[:, cols])
        own_sums[:, cols] = mixed[:half]
        far_sums[:, cols] = mixed[half:]
    stats = held[...].T
    own_stats[...] = stats[:half]
    far_stats[...] = stats[half:]


def text_join_body(sums, stats, far_sums, far_stats, text_key, text_value, *rest):
    out = rest[-1]
    half, width = sums.shape
    heads = width // DEPTH
    lane = lax.broadcasted_iota(jnp.int32, stats.shape, 1)
    held = jnp.zeros(stats.shape, jnp.float32)
    for head in range(heads):
        cols = slice(head * DEPTH, (head + 1) * DEPTH)
        first, second = stats[:, head : head + 1], far_stats[:, head : head + 1]
        top = jnp.maximum(first, second)
        first, second = jnp.exp2(first - top), jnp.exp2(second - top)
        total = stats[:, 16 + head : 17 + head] * first + far_stats[:, 16 + head : 17 + head] * second
        out[slot(head)] = sums[:, cols] * first + far_sums[:, cols] * second
        held = jnp.where(lane == head, top, jnp.where(lane == 16 + head, total, held))
        out[slot(heads + 1 + head)] = jnp.broadcast_to(high(text_key[:, cols]), (half, DEPTH))
        out[slot(2 * heads + 1 + head)] = jnp.broadcast_to(high(text_value[:, cols]), (half, DEPTH))
    out[slot(heads)] = held


def text_masks(count, rows, cols):
    place = 2 * lax.broadcasted_iota(jnp.int32, (rows, cols), 0)
    core = lax.axis_index("co")
    return place + core < count, place + 1 - core < count


def narrow_body(
    windows, count, query, key, value, queries, got, got_other, finished, out, sums, stats,
    text_keys, text_values, ids,
):
    heads = windows.shape[1]
    half = got.shape[0] // SLOTS
    for head in range(heads):
        for at, source in enumerate((got, got_other)):
            rows = slice(at * half, (at + 1) * half)
            text_keys[head, rows] = low(source[slot(heads + 1 + head)])
            text_values[head, rows] = low(source[slot(2 * heads + 1 + head)])
    found = jnp.int32(0)
    for head in range(heads):
        wide = (windows[0, head] > 1) | (windows[1, head] > 1) | (windows[2, head] > 1)
        ids[jnp.where(wide, heads, found)] = head
        found = found + 1 - wide.astype(jnp.int32)
    tokens = query.shape[0]
    valid = jnp.concatenate(
        [high(mask.astype(jnp.int32)) for mask in text_masks(count[0], half, DEPTH)], axis=0
    ) > 0.5

    def step(group, carry):
        for at in range(3):
            head = ids[group * 3 + at]
            cols = lanes(head)
            keys = jnp.concatenate((key[:, cols], text_keys[head]), axis=0)
            values = jnp.concatenate((value[:, cols], text_values[head]), axis=0).T
            asked = query[:, cols].T
            for first in range(0, tokens, DEPTH):
                scores = inner(keys, asked[:, first : first + DEPTH]) * SCALE
                near, text = scores[:tokens], jnp.where(valid, scores[tokens:], NEVER)
                peak = jnp.maximum(
                    jnp.max(near, axis=0, keepdims=True), jnp.max(text, axis=0, keepdims=True)
                )
                weights = jnp.exp2(jnp.concatenate((near, text), axis=0) - peak)
                total = jnp.sum(weights, axis=0, keepdims=True)
                mixed = inner(values, low(weights))
                out[first : first + DEPTH, cols] = low((mixed / total).T)
        return carry

    lax.fori_loop(0, (heads - WIDE) // 3, step, 0)
    row = lax.broadcasted_iota(jnp.int32, (stats.shape[1], DEPTH), 0)
    for at, head in enumerate(wide_heads(windows)):
        keys = text_keys[head]
        values = text_values[head].T
        for first in range(0, tokens, DEPTH):
            some = slice(first, first + DEPTH)
            scores = jnp.where(valid, inner(keys, queries[at, :, some]) * SCALE, NEVER)
            peak = jnp.max(scores, axis=0, keepdims=True)
            weights = jnp.exp2(scores - peak)
            stats[at, :, some] = jnp.where(row == 0, peak, jnp.sum(weights, axis=0, keepdims=True))
            sums[at, :, some] = inner(values, low(weights))


def place_ok(windows, head, a, c):
    row_at, zone, core = lax.axis_index("ha"), lax.axis_index("zh"), lax.axis_index("co")
    ok = jnp.bool_(True)
    if a > 0:
        ok = windows[1, head] > 1
        ok = ok & ((row_at > 0) if a == 1 else (row_at < lax.axis_size("ha") - 1))
    if c > 0:
        ok = ok & (windows[2, head] > 1)
    if c == 1:
        ok = ok & jnp.where(core == 0, zone > 0, zone < lax.axis_size("zh") - 1)
    return ok


def wide_walk(
    windows, tables, asked, before, keys, values, peak, total, mixed, counts, sems, finish
):
    ids = wide_heads(windows)
    tokens = asked[0].shape[2]
    places = list(tables)
    for at in range(WIDE):
        found = jnp.int32(0)
        for number, (a, c) in enumerate(places):
            source = tables[a, c]
            ok = place_ok(windows, ids[at], a, c)
            slot_at = at * len(places) + number
            rows = pl.ds(pl.multiple_of(found * tokens, tokens), tokens)

            @pl.when(ok)
            def _(source=source, slot_at=slot_at, rows=rows, at=at):
                pltpu.make_async_copy(source.at[at], keys.at[at, rows], sems.at[slot_at, 0]).start()
                pltpu.make_async_copy(
                    source.at[WIDE + at], values.at[at, rows], sems.at[slot_at, 1]
                ).start()

            found = found + ok.astype(jnp.int32)
        counts[at] = found
        counts[WIDE + at] = ids[at]
    any_tile = tables[places[0]]

    def head_step(at, carry):
        head = counts[WIDE + at]
        count = counts[at]
        for number, (a, c) in enumerate(places):

            @pl.when(place_ok(windows, head, a, c))
            def _(number=number):
                slot_at = at * len(places) + number
                whole = pl.ds(0, tokens)
                pltpu.make_async_copy(any_tile.at[0], keys.at[at, whole], sems.at[slot_at, 0]).wait()
                pltpu.make_async_copy(any_tile.at[0], values.at[at, whole], sems.at[slot_at, 1]).wait()

        before(at)

        def span(start, size, sources):
            rows = pl.ds(pl.multiple_of(start, tokens), size)
            key = keys[at, rows]
            value = values[at, rows]
            value = jnp.concatenate(
                [value[row : row + DEPTH] for row in range(0, size, DEPTH)], axis=1
            )
            for part, source in sources:
                for first in range(0, tokens, DEPTH):
                    some = slice(part * tokens + first, part * tokens + first + DEPTH)
                    scores = inner(key, source[at, :, first : first + DEPTH]) * SCALE
                    held = peak[:, some]
                    top = jnp.maximum(held, jnp.max(scores, axis=0, keepdims=True))
                    factor = jnp.exp2(held - top)
                    weights = jnp.exp2(scores - top)
                    total[:, some] = total[:, some] * factor + jnp.sum(
                        weights, axis=0, keepdims=True
                    )
                    mixed[:, some] = mixed[:, some] * factor + inner(value, low(weights))
                    peak[:, some] = top

        def spans(sources):
            @pl.when(count == len(places))
            def _():
                span(0, len(places) * tokens, sources)

            @pl.when(count < len(places))
            def _():
                threes = count // 3 if len(places) > 3 else 0

                def three(step, carry):
                    span(step * 3 * tokens, 3 * tokens, sources)
                    return carry

                def one(step, carry):
                    span(step * tokens, tokens, sources)
                    return carry

                if len(places) > 3:
                    lax.fori_loop(0, threes, three, 0)
                lax.fori_loop(threes * 3, count, one, 0)

        spans(((0, asked[0]),))

        @pl.when(windows[0, head] > 1)
        def _():
            spans(((1, asked[1]), (2, asked[2])))

        finish(at)
        return carry

    lax.fori_loop(0, WIDE, head_step, 0)


def wide_near_body(
    windows, own, left, right, own_in, left_in, right_in, queries, before, after,
    sums, stats, keys, values, peak, total, mixed, counts, sems,
):
    def start(at):
        peak[...] = jnp.full(peak.shape, NEVER, jnp.float32)
        total[...] = jnp.zeros(total.shape, jnp.float32)
        mixed[...] = jnp.zeros(mixed.shape, jnp.float32)

    def finish(at):
        sums[at] = mixed[...]
        row = lax.broadcasted_iota(jnp.int32, stats.shape[1:], 0)
        stats[at] = jnp.where(row == 0, peak[...], total[...])

    tables = {
        (0, 0): own, (0, 2): own_in, (1, 0): left, (1, 2): left_in, (2, 0): right, (2, 2): right_in
    }
    asked = (queries, before, after)
    wide_walk(
        windows, tables, asked, start, keys, values, peak, total, mixed, counts, sems, finish
    )


def wide_far_body(
    windows, own, left, right, queries, before, after, held_sums, held_stats,
    sums, stats, out0, out1, keys, values, peak, total, mixed, counts, sems,
):
    tokens = queries.shape[2]

    def start(at):
        peak[...] = held_stats[at, 0:1]
        total[...] = held_stats[at, 1:2]
        mixed[...] = held_sums[at]

    def finish(at):
        sums[at] = mixed[:, :tokens]
        row = lax.broadcasted_iota(jnp.int32, stats.shape[1:], 0)
        stats[at] = jnp.where(row == 0, peak[:, :tokens], total[:, :tokens])
        for part, out in ((1, out0), (2, out1)):
            some = slice(part * tokens, (part + 1) * tokens)
            top = high(low(peak[:, some]))
            factor = jnp.exp2(peak[:, some] - top)
            whole = total[:, some] * factor
            big = high(low(whole))
            row = lax.broadcasted_iota(jnp.int32, (16, tokens), 0)
            held = jnp.where(row == 0, top, jnp.where(row == 1, big, whole - big))
            out[at, :DEPTH] = low(mixed[:, some] * factor)
            out[at, DEPTH:] = low(held)

    tables = {(0, 1): own, (1, 1): left, (2, 1): right}
    asked = (queries, before, after)
    wide_walk(
        windows, tables, asked, start, keys, values, peak, total, mixed, counts, sems, finish
    )


def text_merge_body(query, count, got, got_other, after, out):
    heads = query.shape[1] // DEPTH
    core = lax.axis_index("co")
    chip = (
        lax.axis_index("ta") * lax.axis_size("ha") + lax.axis_index("ha")
    ) * lax.axis_size("zh") + lax.axis_index("zh")
    sources = got.shape[0] // SLOTS
    at = core * sources + chip
    block = high(query[pl.ds(pl.multiple_of(at // 16 * 16, 16), 16), :])
    row = lax.broadcasted_iota(jnp.int32, block.shape, 0)
    asked = jnp.sum(jnp.where(row == at % 16, block, 0.0), axis=0, keepdims=True)
    near, far = text_masks(count[0], sources, 1)
    stats = got[slot(heads)]
    blocks = []
    for head in range(heads):
        peak = stats[:, head : head + 1]
        mine = asked[:, head * DEPTH : (head + 1) * DEPTH]
        key_at, value_at = slot(heads + 1 + head), slot(2 * heads + 1 + head)
        first = jnp.sum(got[key_at] * mine, axis=1, keepdims=True) * SCALE
        second = jnp.sum(got_other[key_at] * mine, axis=1, keepdims=True) * SCALE
        first = jnp.where(near, first, NEVER)
        second = jnp.where(far, second, NEVER)
        top = jnp.max(jnp.maximum(peak, jnp.maximum(first, second)), axis=0, keepdims=True)
        factor = jnp.exp2(peak - top)
        first = jnp.exp2(first - top)
        second = jnp.exp2(second - top)
        whole = jnp.sum(
            factor * stats[:, 16 + head : 17 + head] + first + second, axis=0, keepdims=True
        )
        mixed = jnp.sum(
            factor * got[slot(head)] + first * got[value_at] + second * got_other[value_at],
            axis=0,
            keepdims=True,
        )
        blocks.append(mixed / whole)
    blocks.append(jnp.zeros((ENDS - heads, DEPTH), jnp.float32))
    chunk = jnp.concatenate(blocks, axis=0)
    for source in range(sources):
        out[source * ENDS : (source + 1) * ENDS] = chunk


def text_out_body(mine, other, out):
    half = mine.shape[0] // ENDS
    heads = out.shape[1] // DEPTH
    core = lax.axis_index("co")
    for source, place in ((mine, core), (other, 1 - core)):
        rows = pl.ds(pl.multiple_of(place * half, half), half)
        for head in range(heads):
            picked = source[pl.ds(head, half, stride=ENDS), :]
            out[rows, head * DEPTH : (head + 1) * DEPTH] = low(picked)


def final_body(
    windows, sums, stats, text_sums, text_stats, back0, back1, narrow, w_own, w_mine, w_other,
    hidden, modulation, final, out, attended, weight, updated, residual,
    spread, sems, *, parts,
):
    ids = wide_heads(windows)
    branch, core = lax.axis_index("cfg"), lax.axis_index("co")
    half, model = w_own.shape
    part_cols = model // parts
    first = pltpu.make_async_copy(narrow, attended, sems.at[parts, 0])
    first.start()
    copies = []
    for part in range(parts):
        cols = pl.ds(part * part_cols, part_cols)
        for at, (source, row) in enumerate(
            (
                (w_own, branch * half),
                (w_mine, (1 - branch) * half + core * (half // 2)),
                (w_other, (1 - branch) * half + (1 - core) * (half // 2)),
            )
        ):
            rows = pl.ds(pl.multiple_of(row, half // 2), source.shape[0])
            copies.append(
                pltpu.make_async_copy(
                    source.at[:, cols], weight.at[rows, cols], sems.at[part, at]
                )
            )
        copies.append(
            pltpu.make_async_copy(hidden.at[:, cols], residual.at[:, cols], sems.at[part, 3])
        )
    for copy in copies:
        copy.start()
    time_at = lax.axis_index("ta")
    inside = (time_at > 0, time_at < lax.axis_size("ta") - 1)
    first.wait()
    for at in range(WIDE):
        peaks = [stats[at, 0:1], text_stats[at, 0:1]]
        totals = [stats[at, 1:2], text_stats[at, 1:2]]
        for back, ok in zip((back0, back1), inside):
            rows = high(back[at, DEPTH:])
            peaks.append(jnp.where(ok, rows[0:1], NEVER))
            totals.append(jnp.where(ok, rows[1:2] + rows[2:3], 0.0))
        top = functools.reduce(jnp.maximum, peaks)
        factors = [jnp.exp2(peak - top) for peak in peaks]
        total = sum(factor * whole for factor, whole in zip(factors, totals))
        mixed = (
            sums[at] * factors[0]
            + text_sums[at] * factors[1]
            + high(back0[at, :DEPTH]) * factors[2]
            + high(back1[at, :DEPTH]) * factors[3]
        )
        attended[:, lanes(ids[at])] = low((mixed / total).T)
    tokens = attended.shape[0]
    pivot = None
    running = jnp.zeros((tokens, DEPTH), jnp.float32)
    squares = jnp.zeros((tokens, DEPTH), jnp.float32)
    for part in range(parts):
        cols = slice(part * part_cols, (part + 1) * part_cols)
        for copy in copies[4 * part : 4 * part + 4]:
            copy.wait()
        projected = inner(attended[...], weight[:, cols])
        fresh = high(residual[:, cols]) + modulation[0, :, cols] * projected
        if pivot is None:
            pivot = jnp.sum(fresh, axis=1, keepdims=True) / part_cols
        fresh = fresh - pivot
        updated[:, cols] = fresh
        for lane in range(0, part_cols, DEPTH):
            some = fresh[:, lane : lane + DEPTH]
            running = running + some
            squares = squares + some * some
    mean = jnp.sum(running, axis=1, keepdims=True) / model
    variance = jnp.sum(squares, axis=1, keepdims=True) / model - mean * mean
    factor = lax.rsqrt(jnp.maximum(variance, 0.0) + 1e-06)
    channels = final.shape[0]
    result = jnp.zeros((tokens, channels), jnp.float32)
    for part in range(parts):
        cols = slice(part * part_cols, (part + 1) * part_cols)
        normed = (updated[:, cols] - mean) * factor * (1.0 + modulation[2, :, cols])
        normed = normed + modulation[1, :, cols]
        result = result + outer(low(normed), final[:, cols])
    spread[:, :channels] = result
    columns = out.shape[1] // channels
    for column in range(columns):
        out[:, column * channels : (column + 1) * channels] = spread[
            pl.ds(column, tokens // columns, stride=columns), :
        ][:, :channels]


def shift(x, axis, step):
    size = lax.axis_size(axis)
    return lax.ppermute(x, axis, [(i, i + step) for i in range(size) if 0 <= i + step < size])


def swap_core(x):
    return lax.ppermute(x, "co", [(0, 1), (1, 0)])


def local(
    video_query, video_key, video_value, text_query, text_key, text_value, text_count, head_windows,
    hidden_state, out_weight, final_weight, modulation, guidance,
):
    frames, rows, cols, width = video_query.shape[1:]
    tokens = frames * rows * cols
    heads = head_windows.shape[0]
    text_len = text_query.shape[1]
    half_text = text_len // 2
    model = out_weight.shape[1]
    half_width = out_weight.shape[0]
    bf16, f32 = jnp.bfloat16, jnp.float32
    shape = jax.ShapeDtypeStruct
    query = video_query.reshape(tokens, width)
    key = video_key.reshape(tokens, width)
    value = video_value.reshape(tokens, width)
    text_query = text_query[0]
    windows = head_windows.T
    core = lax.axis_index("co")
    branch = lax.axis_index("cfg")
    zones = lax.axis_size("zh")

    pairs, queries = call(
        pack_body,
        (shape((2 * WIDE, tokens, DEPTH), bf16), shape((WIDE, DEPTH, tokens), bf16)),
        [SMEM, HBM, HBM, HBM],
        (VMEM, VMEM),
        [pltpu.VMEM((2 * WIDE, tokens, DEPTH), bf16), pltpu.SemaphoreType.DMA((3 * WIDE,))],
        8, 0, 4 * MIB,
        windows, query, key, value,
    )
    beside = [(2 * z + 1, 2 * z + 2) for z in range(zones - 1)]
    beside = beside + [(b, a) for a, b in beside]
    next_pairs = lax.ppermute(pairs, ("zh", "co"), beside)
    from_before = shift(queries, "ta", 1)
    from_after = shift(queries, "ta", -1)
    pairs_in = swap_core(pairs)
    left = shift(pairs, "ha", 1)
    right = shift(pairs, "ha", -1)

    part_shape = shape((half_text, width), f32)
    stat_shape = shape((half_text, DEPTH), f32)
    text_sums, far_sums, text_stats, far_stats = call(
        text_video_body,
        (part_shape, part_shape, stat_shape, stat_shape),
        [VMEM] * 3 + [HBM], (VMEM,) * 4, [pltpu.VMEM((DEPTH, DEPTH), f32)],
        16, 4 * text_len * tokens * width, 4 * tokens * width,
        text_query, key, value, pairs,
    )
    parcel = call(
        text_join_body,
        shape((SLOTS * half_text, DEPTH), f32),
        [VMEM] * 6 + [HBM] * 3, VMEM, [], 12, 0, 2 * MIB,
        text_sums, text_stats, swap_core(far_sums), swap_core(far_stats), text_key[0], text_value[0],
        next_pairs, left, right,
    )

    next_left = shift(next_pairs, "ha", 1)
    next_right = shift(next_pairs, "ha", -1)
    left_in = swap_core(left)
    right_in = swap_core(right)

    def at(branch_at, zone, core_at):
        return (branch_at * zones + zone) * 2 + core_at

    weight_pairs = []
    for z in range(zones):
        weight_pairs.append((at(0, z, 0), at(1, z, 0)))
        weight_pairs.append((at(0, (z + 1) % zones, 1), at(1, z, 1)))
    weight_pairs = weight_pairs + [(b, a) for a, b in weight_pairs]
    quarter = call(
        quarter_body,
        shape((half_width // 2, model), bf16),
        [HBM] * 2, HBM,
        [pltpu.VMEM((half_width // 2, model), bf16), pltpu.SemaphoreType.DMA((2, 4))],
        8, 0, 2 * half_width * model,
        out_weight, next_pairs,
    )
    w_mine = lax.ppermute(quarter, ("cfg", "zh", "co"), weight_pairs)
    parcel = after(parcel, quarter, pairs_in, left_in, right_in, from_before, from_after)
    got = lax.all_to_all(parcel, CHIPS, 0, 0, tiled=True)
    wide_sums = shape((WIDE, DEPTH, tokens), f32)
    wide_stats = shape((WIDE, 8, tokens), f32)
    lent = shape((WIDE, DEPTH + 16, tokens), bf16)
    def wide_scratch(places):
        return [
            pltpu.VMEM((WIDE, places * tokens, DEPTH), bf16),
            pltpu.VMEM((WIDE, places * tokens, DEPTH), bf16),
            pltpu.VMEM((1, 3 * tokens), f32),
            pltpu.VMEM((1, 3 * tokens), f32),
            pltpu.VMEM((DEPTH, 3 * tokens), f32),
            pltpu.SMEM((2 * WIDE,), jnp.int32),
            pltpu.SemaphoreType.DMA((WIDE * places, 2)),
        ]

    near_sums, near_stats = call(
        wide_near_body,
        (shape((WIDE, DEPTH, 3 * tokens), f32), shape((WIDE, 8, 3 * tokens), f32)),
        [SMEM] + [HBM] * 6 + [VMEM] * 3, (VMEM,) * 2,
        wide_scratch(6),
        24, 12 * WIDE * 6 * tokens * tokens * DEPTH, 8 * MIB,
        windows, pairs, left, right, pairs_in, left_in, right_in, queries, from_before, from_after,
    )
    sums, stats, to_before, to_after = call(
        wide_far_body,
        (wide_sums, wide_stats, lent, lent),
        [SMEM] + [HBM] * 3 + [VMEM] * 5, (VMEM,) * 4,
        wide_scratch(3),
        24, 12 * WIDE * 3 * tokens * tokens * DEPTH, 8 * MIB,
        windows, next_pairs, next_left, next_right, queries, from_before, from_after,
        near_sums, near_stats,
    )
    back_after = shift(to_before, "ta", -1)
    back_before = shift(to_after, "ta", 1)

    got = after(got, to_before)
    got_other = swap_core(got)
    finished = call(
        text_merge_body,
        shape((ENDS * half_text, DEPTH), f32),
        [VMEM, SMEM, VMEM, VMEM, HBM], VMEM, [], 16, 0, 3 * MIB,
        text_query, text_count, got, got_other, to_before,
    )
    finished = after(finished, back_before, back_after)
    w_mine = after(w_mine, finished)
    w_other = swap_core(w_mine)
    narrow, beside_sums, beside_stats = call(
        narrow_body,
        (shape((tokens, width), bf16), wide_sums, wide_stats),
        [SMEM, SMEM] + [VMEM] * 6 + [HBM], (VMEM,) * 3,
        [
            pltpu.VMEM((heads, text_len, DEPTH), bf16),
            pltpu.VMEM((heads, text_len, DEPTH), bf16),
            pltpu.SMEM((heads + 1,), jnp.int32),
        ],
        24, 4 * (heads - WIDE) * tokens * (tokens + text_len) * DEPTH, 5 * tokens * width * 2,
        windows, text_count, query, key, value, queries, got, got_other, finished,
    )

    text_mine = lax.all_to_all(finished, CHIPS, 0, 0, tiled=True)
    parts = 6
    branch_out = call(
        functools.partial(final_body, parts=parts),
        shape((frames * rows, cols * final_weight.shape[1]), f32),
        [SMEM] + [VMEM] * 6 + [HBM] * 5 + [VMEM] * 2, VMEM,
        [
            pltpu.VMEM((tokens, width), bf16),
            pltpu.VMEM((width, model), bf16),
            pltpu.VMEM((tokens, model), f32),
            pltpu.VMEM((tokens, model), bf16),
            pltpu.VMEM((tokens, DEPTH), f32),
            pltpu.SemaphoreType.DMA((parts + 1, 4)),
        ],
        40, 2 * tokens * width * model, 16 * MIB,
        windows, sums, stats, beside_sums, beside_stats, back_before, back_after, narrow,
        out_weight, w_mine, w_other,
        hidden_state.reshape(tokens, model), modulation.transpose(1, 0, 2), final_weight.T,
    )
    text_mine = after(text_mine, branch_out)
    text_out = call(
        text_out_body, shape((text_len, width), bf16), [VMEM, VMEM], VMEM, [], 8, 0, MIB,
        text_mine, swap_core(text_mine),
    )
    half_rows = rows // 2
    grid = branch_out.reshape(frames, rows, cols * final_weight.shape[1])
    kept = lax.dynamic_slice_in_dim(grid, branch * half_rows, half_rows, 1)
    sent = lax.dynamic_slice_in_dim(grid, (1 - branch) * half_rows, half_rows, 1)
    received = lax.ppermute(sent, "cfg", [(0, 1), (1, 0)])
    conditional = jnp.where(branch == 0, kept, received)
    unconditional = jnp.where(branch == 0, received, kept)
    guided = unconditional + guidance[0] * (conditional - unconditional)
    return (guided, text_out[None])


def solution(mesh):
    devices = mesh.devices.reshape(mesh.devices.shape[:3] + (mesh.devices.shape[3] // 2, 2))
    split = Mesh(devices, ("cfg", "ta", "ha", "zh", "co"))
    wa = ("zh", "co")
    everyone = ("ta", "ha", "zh", "co")
    video = P("cfg", "ta", "ha", wa, None)
    in_specs = (
        video, video, video,
        P("cfg", None, None),
        P("cfg", everyone, None),
        P("cfg", everyone, None),
        P("cfg"),
        P(),
        video,
        P("cfg", None),
        P(),
        P("cfg", None, None),
        P(),
    )
    out_specs = (P("ta", ("ha", "cfg"), wa), P("cfg", None, None))
    return jax.shard_map(local, mesh=split, in_specs=in_specs, out_specs=out_specs, check_vma=False)
```

time: 186 us -> 150 us (0.81)
  the two profiles are of different devices: /device:TPU:74 before, /device:TPU:1 now
where the time goes in v2:
time: 150 us; the launch traced here: 149 us
  Pallas kernels  65.5 us (44%)
  starting transfers between devices  57.2 us (38%)
  waiting for transfers between devices  22.8 us (15%)
  between operations  2.13 us (1%)
    pallas_call x10, Pallas kernels, call(): pl.pallas_call(body, grid=(1,), out_shape=out_shape, in_specs=in_specs, o...  65.5 us
    ppermute x8, starting transfers between devices, shift(): lax.ppermute(x, axis, [(i, i + step) for i in range(size) if 0 <= i + ste...  21.6 us
    ppermute x8, waiting for transfers between devices, shift(): lax.ppermute(x, axis, [(i, i + step) for i in range(size) if 0 <= i + ste...  17.7 us
    all_to_all x1, starting transfers between devices, local(): got = lax.all_to_all(parcel, CHIPS, 0, 0, tiled=True)  12.3 us
    all_to_all x1, starting transfers between devices, local(): text_mine = lax.all_to_all(finished, CHIPS, 0, 0, tiled=True)  11.5 us
    ppermute x1, starting transfers between devices, local(): next_pairs = lax.ppermute(pairs, ('zh', 'co'), beside)  5.74 us
    ppermute x8, starting transfers between devices, swap_core(): return lax.ppermute(x, 'co', [(0, 1), (1, 0)])  3.89 us
  transfers between devices with their start and end apart: 21, of which 7 were waited for; matrix products, arithmetic and copies ran while one was open for 1% of the time, Pallas kernels for 40%

profile of v2, /device:TPU:1, one launch (start us, length us, event | category | flops | bytes accessed | tf_op | source)
XLA Modules:
  0.0 149.1 jit_solution(441616085382473646)
XLA Ops:
  0.6 3.2 %shard_map.140 = (bf16[6,384,128]{2,1,0:T(8,128)(2,1)}, bf16[3,128,384]{2,1,0:T(8,128)(2,1)}) custom-call(s32[3,12]{1,0:T(4,128)} %bitcast.35, bf16[384,1536]{1,0:T(8,128)(2,1)} %bitcast.25, bf16[384,1536]{1,0:T(8,128)(2,1)} %bitcast.19, bf16[384,1536]{1,0:T(8,128)(2,1)} %bitcast.22), custom_call_target="tpu_custom_call" | custom-call | bytes 4194304 | tf_op jit(solution)/shard_map/pallas_call | solution.py:28
  3.9 4.8 %collective-permute-start.5 = (bf16[6,384,128]{2,1,0:T(8,128)(2,1)}, bf16[6,384,128]{2,1,0:T(8,128)(2,1)}, u32[]{:S(2)}, u32[]{:S(2)}) collective-permute-start(bf16[6,384,128]{2,1,0:T(8,128)(2,1)} %get-tuple-element.17.own.after), channel_id=1, source_target_pairs={{0,8},{8,16},{16,24},{1,9},{9,17},{17,25},{2,10},{10,18},{18,26},{... | collective-permute-start | bytes 1769480 | tf_op jit(solution)/shard_map/ppermute | solution.py:536
  9.9 5.7 %collective-permute-start = (bf16[6,384,128]{2,1,0:T(8,128)(2,1)}, bf16[6,384,128]{2,1,0:T(8,128)(2,1)}, u32[]{:S(2)}, u32[]{:S(2)}) collective-permute-start(bf16[6,384,128]{2,1,0:T(8,128)(2,1)} %get-tuple-element.17.own.after), channel_id=1, source_target_pairs={{1,2},{3,4},{5,6},{2,1},{4,3},{6,5},{9,10},{11,12},{13,14},{10,9},... | collective-permute-start | bytes 1769480 | tf_op jit(solution)/shard_map/ppermute | solution.py:576
  15.7 3.7 %shard_map.143 = (f32[64,1536]{1,0:T(8,128)}, f32[64,1536]{1,0:T(8,128)}, f32[64,128]{1,0:T(8,128)}, f32[64,128]{1,0:T(8,128)}) custom-call(bf16[128,1536]{1,0:T(8,128)(2,1)} %bitcast.28, bf16[384,1536]{1,0:T(8,128)(2,1)} %bitcast.20, bf16[384,1536]{1,0:T(8,128)(2,1)} %bitcast.23, bf16[6,384,128]{2,1,0:T(8,128)(2,1)} %get-tuple-element.17.own.after), custom_call_target="tpu_custom_call" | custom-call | flops 301989888 | bytes 2359296 | tf_op jit(solution)/shard_map/pallas_call | solution.py:28
  22.0 2.7 %collective-permute-done.6.right.rest_2_ = bf16[6,384,128]{2,1,0:T(8,128)(2,1)} collective-permute-done((bf16[6,384,128]{2,1,0:T(8,128)(2,1)}, bf16[6,384,128]{2,1,0:T(8,128)(2,1)}, u32[]{:S(2)}, u32[]{:S(2)}) %collective-permute-start.6) | collective-permute-done | bytes 589856 | tf_op jit(solution)/shard_map/ppermute | solution.py:536
  24.7 1.9 %collective-permute-start.9 = (bf16[6,384,128]{2,1,0:T(8,128)(2,1)}, bf16[6,384,128]{2,1,0:T(8,128)(2,1)}, u32[]{:S(2)}, u32[]{:S(2)}) collective-permute-start(bf16[6,384,128]{2,1,0:T(8,128)(2,1)} %collective-permute-done.6.right.rest_2_), channel_id=1, source_target_pairs={{0,1},{1,0},{2,3},{3,2},{4,5},{5,4},{6,7},{7,6},{8,9},{9,8},{10,11... | collective-permute-start | bytes 1769480 | tf_op jit(solution)/shard_map/ppermute | solution.py:540
  26.6 3.9 %collective-permute-start.3 = (bf16[3,128,384]{2,1,0:T(8,128)(2,1)}, bf16[3,128,384]{2,1,0:T(8,128)(2,1)}, u32[]{:S(2)}, u32[]{:S(2)}) collective-permute-start(bf16[3,128,384]{2,1,0:T(8,128)(2,1)} %get-tuple-element.18.queries), channel_id=1, source_target_pairs={{0,32},{32,64},{64,96},{1,33},{33,65},{65,97},{2,34},{34,66},{66,9... | collective-permute-start | bytes 884744 | tf_op jit(solution)/shard_map/ppermute | solution.py:536
  31.8 2.6 %shard_map.145.refs_1_ = bf16[384,3072]{1,0:T(8,128)(2,1)} custom-call(bf16[768,3072]{1,0:T(8,128)(2,1)} %w_own.1, bf16[6,384,128]{2,1,0:T(8,128)(2,1)} %collective-permute-done.own.rest_0_.after), custom_call_target="tpu_custom_call" | custom-call | bytes 4718592 | tf_op jit(solution)/shard_map/pallas_call | solution.py:28
  34.4 3.8 %shard_map.144.refs_0_ = f32[2560,128]{1,0:T(8,128)} custom-call(f32[64,1536]{1,0:T(8,128)} %get-tuple-element.23.sums, f32[64,128]{1,0:T(8,128)} %get-tuple-element.24.stats, f32[64,1536]{1,0:T(8,128)} %collective-permute-done.10.far_sums, f32[64,128]{1,0:T(8,128)} %collective-permute-done.11.far_stats, bf16[1,1536]{1,0:T(2,128)(2,1)} %bitcast.40, ...), custom_call_target="tpu_custom_call" | custom-call | bytes 2097152 | tf_op jit(solution)/shard_map/pallas_call | solution.py:28
  38.1 2.9 %collective-permute-done.4.after.refs_6_ = bf16[3,128,384]{2,1,0:T(8,128)(2,1)} collective-permute-done((bf16[3,128,384]{2,1,0:T(8,128)(2,1)}, bf16[3,128,384]{2,1,0:T(8,128)(2,1)}, u32[]{:S(2)}, u32[]{:S(2)}) %collective-permute-start.4) | collective-permute-done | bytes 294944 | tf_op jit(solution)/shard_map/ppermute | solution.py:536
  41.0 12.3 %all-to-all-start = ((f32[64,40,128]{2,1,0:T(8,128)}), f32[64,40,128]{2,1,0:T(8,128)}, u32[]{:S(2)}, u32[]{:S(2)}) async-start(f32[64,40,128]{2,1,0:T(8,128)} %bitcast.18), calls=%async_computation | async-start | bytes 2621440 | tf_op jit(solution)/shard_map/all_to_all | solution.py:623
  53.4 2.1 %collective-permute-start.15 = (bf16[384,3072]{1,0:T(8,128)(2,1)}, bf16[384,3072]{1,0:T(8,128)(2,1)}, u32[]{:S(2)}, u32[]{:S(2)}) collective-permute-start(bf16[384,3072]{1,0:T(8,128)(2,1)} %shard_map.145.refs_1_), channel_id=1, source_target_pairs={{0,128},{3,129},{2,130},{5,131},{4,132},{7,133},{6,134},{1,135},{1... | collective-permute-start | bytes 7077896 | tf_op jit(solution)/shard_map/ppermute | solution.py:621
  55.5 3.9 %collective-permute-start.1 = (bf16[6,384,128]{2,1,0:T(8,128)(2,1)}, bf16[6,384,128]{2,1,0:T(8,128)(2,1)}, u32[]{:S(2)}, u32[]{:S(2)}) collective-permute-start(bf16[6,384,128]{2,1,0:T(8,128)(2,1)} %collective-permute-done.own.rest_0_.after), channel_id=1, source_target_pairs={{0,8},{8,16},{16,24},{1,9},{9,17},{17,25},{2,10},{10,18},{18,26},{... | collective-permute-start | bytes 1769480 | tf_op jit(solution)/shard_map/ppermute | solution.py:536
  60.7 14.6 %shard_map.141 = (f32[3,128,1152]{2,1,0:T(8,128)}, f32[3,8,1152]{2,1,0:T(8,128)}) custom-call(s32[3,12]{1,0:T(4,128)} %bitcast.36, bf16[6,384,128]{2,1,0:T(8,128)(2,1)} %get-tuple-element.17.own.after, bf16[6,384,128]{2,1,0:T(8,128)(2,1)} %collective-permute-done.5.left.rest_1_, bf16[6,384,128]{2,1,0:T(8,128)(2,1)} %collective-permute-done.6.right.rest_2_, ...), custom_call_target="tpu_custom_call" | custom-call | flops 4076863488 | bytes 8388608 | tf_op jit(solution)/shard_map/pallas_call | solution.py:28
  75.3 8.0 %collective-permute-done.2.right = bf16[6,384,128]{2,1,0:T(8,128)(2,1)} collective-permute-done((bf16[6,384,128]{2,1,0:T(8,128)(2,1)}, bf16[6,384,128]{2,1,0:T(8,128)(2,1)}, u32[]{:S(2)}, u32[]{:S(2)}) %collective-permute-start.2) | collective-permute-done | bytes 589856 | tf_op jit(solution)/shard_map/ppermute | solution.py:536
  83.2 10.4 %shard_map.142 = (f32[3,128,384]{2,1,0:T(8,128)}, f32[3,8,384]{2,1,0:T(8,128)}, bf16[3,144,384]{2,1,0:T(8,128)(2,1)}, bf16[3,144,384]{2,1,0:T(8,128)(2,1)}) custom-call(s32[3,12]{1,0:T(4,128)} %bitcast.37, bf16[6,384,128]{2,1,0:T(8,128)(2,1)} %collective-permute-done.own.rest_0_.after, bf16[6,384,128]{2,1,0:T(8,128)(2,1)} %collective-permute-done.1.left, ...), custom_call_target="tpu_custom_call" | custom-call | flops 2038431744 | bytes 8388608 | tf_op jit(solution)/shard_map/pallas_call | solution.py:28
  93.8 3.8 %collective-permute-start.13 = (bf16[3,144,384]{2,1,0:T(8,128)(2,1)}, bf16[3,144,384]{2,1,0:T(8,128)(2,1)}, u32[]{:S(2)}, u32[]{:S(2)}) collective-permute-start(bf16[3,144,384]{2,1,0:T(8,128)(2,1)} %get-tuple-element.28), channel_id=1, source_target_pairs={{0,32},{32,64},{64,96},{1,33},{33,65},{65,97},{2,34},{34,66},{66,9... | collective-permute-start | bytes 995336 | tf_op jit(solution)/shard_map/ppermute | solution.py:536
  99.6 4.6 %shard_map.148.refs_0_ = f32[1024,128]{1,0:T(8,128)} custom-call(bf16[128,1536]{1,0:T(8,128)(2,1)} %bitcast.29, s32[1]{0:T(128)S(6)} %copy.25.count, f32[2560,128]{1,0:T(8,128)} %shard_map.147.got, f32[2560,128]{1,0:T(8,128)} %collective-permute-done.12.got_other, bf16[3,144,384]{2,1,0:T(8,128)(2,1)} %get-tuple-element.27.refs_1_.after), custom_call_target="tpu_custom_call" | custom-call | bytes 3145728 | tf_op jit(solution)/shard_map/pallas_call | solution.py:28
  104.2 4.2 %collective-permute-done.14.refs_2_.back1 = bf16[3,144,384]{2,1,0:T(8,128)(2,1)} collective-permute-done((bf16[3,144,384]{2,1,0:T(8,128)(2,1)}, bf16[3,144,384]{2,1,0:T(8,128)(2,1)}, u32[]{:S(2)}, u32[]{:S(2)}) %collective-permute-start.14) | collective-permute-done | bytes 331808 | tf_op jit(solution)/shard_map/ppermute | solution.py:536
  110.0 11.5 %all-to-all-start.1 = ((f32[64,16,128]{2,1,0:T(8,128)}), f32[64,16,128]{2,1,0:T(8,128)}, u32[]{:S(2)}, u32[]{:S(2)}) async-start(f32[64,16,128]{2,1,0:T(8,128)} %bitcast.14), calls=%async_computation.1 | async-start | bytes 1048576 | tf_op jit(solution)/shard_map/all_to_all | solution.py:682
  121.5 8.7 %shard_map.150 = (bf16[384,1536]{1,0:T(8,128)(2,1)}, f32[3,128,384]{2,1,0:T(8,128)}, f32[3,8,384]{2,1,0:T(8,128)}) custom-call(s32[3,12]{1,0:T(4,128)} %bitcast.38, s32[1]{0:T(128)S(6)} %copy.25.count, bf16[384,1536]{1,0:T(8,128)(2,1)} %bitcast.26, bf16[384,1536]{1,0:T(8,128)(2,1)} %bitcast.21, bf16[384,1536]{1,0:T(8,128)(2,1)} %bitcast.24, ...), custom_call_target="tpu_custom_call" | custom-call | flops 905969664 | bytes 5898240 | tf_op jit(solution)/shard_map/pallas_call | solution.py:28
  130.2 11.7 %shard_map.152.refs_1_ = f32[48,512]{1,0:T(8,128)} custom-call(s32[3,12]{1,0:T(4,128)} %bitcast.39, f32[3,128,384]{2,1,0:T(8,128)} %get-tuple-element.21.sums, f32[3,8,384]{2,1,0:T(8,128)} %get-tuple-element.22.stats, f32[3,128,384]{2,1,0:T(8,128)} %get-tuple-element.29.text_sums, f32[3,8,384]{2,1,0:T(8,128)} %get-tuple-element.30.text_stats, ...), custom_call_target="tpu_custom_call" | custom-call | flops 3623878656 | bytes 16777216 | tf_op jit(solution)/shard_map/pallas_call | solution.py:28
  144.0 2.3 %collective-permute-done.17 = f32[6,4,512]{2,1,0:T(4,128)S(1)} collective-permute-done((f32[6,4,512]{2,1,0:T(4,128)S(1)}, f32[6,4,512]{2,1,0:T(4,128)S(1)}, u32[]{:S(2)}, u32[]{:S(2)}) %collective-permute-start.17) | collective-permute-done | bytes 49184 | tf_op jit(solution)/shard_map/ppermute | solution.py:710
  146.9 2.2 %shard_map.154 = bf16[128,1536]{1,0:T(8,128)(2,1)} custom-call(f32[1024,128]{1,0:T(8,128)} %shard_map.153.mine, f32[1024,128]{1,0:T(8,128)} %collective-permute-done.18.other), custom_call_target="tpu_custom_call" | custom-call | bytes 1048576 | tf_op jit(solution)/shard_map/pallas_call | solution.py:28
  (37 shorter events, 11.6 us)
Async XLA Ops:
  3.9 17.8 %collective-permute-start.5 = (bf16[6,384,128]{2,1,0:T(8,128)(2,1)}, bf16[6,384,128]{2,1,0:T(8,128)(2,1)}, u32[]{:S(2)}, u32[]{:S(2)}) collective-permute-start(bf16[6,384,128]{2,1,0:T(8,128)(2,1)} %get-tuple-element.17.own.after), channel_id=1, source_target_pairs={{0,8},{8,16},{16,24},{1,9},{9,17},{17,25},{2,10},{10,18},{18,26},{... | collective-permute-start | bytes 1769480 | tf_op jit(solution)/shard_map/ppermute | solution.py:536
  8.6 16.1 %collective-permute-start.6 = (bf16[6,384,128]{2,1,0:T(8,128)(2,1)}, bf16[6,384,128]{2,1,0:T(8,128)(2,1)}, u32[]{:S(2)}, u32[]{:S(2)}) collective-permute-start(bf16[6,384,128]{2,1,0:T(8,128)(2,1)} %get-tuple-element.17.own.after), channel_id=1, source_target_pairs={{8,0},{16,8},{24,16},{9,1},{17,9},{25,17},{10,2},{18,10},{26,18},{... | collective-permute-start | bytes 1769480 | tf_op jit(solution)/shard_map/ppermute | solution.py:536
  9.9 20.6 %collective-permute-start = (bf16[6,384,128]{2,1,0:T(8,128)(2,1)}, bf16[6,384,128]{2,1,0:T(8,128)(2,1)}, u32[]{:S(2)}, u32[]{:S(2)}) collective-permute-start(bf16[6,384,128]{2,1,0:T(8,128)(2,1)} %get-tuple-element.17.own.after), channel_id=1, source_target_pairs={{1,2},{3,4},{5,6},{2,1},{4,3},{6,5},{9,10},{11,12},{13,14},{10,9},... | collective-permute-start | bytes 1769480 | tf_op jit(solution)/shard_map/ppermute | solution.py:576
  19.4 7.2 %collective-permute-start.10 = (f32[64,1536]{1,0:T(8,128)}, f32[64,1536]{1,0:T(8,128)}, u32[]{:S(2)}, u32[]{:S(2)}) collective-permute-start(f32[64,1536]{1,0:T(8,128)} %get-tuple-element.25), channel_id=1, source_target_pairs={{0,1},{1,0},{2,3},{3,2},{4,5},{5,4},{6,7},{7,6},{8,9},{9,8},{10,11... | collective-permute-start | bytes 1179656 | tf_op jit(solution)/shard_map/ppermute | solution.py:540
  19.4 2.1 %collective-permute-start.11 = (f32[64,128]{1,0:T(8,128)}, f32[64,128]{1,0:T(8,128)}, u32[]{:S(2)}, u32[]{:S(2)}) collective-permute-start(f32[64,128]{1,0:T(8,128)} %get-tuple-element.26), channel_id=1, source_target_pairs={{0,1},{1,0},{2,3},{3,2},{4,5},{5,4},{6,7},{7,6},{8,9},{9,8},{10,11... | collective-permute-start | bytes 98312 | tf_op jit(solution)/shard_map/ppermute | solution.py:540
  21.5 19.5 %collective-permute-start.7 = (bf16[6,384,128]{2,1,0:T(8,128)(2,1)}, bf16[6,384,128]{2,1,0:T(8,128)(2,1)}, u32[]{:S(2)}, u32[]{:S(2)}) collective-permute-start(bf16[6,384,128]{2,1,0:T(8,128)(2,1)} %get-tuple-element.17.own.after), channel_id=1, source_target_pairs={{0,1},{1,0},{2,3},{3,2},{4,5},{5,4},{6,7},{7,6},{8,9},{9,8},{10,11... | collective-permute-start | bytes 1769480 | tf_op jit(solution)/shard_map/ppermute | solution.py:540
  21.6 19.4 %collective-permute-start.8 = (bf16[6,384,128]{2,1,0:T(8,128)(2,1)}, bf16[6,384,128]{2,1,0:T(8,128)(2,1)}, u32[]{:S(2)}, u32[]{:S(2)}) collective-permute-start(bf16[6,384,128]{2,1,0:T(8,128)(2,1)} %collective-permute-done.5.left.rest_1_), channel_id=1, source_target_pairs={{0,1},{1,0},{2,3},{3,2},{4,5},{5,4},{6,7},{7,6},{8,9},{9,8},{10,11... | collective-permute-start | bytes 1769480 | tf_op jit(solution)/shard_map/ppermute | solution.py:540
  24.7 16.3 %collective-permute-start.9 = (bf16[6,384,128]{2,1,0:T(8,128)(2,1)}, bf16[6,384,128]{2,1,0:T(8,128)(2,1)}, u32[]{:S(2)}, u32[]{:S(2)}) collective-permute-start(bf16[6,384,128]{2,1,0:T(8,128)(2,1)} %collective-permute-done.6.right.rest_2_), channel_id=1, source_target_pairs={{0,1},{1,0},{2,3},{3,2},{4,5},{5,4},{6,7},{7,6},{8,9},{9,8},{10,11... | collective-permute-start | bytes 1769480 | tf_op jit(solution)/shard_map/ppermute | solution.py:540
  26.6 11.6 %collective-permute-start.3 = (bf16[3,128,384]{2,1,0:T(8,128)(2,1)}, bf16[3,128,384]{2,1,0:T(8,128)(2,1)}, u32[]{:S(2)}, u32[]{:S(2)}) collective-permute-start(bf16[3,128,384]{2,1,0:T(8,128)(2,1)} %get-tuple-element.18.queries), channel_id=1, source_target_pairs={{0,32},{32,64},{64,96},{1,33},{33,65},{65,97},{2,34},{34,66},{66,9... | collective-permute-start | bytes 884744 | tf_op jit(solution)/shard_map/ppermute | solution.py:536
  30.5 10.5 %collective-permute-start.4 = (bf16[3,128,384]{2,1,0:T(8,128)(2,1)}, bf16[3,128,384]{2,1,0:T(8,128)(2,1)}, u32[]{:S(2)}, u32[]{:S(2)}) collective-permute-start(bf16[3,128,384]{2,1,0:T(8,128)(2,1)} %get-tuple-element.18.queries), channel_id=1, source_target_pairs={{32,0},{64,32},{96,64},{33,1},{65,33},{97,65},{34,2},{66,34},{98,6... | collective-permute-start | bytes 884744 | tf_op jit(solution)/shard_map/ppermute | solution.py:536
  41.0 52.6 %all-to-all-start = ((f32[64,40,128]{2,1,0:T(8,128)}), f32[64,40,128]{2,1,0:T(8,128)}, u32[]{:S(2)}, u32[]{:S(2)}) async-start(f32[64,40,128]{2,1,0:T(8,128)} %bitcast.18), calls=%async_computation | async-start | bytes 2621440 | tf_op jit(solution)/shard_map/all_to_all | solution.py:623
  53.4 56.1 %collective-permute-start.15 = (bf16[384,3072]{1,0:T(8,128)(2,1)}, bf16[384,3072]{1,0:T(8,128)(2,1)}, u32[]{:S(2)}, u32[]{:S(2)}) collective-permute-start(bf16[384,3072]{1,0:T(8,128)(2,1)} %shard_map.145.refs_1_), channel_id=1, source_target_pairs={{0,128},{3,129},{2,130},{5,131},{4,132},{7,133},{6,134},{1,135},{1... | collective-permute-start | bytes 7077896 | tf_op jit(solution)/shard_map/ppermute | solution.py:621
  55.5 19.8 %collective-permute-start.1 = (bf16[6,384,128]{2,1,0:T(8,128)(2,1)}, bf16[6,384,128]{2,1,0:T(8,128)(2,1)}, u32[]{:S(2)}, u32[]{:S(2)}) collective-permute-start(bf16[6,384,128]{2,1,0:T(8,128)(2,1)} %collective-permute-done.own.rest_0_.after), channel_id=1, source_target_pairs={{0,8},{8,16},{16,24},{1,9},{9,17},{17,25},{2,10},{10,18},{18,26},{... | collective-permute-start | bytes 1769480 | tf_op jit(solution)/shard_map/ppermute | solution.py:536
  59.4 23.8 %collective-permute-start.2 = (bf16[6,384,128]{2,1,0:T(8,128)(2,1)}, bf16[6,384,128]{2,1,0:T(8,128)(2,1)}, u32[]{:S(2)}, u32[]{:S(2)}) collective-permute-start(bf16[6,384,128]{2,1,0:T(8,128)(2,1)} %collective-permute-done.own.rest_0_.after), channel_id=1, source_target_pairs={{8,0},{16,8},{24,16},{9,1},{17,9},{25,17},{10,2},{18,10},{26,18},{... | collective-permute-start | bytes 1769480 | tf_op jit(solution)/shard_map/ppermute | solution.py:536
  93.7 5.9 %collective-permute-start.12 = (f32[2560,128]{1,0:T(8,128)}, f32[2560,128]{1,0:T(8,128)}, u32[]{:S(2)}, u32[]{:S(2)}) collective-permute-start(f32[2560,128]{1,0:T(8,128)} %shard_map.147.got), channel_id=1, source_target_pairs={{0,1},{1,0},{2,3},{3,2},{4,5},{5,4},{6,7},{7,6},{8,9},{9,8},{10,11... | collective-permute-start | bytes 3932168 | tf_op jit(solution)/shard_map/ppermute | solution.py:540
  93.8 10.4 %collective-permute-start.13 = (bf16[3,144,384]{2,1,0:T(8,128)(2,1)}, bf16[3,144,384]{2,1,0:T(8,128)(2,1)}, u32[]{:S(2)}, u32[]{:S(2)}) collective-permute-start(bf16[3,144,384]{2,1,0:T(8,128)(2,1)} %get-tuple-element.28), channel_id=1, source_target_pairs={{0,32},{32,64},{64,96},{1,33},{33,65},{65,97},{2,34},{34,66},{66,9... | collective-permute-start | bytes 995336 | tf_op jit(solution)/shard_map/ppermute | solution.py:536
  97.6 10.8 %collective-permute-start.14 = (bf16[3,144,384]{2,1,0:T(8,128)(2,1)}, bf16[3,144,384]{2,1,0:T(8,128)(2,1)}, u32[]{:S(2)}, u32[]{:S(2)}) collective-permute-start(bf16[3,144,384]{2,1,0:T(8,128)(2,1)} %get-tuple-element.27.refs_1_.after), channel_id=1, source_target_pairs={{32,0},{64,32},{96,64},{33,1},{65,33},{97,65},{34,2},{66,34},{98,6... | collective-permute-start | bytes 995336 | tf_op jit(solution)/shard_map/ppermute | solution.py:536
  109.5 20.7 %collective-permute-start.16 = (bf16[384,3072]{1,0:T(8,128)(2,1)}, bf16[384,3072]{1,0:T(8,128)(2,1)}, u32[]{:S(2)}, u32[]{:S(2)}) collective-permute-start(bf16[384,3072]{1,0:T(8,128)(2,1)} %shard_map.151.w_mine), channel_id=1, source_target_pairs={{0,1},{1,0},{2,3},{3,2},{4,5},{5,4},{6,7},{7,6},{8,9},{9,8},{10,11... | collective-permute-start | bytes 7077896 | tf_op jit(solution)/shard_map/ppermute | solution.py:540
  110.0 31.9 %all-to-all-start.1 = ((f32[64,16,128]{2,1,0:T(8,128)}), f32[64,16,128]{2,1,0:T(8,128)}, u32[]{:S(2)}, u32[]{:S(2)}) async-start(f32[64,16,128]{2,1,0:T(8,128)} %bitcast.14), calls=%async_computation.1 | async-start | bytes 1048576 | tf_op jit(solution)/shard_map/all_to_all | solution.py:682
  141.9 4.4 %copy-start = (f32[48,512]{1,0:T(8,128)S(1)}, f32[48,512]{1,0:T(8,128)}, u32[]{:S(2)}) copy-start(f32[48,512]{1,0:T(8,128)} %shard_map.152.refs_1_) | copy-start | bytes 294916
  142.0 5.0 %collective-permute-start.18 = (f32[1024,128]{1,0:T(8,128)}, f32[1024,128]{1,0:T(8,128)}, u32[]{:S(2)}, u32[]{:S(2)}) collective-permute-start(f32[1024,128]{1,0:T(8,128)} %shard_map.153.mine), channel_id=1, source_target_pairs={{0,1},{1,0},{2,3},{3,2},{4,5},{5,4},{6,7},{7,6},{8,9},{9,8},{10,11... | collective-permute-start | bytes 1572872 | tf_op jit(solution)/shard_map/ppermute | solution.py:540
  143.3 3.0 %collective-permute-start.17 = (f32[6,4,512]{2,1,0:T(4,128)S(1)}, f32[6,4,512]{2,1,0:T(4,128)S(1)}, u32[]{:S(2)}, u32[]{:S(2)}) collective-permute-start(f32[6,4,512]{2,1,0:T(4,128)S(1)} %constant_dynamic-slice_fusion), channel_id=1, source_target_pairs={{0,128},{128,0},{1,129},{129,1},{2,130},{130,2},{3,131},{131,3},{4... | collective-permute-start | bytes 147464 | tf_op jit(solution)/shard_map/ppermute | solution.py:710

commit v3 on v2

--- a/solution.py
+++ b/solution.py
@@ -13,7 +13,7 @@
 WIDE = 3
 NEVER = -(2.0**100)
 CHIPS = ("ta", "ha", "zh")
-SLOTS = 40
+SLOTS = 56
 ENDS = 16
 LOG2E = math.log2(math.e)
 SCALE = LOG2E / math.sqrt(DEPTH)
@@ -86,71 +86,72 @@
     )(x, *others)
 
 
-def pack_body(windows, query, key, value, pairs, queries, held, sems):
+def front_body(
+    windows, text, query, key_at, value_at, weight,
+    pairs, queries, quarter, own_sums, far_sums, own_stats, far_stats,
+    key, value, held, stats, passing, sems, weight_sems,
+):
     ids = wide_heads(windows)
     tokens = query.shape[0]
-    copies = []
+    copies = [
+        pltpu.make_async_copy(key_at, key, sems.at[WIDE]),
+        pltpu.make_async_copy(value_at, value, sems.at[WIDE + 1]),
+    ]
     for at in range(WIDE):
-        cols = lanes(ids[at])
-        copies.append(pltpu.make_async_copy(query.at[:, cols], held.at[at], sems.at[at]))
-        copies.append(
-            pltpu.make_async_copy(value.at[:, cols], held.at[WIDE + at], sems.at[WIDE + at])
-        )
-        copies.append(pltpu.make_async_copy(key.at[:, cols], pairs.at[at], sems.at[2 * WIDE + at]))
+        copies.append(pltpu.make_async_copy(query.at[:, lanes(ids[at])], held.at[at], sems.at[at]))
     for copy in copies:
         copy.start()
-    for copy in copies:
-        copy.wait()
-    for at in range(WIDE):
-        queries[at] = held[at].T
-        for row in range(0, tokens, DEPTH):
-            pairs[WIDE + at, row : row + DEPTH] = held[WIDE + at, row : row + DEPTH].T
-
-
-def quarter_body(weight, after, out, held, sems):
-    rows = out.shape[0]
-    first = lax.axis_index("co") * rows
+    core = lax.axis_index("co")
+    rows = quarter.shape[0]
     chunk = rows // 4
     loads = []
     stores = []
     for at in range(4):
-        source = pl.ds(pl.multiple_of(first + at * chunk, chunk), chunk)
+        source = pl.ds(pl.multiple_of(core * rows + at * chunk, chunk), chunk)
         here = pl.ds(at * chunk, chunk)
-        loads.append(pltpu.make_async_copy(weight.at[source, :], held.at[here], sems.at[0, at]))
-        stores.append(pltpu.make_async_copy(held.at[here], out.at[here], sems.at[1, at]))
+        loads.append(
+            pltpu.make_async_copy(weight.at[source, :], passing.at[here], weight_sems.at[0, at])
+        )
+        stores.append(
+            pltpu.make_async_copy(passing.at[here], quarter.at[here], weight_sems.at[1, at])
+        )
+    for copy in copies:
+        copy.wait()
     for load in loads:
         load.start()
-    for load, store in zip(loads, stores):
-        load.wait()
-        store.start()
-    for store in stores:
-        store.wait()
-
-
-def text_video_body(query, key, value, after, own_sums, far_sums, own_stats, far_stats, held):
+    for at in range(WIDE):
+        queries[at] = held[at].T
+        pairs[at] = key[:, lanes(ids[at])]
+        picked = value[:, lanes(ids[at])]
+        for row in range(0, tokens, DEPTH):
+            pairs[WIDE + at, row : row + DEPTH] = picked[row : row + DEPTH].T
     half = own_sums.shape[0]
-    core = lax.axis_index("co")
     own_rows = pl.ds(pl.multiple_of(core * half, half), half)
     far_rows = pl.ds(pl.multiple_of((1 - core) * half, half), half)
-    held[...] = jnp.zeros(held.shape, jnp.float32)
-    for head in range(query.shape[1] // DEPTH):
+    stats[...] = jnp.zeros(stats.shape, jnp.float32)
+    for head in range(text.shape[1] // DEPTH):
+        if head % 3 == 2:
+            loads[head // 3].wait()
+            stores[head // 3].start()
         cols = slice(head * DEPTH, (head + 1) * DEPTH)
-        asked = jnp.concatenate((query[own_rows, cols], query[far_rows, cols]), axis=0).T
+        asked = jnp.concatenate((text[own_rows, cols], text[far_rows, cols]), axis=0).T
         scores = inner(key[:, cols], asked) * SCALE
         peak = jnp.max(scores, axis=0, keepdims=True)
         weights = jnp.exp2(scores - peak)
-        held[head : head + 1] = peak
-        held[16 + head : 17 + head] = jnp.sum(weights, axis=0, keepdims=True)
+        stats[head : head + 1] = peak
+        stats[16 + head : 17 + head] = jnp.sum(weights, axis=0, keepdims=True)
         mixed = inner(low(weights).T, value[:, cols])
         own_sums[:, cols] = mixed[:half]
         far_sums[:, cols] = mixed[half:]
-    stats = held[...].T
-    own_stats[...] = stats[:half]
-    far_stats[...] = stats[half:]
+    turned = stats[...].T
+    own_stats[...] = turned[:half]
+    far_stats[...] = turned[half:]
+    for store in stores:
+        store.wait()
 
 
 def text_join_body(sums, stats, far_sums, far_stats, text_key, text_value, *rest):
-    out = rest[-1]
+    parcel, out = rest[-2:]
     half, width = sums.shape
     heads = width // DEPTH
     lane = lax.broadcasted_iota(jnp.int32, stats.shape, 1)
@@ -158,14 +159,24 @@
     for head in range(heads):
         cols = slice(head * DEPTH, (head + 1) * DEPTH)
         first, second = stats[:, head : head + 1], far_stats[:, head : head + 1]
-        top = jnp.maximum(first, second)
+        top = high(low(jnp.maximum(first, second)))
         first, second = jnp.exp2(first - top), jnp.exp2(second - top)
         total = stats[:, 16 + head : 17 + head] * first + far_stats[:, 16 + head : 17 + head] * second
-        out[slot(head)] = sums[:, cols] * first + far_sums[:, cols] * second
-        held = jnp.where(lane == head, top, jnp.where(lane == 16 + head, total, held))
-        out[slot(heads + 1 + head)] = jnp.broadcast_to(high(text_key[:, cols]), (half, DEPTH))
-        out[slot(2 * heads + 1 + head)] = jnp.broadcast_to(high(text_value[:, cols]), (half, DEPTH))
-    out[slot(heads)] = held
+        mixed = sums[:, cols] * first + far_sums[:, cols] * second
+        coarse = high(low(mixed))
+        out[slot(head)] = coarse
+        out[slot(heads + head)] = mixed - coarse
+        big = high(low(total))
+        held = jnp.where(lane == head, top, held)
+        held = jnp.where(lane == 16 + head, big, held)
+        held = jnp.where(lane == 32 + head, total - big, held)
+        out[slot(2 * heads + 1 + head)] = jnp.broadcast_to(high(text_key[:, cols]), (half, DEPTH))
+        out[slot(3 * heads + 1 + head)] = jnp.broadcast_to(high(text_value[:, cols]), (half, DEPTH))
+    out[slot(2 * heads)] = held
+    spare = jnp.zeros((half, DEPTH), jnp.float32)
+    for index in range(4 * heads + 1, SLOTS):
+        out[slot(index)] = spare
+    parcel[...] = low(out[...])
 
 
 def text_masks(count, rows, cols):
@@ -174,17 +185,20 @@
     return place + core < count, place + 1 - core < count
 
 
-def narrow_body(
-    windows, count, query, key, value, queries, got, got_other, finished, out, sums, stats,
-    text_keys, text_values, ids,
+def back_body(
+    windows, count, text, query, key, value, queries, got_low, got_other_low, after,
+    finished, out, sums, stats, text_keys, text_values, ids, got, got_other,
 ):
+    got[...] = high(got_low[...])
+    got_other[...] = high(got_other_low[...])
+    text_merge(text, count, got, got_other, finished)
     heads = windows.shape[1]
     half = got.shape[0] // SLOTS
     for head in range(heads):
         for at, source in enumerate((got, got_other)):
             rows = slice(at * half, (at + 1) * half)
-            text_keys[head, rows] = low(source[slot(heads + 1 + head)])
-            text_values[head, rows] = low(source[slot(2 * heads + 1 + head)])
+            text_keys[head, rows] = low(source[slot(2 * heads + 1 + head)])
+            text_values[head, rows] = low(source[slot(3 * heads + 1 + head)])
     found = jnp.int32(0)
     for head in range(heads):
         wide = (windows[0, head] > 1) | (windows[1, head] > 1) | (windows[2, head] > 1)
@@ -391,7 +405,7 @@
     )
 
 
-def text_merge_body(query, count, got, got_other, after, out):
+def text_merge(query, count, got, got_other, out):
     heads = query.shape[1] // DEPTH
     core = lax.axis_index("co")
     chip = (
@@ -403,12 +417,12 @@
     row = lax.broadcasted_iota(jnp.int32, block.shape, 0)
     asked = jnp.sum(jnp.where(row == at % 16, block, 0.0), axis=0, keepdims=True)
     near, far = text_masks(count[0], sources, 1)
-    stats = got[slot(heads)]
+    stats = got[slot(2 * heads)]
     blocks = []
     for head in range(heads):
         peak = stats[:, head : head + 1]
         mine = asked[:, head * DEPTH : (head + 1) * DEPTH]
-        key_at, value_at = slot(heads + 1 + head), slot(2 * heads + 1 + head)
+        key_at, value_at = slot(2 * heads + 1 + head), slot(3 * heads + 1 + head)
         first = jnp.sum(got[key_at] * mine, axis=1, keepdims=True) * SCALE
         second = jnp.sum(got_other[key_at] * mine, axis=1, keepdims=True) * SCALE
         first = jnp.where(near, first, NEVER)
@@ -418,10 +432,14 @@
         first = jnp.exp2(first - top)
         second = jnp.exp2(second - top)
         whole = jnp.sum(
-            factor * stats[:, 16 + head : 17 + head] + first + second, axis=0, keepdims=True
+            factor * (stats[:, 16 + head : 17 + head] + stats[:, 32 + head : 33 + head])
+            + first
+            + second,
+            axis=0,
+            keepdims=True,
         )
         mixed = jnp.sum(
-            factor * got[slot(head)] + first * got[value_at] + second * got_other[value_at],
+            factor * (got[slot(head)] + got[slot(heads + head)]) + first * got[value_at] + second * got_other[value_at],
             axis=0,
             keepdims=True,
         )
@@ -562,39 +580,42 @@
     branch = lax.axis_index("cfg")
     zones = lax.axis_size("zh")
 
-    pairs, queries = call(
-        pack_body,
-        (shape((2 * WIDE, tokens, DEPTH), bf16), shape((WIDE, DEPTH, tokens), bf16)),
-        [SMEM, HBM, HBM, HBM],
-        (VMEM, VMEM),
-        [pltpu.VMEM((2 * WIDE, tokens, DEPTH), bf16), pltpu.SemaphoreType.DMA((3 * WIDE,))],
-        8, 0, 4 * MIB,
-        windows, query, key, value,
+    part_shape = shape((half_text, width), f32)
+    stat_shape = shape((half_text, DEPTH), f32)
+    pairs, queries, quarter, text_sums, far_sums, text_stats, far_stats = call(
+        front_body,
+        (
+            shape((2 * WIDE, tokens, DEPTH), bf16), shape((WIDE, DEPTH, tokens), bf16),
+            shape((half_width // 2, model), bf16), part_shape, part_shape, stat_shape, stat_shape,
+        ),
+        [SMEM, VMEM] + [HBM] * 4,
+        (VMEM, VMEM, HBM) + (VMEM,) * 4,
+        [
+            pltpu.VMEM((tokens, width), bf16),
+            pltpu.VMEM((tokens, width), bf16),
+            pltpu.VMEM((WIDE, tokens, DEPTH), bf16),
+            pltpu.VMEM((DEPTH, DEPTH), f32),
+            pltpu.VMEM((half_width // 2, model), bf16),
+            pltpu.SemaphoreType.DMA((WIDE + 2,)),
+            pltpu.SemaphoreType.DMA((2, 4)),
+        ],
+        24, 0, 0,
+        windows, text_query, query, key, value, out_weight,
     )
     beside = [(2 * z + 1, 2 * z + 2) for z in range(zones - 1)]
     beside = beside + [(b, a) for a, b in beside]
     next_pairs = lax.ppermute(pairs, ("zh", "co"), beside)
-    from_before = shift(queries, "ta", 1)
-    from_after = shift(queries, "ta", -1)
     pairs_in = swap_core(pairs)
     left = shift(pairs, "ha", 1)
     right = shift(pairs, "ha", -1)
 
-    part_shape = shape((half_text, width), f32)
-    stat_shape = shape((half_text, DEPTH), f32)
-    text_sums, far_sums, text_stats, far_stats = call(
-        text_video_body,
-        (part_shape, part_shape, stat_shape, stat_shape),
-        [VMEM] * 3 + [HBM], (VMEM,) * 4, [pltpu.VMEM((DEPTH, DEPTH), f32)],
-        16, 4 * text_len * tokens * width, 4 * tokens * width,
-        text_query, key, value, pairs,
-    )
     parcel = call(
         text_join_body,
-        shape((SLOTS * half_text, DEPTH), f32),
-        [VMEM] * 6 + [HBM] * 3, VMEM, [], 12, 0, 2 * MIB,
+        shape((SLOTS * half_text, DEPTH), bf16),
+        [VMEM] * 6 + [HBM] * 2, VMEM, [pltpu.VMEM((SLOTS * half_text, DEPTH), f32)],
+        16, 0, 2 * MIB,
         text_sums, text_stats, swap_core(far_sums), swap_core(far_stats), text_key[0], text_value[0],
-        next_pairs, left, right,
+        left, right,
     )
 
     next_left = shift(next_pairs, "ha", 1)
@@ -610,16 +631,10 @@
         weight_pairs.append((at(0, z, 0), at(1, z, 0)))
         weight_pairs.append((at(0, (z + 1) % zones, 1), at(1, z, 1)))
     weight_pairs = weight_pairs + [(b, a) for a, b in weight_pairs]
-    quarter = call(
-        quarter_body,
-        shape((half_width // 2, model), bf16),
-        [HBM] * 2, HBM,
-        [pltpu.VMEM((half_width // 2, model), bf16), pltpu.SemaphoreType.DMA((2, 4))],
-        8, 0, 2 * half_width * model,
-        out_weight, next_pairs,
-    )
-    w_mine = lax.ppermute(quarter, ("cfg", "zh", "co"), weight_pairs)
-    parcel = after(parcel, quarter, pairs_in, left_in, right_in, from_before, from_after)
+    queries = after(queries, parcel)
+    from_before = shift(queries, "ta", 1)
+    from_after = shift(queries, "ta", -1)
+    parcel = after(parcel, next_pairs)
     got = lax.all_to_all(parcel, CHIPS, 0, 0, tiled=True)
     wide_sums = shape((WIDE, DEPTH, tokens), f32)
     wide_stats = shape((WIDE, 8, tokens), f32)
@@ -640,7 +655,7 @@
         (shape((WIDE, DEPTH, 3 * tokens), f32), shape((WIDE, 8, 3 * tokens), f32)),
         [SMEM] + [HBM] * 6 + [VMEM] * 3, (VMEM,) * 2,
         wide_scratch(6),
-        24, 12 * WIDE * 6 * tokens * tokens * DEPTH, 8 * MIB,
+        24, 0, 0,
         windows, pairs, left, right, pairs_in, left_in, right_in, queries, from_before, from_after,
     )
     sums, stats, to_before, to_after = call(
@@ -648,38 +663,38 @@
         (wide_sums, wide_stats, lent, lent),
         [SMEM] + [HBM] * 3 + [VMEM] * 5, (VMEM,) * 4,
         wide_scratch(3),
-        24, 12 * WIDE * 3 * tokens * tokens * DEPTH, 8 * MIB,
+        24, 10**12, 0,
         windows, next_pairs, next_left, next_right, queries, from_before, from_after,
         near_sums, near_stats,
     )
+    w_mine = lax.ppermute(after(quarter, near_stats), ("cfg", "zh", "co"), weight_pairs)
     back_after = shift(to_before, "ta", -1)
     back_before = shift(to_after, "ta", 1)
 
     got = after(got, to_before)
     got_other = swap_core(got)
-    finished = call(
-        text_merge_body,
-        shape((ENDS * half_text, DEPTH), f32),
-        [VMEM, SMEM, VMEM, VMEM, HBM], VMEM, [], 16, 0, 3 * MIB,
-        text_query, text_count, got, got_other, to_before,
-    )
-    finished = after(finished, back_before, back_after)
-    w_mine = after(w_mine, finished)
-    w_other = swap_core(w_mine)
-    narrow, beside_sums, beside_stats = call(
-        narrow_body,
-        (shape((tokens, width), bf16), wide_sums, wide_stats),
-        [SMEM, SMEM] + [VMEM] * 6 + [HBM], (VMEM,) * 3,
+    finished, narrow, beside_sums, beside_stats = call(
+        back_body,
+        (
+            shape((ENDS * half_text, DEPTH), f32), shape((tokens, width), bf16), wide_sums,
+            wide_stats,
+        ),
+        [SMEM, SMEM] + [VMEM] * 7 + [HBM], (VMEM,) * 4,
         [
             pltpu.VMEM((heads, text_len, DEPTH), bf16),
             pltpu.VMEM((heads, text_len, DEPTH), bf16),
             pltpu.SMEM((heads + 1,), jnp.int32),
+            pltpu.VMEM((SLOTS * half_text, DEPTH), f32),
+            pltpu.VMEM((SLOTS * half_text, DEPTH), f32),
         ],
         24, 4 * (heads - WIDE) * tokens * (tokens + text_len) * DEPTH, 5 * tokens * width * 2,
-        windows, text_count, query, key, value, queries, got, got_other, finished,
-    )
-
+        windows, text_count, text_query, query, key, value, queries, got, got_other, to_before,
+    )
+    finished = after(finished, back_before, back_after)
+    w_mine = after(w_mine, finished)
+    w_other = swap_core(w_mine)
     text_mine = lax.all_to_all(finished, CHIPS, 0, 0, tiled=True)
+
     parts = 6
     branch_out = call(
         functools.partial(final_body, parts=parts),
@@ -707,7 +722,7 @@
     grid = branch_out.reshape(frames, rows, cols * final_weight.shape[1])
     kept = lax.dynamic_slice_in_dim(grid, branch * half_rows, half_rows, 1)
     sent = lax.dynamic_slice_in_dim(grid, (1 - branch) * half_rows, half_rows, 1)
-    received = lax.ppermute(sent, "cfg", [(0, 1), (1, 0)])
+    received = after(lax.ppermute(sent, "cfg", [(0, 1), (1, 0)]), text_out)
     conditional = jnp.where(branch == 0, kept, received)
     unconditional = jnp.where(branch == 0, received, kept)
     guided = unconditional + guidance[0] * (conditional - unconditional)

time: 150 us -> 148 us (0.987)
  Pallas kernels: 65.5 us -> 52.7 us
  starting transfers between devices: 57.2 us -> 63.4 us
  waiting for transfers between devices: 22.8 us -> 25.6 us
    ppermute x8, waiting for transfers between devices: 17.7 us -> 4.5 us  [shift(): lax.ppermute(x, axis, [(i, i + step) for i in range(size) if 0 <= i + ste...]
    pallas_call x10 -> x7, Pallas kernels: 65.5 us -> 52.7 us  [call(): pl.pallas_call(body, grid=(1,), out_shape=out_shape, in_specs=in_specs, o...]
    all_to_all x1, waiting for transfers between devices: 0.01 us -> 7.36 us  [local(): text_mine = lax.all_to_all(finished, CHIPS, 0, 0, tiled=True)]
    all_to_all x1, waiting for transfers between devices: 0.01 us -> 5.5 us  [local(): got = lax.all_to_all(parcel, CHIPS, 0, 0, tiled=True)]
    ppermute x8, starting transfers between devices: 3.89 us -> 8.8 us  [swap_core(): return lax.ppermute(x, 'co', [(0, 1), (1, 0)])]
    all_to_all x1, starting transfers between devices: 12.3 us -> 15.3 us  [local(): got = lax.all_to_all(parcel, CHIPS, 0, 0, tiled=True)]
    ppermute x8, starting transfers between devices: 21.6 us -> 18.9 us  [shift(): lax.ppermute(x, axis, [(i, i + step) for i in range(size) if 0 <= i + ste...]
    ppermute x8, waiting for transfers between devices: 1.62 us -> 3.83 us  [swap_core(): return lax.ppermute(x, 'co', [(0, 1), (1, 0)])]
  transfers between devices with their start and end apart: 21 -> 21, of which waited for: 7 -> 6; matrix products, arithmetic and copies ran while one was open for 1% -> 1% of each run, Pallas kernels for 40% -> 31%
where the time goes in v3:
time: 148 us; the launch traced here: 147 us
  starting transfers between devices  63.4 us (43%)
  Pallas kernels  52.7 us (36%)
  waiting for transfers between devices  25.6 us (17%)
  between operations  2.12 us (1%)
  other arithmetic  1.57 us (1%)
  local copies, waits for them, and re-layouts  1.52 us (1%)
    pallas_call x7, Pallas kernels, call(): pl.pallas_call(body, grid=(1,), out_shape=out_shape, in_specs=in_specs, o...  52.7 us
    ppermute x8, starting transfers between devices, shift(): lax.ppermute(x, axis, [(i, i + step) for i in range(size) if 0 <= i + ste...  18.9 us
    all_to_all x1, starting transfers between devices, local(): got = lax.all_to_all(parcel, CHIPS, 0, 0, tiled=True)  15.3 us
    all_to_all x1, starting transfers between devices, local(): text_mine = lax.all_to_all(finished, CHIPS, 0, 0, tiled=True)  11 us
    ppermute x8, starting transfers between devices, swap_core(): return lax.ppermute(x, 'co', [(0, 1), (1, 0)])  8.8 us
    all_to_all x1, waiting for transfers between devices, local(): text_mine = lax.all_to_all(finished, CHIPS, 0, 0, tiled=True)  7.36 us
    ppermute x1, starting transfers between devices, local(): next_pairs = lax.ppermute(pairs, ('zh', 'co'), beside)  5.74 us
    all_to_all x1, waiting for transfers between devices, local(): got = lax.all_to_all(parcel, CHIPS, 0, 0, tiled=True)  5.5 us
  transfers between devices with their start and end apart: 21, of which 6 were waited for; matrix products, arithmetic and copies ran while one was open for 1% of the time, Pallas kernels for 31%

profile of v3, /device:TPU:1, one launch (start us, length us, event | category | flops | bytes accessed | tf_op | source)
XLA Modules:
  0.0 146.9 jit_solution(14377904492443223493)
XLA Ops:
  0.6 7.6 %shard_map.140 = (bf16[6,384,128]{2,1,0:T(8,128)(2,1)}, bf16[3,128,384]{2,1,0:T(8,128)(2,1)}, bf16[384,3072]{1,0:T(8,128)(2,1)}, f32[64,1536]{1,0:T(8,128)}, f32...) custom-call(s32[3,12]{1,0:T(4,128)} %bitcast.33, bf16[128,1536]{1,0:T(8,128)(2,1)} %bitcast.26, ...), custom_call_target="tpu_custom_call" | custom-call | tf_op jit(solution)/shard_map/pallas_call | solution.py:28
  8.2 4.8 %collective-permute-start.5 = (bf16[6,384,128]{2,1,0:T(8,128)(2,1)}, bf16[6,384,128]{2,1,0:T(8,128)(2,1)}, u32[]{:S(2)}, u32[]{:S(2)}) collective-permute-start(bf16[6,384,128]{2,1,0:T(8,128)(2,1)} %get-tuple-element.19.own), channel_id=1, source_target_pairs={{0,8},{8,16},{16,24},{1,9},{9,17},{17,25},{2,10},{10,18},{18,26},{... | collective-permute-start | bytes 1769480 | tf_op jit(solution)/shard_map/ppermute | solution.py:554
  14.2 5.7 %collective-permute-start = (bf16[6,384,128]{2,1,0:T(8,128)(2,1)}, bf16[6,384,128]{2,1,0:T(8,128)(2,1)}, u32[]{:S(2)}, u32[]{:S(2)}) collective-permute-start(bf16[6,384,128]{2,1,0:T(8,128)(2,1)} %get-tuple-element.19.own), channel_id=1, source_target_pairs={{1,2},{3,4},{5,6},{2,1},{4,3},{6,5},{9,10},{11,12},{13,14},{10,9},... | collective-permute-start | bytes 1769480 | tf_op jit(solution)/shard_map/ppermute | solution.py:607
  20.6 1.9 %collective-permute-done.4.far_stats = f32[64,128]{1,0:T(8,128)} collective-permute-done((f32[64,128]{1,0:T(8,128)}, f32[64,128]{1,0:T(8,128)}, u32[]{:S(2)}, u32[]{:S(2)}) %collective-permute-start.4) | collective-permute-done | bytes 32800 | tf_op jit(solution)/shard_map/ppermute | solution.py:558
  22.6 1.9 %collective-permute-done.3.far_sums = f32[64,1536]{1,0:T(8,128)} collective-permute-done((f32[64,1536]{1,0:T(8,128)}, f32[64,1536]{1,0:T(8,128)}, u32[]{:S(2)}, u32[]{:S(2)}) %collective-permute-start.3) | collective-permute-done | bytes 393248 | tf_op jit(solution)/shard_map/ppermute | solution.py:558
  24.5 4.5 %collective-permute-done.6.rest_1_.right = bf16[6,384,128]{2,1,0:T(8,128)(2,1)} collective-permute-done((bf16[6,384,128]{2,1,0:T(8,128)(2,1)}, bf16[6,384,128]{2,1,0:T(8,128)(2,1)}, u32[]{:S(2)}, u32[]{:S(2)}) %collective-permute-start.6) | collective-permute-done | bytes 589856 | tf_op jit(solution)/shard_map/ppermute | solution.py:554
  29.0 3.6 %shard_map.141.refs_1_.refs_0_ = bf16[3584,128]{1,0:T(8,128)(2,1)} custom-call(f32[64,1536]{1,0:T(8,128)} %get-tuple-element.21.sums, f32[64,128]{1,0:T(8,128)} %get-tuple-element.22.stats, f32[64,1536]{1,0:T(8,128)} %collective-permute-done.3.far_sums, f32[64,128]{1,0:T(8,128)} %collective-permute-done.4.far_stats, bf16[1,1536]{1,0:T(2,128)(2,1)} %bitcast.38, ...), custom_call_target="tpu_custom_call" | custom-call | bytes 2097152 | tf_op jit(solution)/shard_map/pallas_call | solution.py:28
  32.6 3.9 %collective-permute-start.7 = (bf16[3,128,384]{2,1,0:T(8,128)(2,1)}, bf16[3,128,384]{2,1,0:T(8,128)(2,1)}, u32[]{:S(2)}, u32[]{:S(2)}) collective-permute-start(bf16[3,128,384]{2,1,0:T(8,128)(2,1)} %shard_map.142.queries), channel_id=1, source_target_pairs={{0,32},{32,64},{64,96},{1,33},{33,65},{65,97},{2,34},{34,66},{66,9... | collective-permute-start | bytes 884744 | tf_op jit(solution)/shard_map/ppermute | solution.py:554
  36.5 2.2 %collective-permute-start.10 = (bf16[6,384,128]{2,1,0:T(8,128)(2,1)}, bf16[6,384,128]{2,1,0:T(8,128)(2,1)}, u32[]{:S(2)}, u32[]{:S(2)}) collective-permute-start(bf16[6,384,128]{2,1,0:T(8,128)(2,1)} %collective-permute-done.5.rest_0_.left), channel_id=1, source_target_pairs={{0,1},{1,0},{2,3},{3,2},{4,5},{5,4},{6,7},{7,6},{8,9},{9,8},{10,11... | collective-permute-start | bytes 1769480 | tf_op jit(solution)/shard_map/ppermute | solution.py:558
  38.7 3.1 %collective-permute-start.1 = (bf16[6,384,128]{2,1,0:T(8,128)(2,1)}, bf16[6,384,128]{2,1,0:T(8,128)(2,1)}, u32[]{:S(2)}, u32[]{:S(2)}) collective-permute-start(bf16[6,384,128]{2,1,0:T(8,128)(2,1)} %collective-permute-done.own.refs_1_), channel_id=1, source_target_pairs={{0,8},{8,16},{16,24},{1,9},{9,17},{17,25},{2,10},{10,18},{18,26},{... | collective-permute-start | bytes 1769480 | tf_op jit(solution)/shard_map/ppermute | solution.py:554
  44.4 15.3 %all-to-all-start = ((bf16[64,56,128]{2,1,0:T(8,128)(2,1)}), bf16[64,56,128]{2,1,0:T(8,128)(2,1)}, u32[]{:S(2)}, u32[]{:S(2)}) async-start(bf16[64,56,128]{2,1,0:T(8,128)(2,1)} %bitcast.18), calls=%async_computation | async-start | bytes 1835008 | tf_op jit(solution)/shard_map/all_to_all | solution.py:638
  59.7 10.3 %shard_map.143 = (f32[3,128,1152]{2,1,0:T(8,128)}, f32[3,8,1152]{2,1,0:T(8,128)}) custom-call(s32[3,12]{1,0:T(4,128)} %bitcast.34, bf16[6,384,128]{2,1,0:T(8,128)(2,1)} %get-tuple-element.19.own, bf16[6,384,128]{2,1,0:T(8,128)(2,1)} %collective-permute-done.5.rest_0_.left, bf16[6,384,128]{2,1,0:T(8,128)(2,1)} %collective-permute-done.6.rest_1_.right, ...), custom_call_target="tpu_custom_call" | custom-call | tf_op jit(solution)/shard_map/pallas_call | solution.py:28
  70.0 2.7 %collective-permute-start.15 = (bf16[384,3072]{1,0:T(8,128)(2,1)}, bf16[384,3072]{1,0:T(8,128)(2,1)}, u32[]{:S(2)}, u32[]{:S(2)}) collective-permute-start(bf16[384,3072]{1,0:T(8,128)(2,1)} %shard_map.148), channel_id=1, source_target_pairs={{0,128},{3,129},{2,130},{5,131},{4,132},{7,133},{6,134},{1,135},{1... | collective-permute-start | bytes 7077896 | tf_op jit(solution)/shard_map/ppermute | solution.py:670
  72.8 6.8 %shard_map.144 = (f32[3,128,384]{2,1,0:T(8,128)}, f32[3,8,384]{2,1,0:T(8,128)}, bf16[3,144,384]{2,1,0:T(8,128)(2,1)}, bf16[3,144,384]{2,1,0:T(8,128)(2,1)}) custom-call(s32[3,12]{1,0:T(4,128)} %bitcast.35, bf16[6,384,128]{2,1,0:T(8,128)(2,1)} %collective-permute-done.own.refs_1_, bf16[6,384,128]{2,1,0:T(8,128)(2,1)} %collective-permute-done.1.left, ...), custom_call_target="tpu_custom_call" | custom-call | flops 999999995904 | tf_op jit(solution)/shard_map/pallas_call | solution.py:28
  79.6 5.5 %all-to-all-done = bf16[64,56,128]{2,1,0:T(8,128)(2,1)} async-done(((bf16[64,56,128]{2,1,0:T(8,128)(2,1)}), bf16[64,56,128]{2,1,0:T(8,128)(2,1)}, u32[]{:S(2)}, u32[]{:S(2)}) %all-to-all-start) | async-done | bytes 917536 | tf_op jit(solution)/shard_map/all_to_all | solution.py:638
  85.1 3.7 %collective-permute-start.12 = (bf16[3584,128]{1,0:T(8,128)(2,1)}, bf16[3584,128]{1,0:T(8,128)(2,1)}, u32[]{:S(2)}, u32[]{:S(2)}) collective-permute-start(bf16[3584,128]{1,0:T(8,128)(2,1)} %shard_map.146.got_low), channel_id=1, source_target_pairs={{0,1},{1,0},{2,3},{3,2},{4,5},{5,4},{6,7},{7,6},{8,9},{9,8},{10,11... | collective-permute-start | bytes 2752520 | tf_op jit(solution)/shard_map/ppermute | solution.py:558
  88.8 2.0 %collective-permute-start.13 = (bf16[3,144,384]{2,1,0:T(8,128)(2,1)}, bf16[3,144,384]{2,1,0:T(8,128)(2,1)}, u32[]{:S(2)}, u32[]{:S(2)}) collective-permute-start(bf16[3,144,384]{2,1,0:T(8,128)(2,1)} %get-tuple-element.32), channel_id=1, source_target_pairs={{0,32},{32,64},{64,96},{1,33},{33,65},{65,97},{2,34},{34,66},{66,9... | collective-permute-start | bytes 995336 | tf_op jit(solution)/shard_map/ppermute | solution.py:554
  92.8 10.5 %shard_map.147 = (f32[1024,128]{1,0:T(8,128)}, bf16[384,1536]{1,0:T(8,128)(2,1)}, f32[3,128,384]{2,1,0:T(8,128)}, f32[3,8,384]{2,1,0:T(8,128)}) custom-call(s32[3,12]{1,0:T(4,128)} %bitcast.36, s32[1]{0:T(128)S(6)} %copy.31.count, bf16[128,1536]{1,0:T(8,128)(2,1)} %bitcast.27, bf16[384,1536]{1,0:T(8,128)(2,1)} %bitcast.20, bf16[384,1536]{1,0:T(8,128)(2,1)} %bitcast.22, ...), custom_call_target="tpu_custom_call" | custom-call | flops 905969664 | bytes 5898240 | tf_op jit(solution)/shard_map/pallas_call | solution.py:28
  103.3 4.4 %collective-permute-done.15.refs_0_ = bf16[384,3072]{1,0:T(8,128)(2,1)} collective-permute-done((bf16[384,3072]{1,0:T(8,128)(2,1)}, bf16[384,3072]{1,0:T(8,128)(2,1)}, u32[]{:S(2)}, u32[]{:S(2)}) %collective-permute-start.15) | collective-permute-done | bytes 2359328 | tf_op jit(solution)/shard_map/ppermute | solution.py:670
  107.8 11.0 %all-to-all-start.1 = ((f32[64,16,128]{2,1,0:T(8,128)}), f32[64,16,128]{2,1,0:T(8,128)}, u32[]{:S(2)}, u32[]{:S(2)}) async-start(f32[64,16,128]{2,1,0:T(8,128)} %bitcast.13), calls=%async_computation.1 | async-start | bytes 1048576 | tf_op jit(solution)/shard_map/all_to_all | solution.py:696
  118.8 11.7 %shard_map.151.refs_1_ = f32[48,512]{1,0:T(8,128)} custom-call(s32[3,12]{1,0:T(4,128)} %bitcast.37, f32[3,128,384]{2,1,0:T(8,128)} %get-tuple-element.27.sums, f32[3,8,384]{2,1,0:T(8,128)} %get-tuple-element.28.stats, f32[3,128,384]{2,1,0:T(8,128)} %get-tuple-element.30.text_sums, f32[3,8,384]{2,1,0:T(8,128)} %get-tuple-element.31.text_stats, ...), custom_call_target="tpu_custom_call" | custom-call | flops 3623878656 | bytes 16777216 | tf_op jit(solution)/shard_map/pallas_call | solution.py:28
  130.5 7.4 %all-to-all-done.1 = f32[64,16,128]{2,1,0:T(8,128)} async-done(((f32[64,16,128]{2,1,0:T(8,128)}), f32[64,16,128]{2,1,0:T(8,128)}, u32[]{:S(2)}, u32[]{:S(2)}) %all-to-all-start.1) | async-done | bytes 524320 | tf_op jit(solution)/shard_map/all_to_all | solution.py:696
  137.9 2.2 %collective-permute-start.18 = (f32[1024,128]{1,0:T(8,128)}, f32[1024,128]{1,0:T(8,128)}, u32[]{:S(2)}, u32[]{:S(2)}) collective-permute-start(f32[1024,128]{1,0:T(8,128)} %shard_map.152.mine), channel_id=1, source_target_pairs={{0,1},{1,0},{2,3},{3,2},{4,5},{5,4},{6,7},{7,6},{8,9},{9,8},{10,11... | collective-permute-start | bytes 1572872 | tf_op jit(solution)/shard_map/ppermute | solution.py:558
  143.1 2.2 %shard_map.153.refs_1_ = bf16[128,1536]{1,0:T(8,128)(2,1)} custom-call(f32[1024,128]{1,0:T(8,128)} %shard_map.152.mine, f32[1024,128]{1,0:T(8,128)} %collective-permute-done.18.other), custom_call_target="tpu_custom_call" | custom-call | bytes 1048576 | tf_op jit(solution)/shard_map/pallas_call | solution.py:28
  (35 shorter events, 9.8 us)
Async XLA Ops:
  8.2 16.4 %collective-permute-start.5 = (bf16[6,384,128]{2,1,0:T(8,128)(2,1)}, bf16[6,384,128]{2,1,0:T(8,128)(2,1)}, u32[]{:S(2)}, u32[]{:S(2)}) collective-permute-start(bf16[6,384,128]{2,1,0:T(8,128)(2,1)} %get-tuple-element.19.own), channel_id=1, source_target_pairs={{0,8},{8,16},{16,24},{1,9},{9,17},{17,25},{2,10},{10,18},{18,26},{... | collective-permute-start | bytes 1769480 | tf_op jit(solution)/shard_map/ppermute | solution.py:554
  13.0 16.1 %collective-permute-start.6 = (bf16[6,384,128]{2,1,0:T(8,128)(2,1)}, bf16[6,384,128]{2,1,0:T(8,128)(2,1)}, u32[]{:S(2)}, u32[]{:S(2)}) collective-permute-start(bf16[6,384,128]{2,1,0:T(8,128)(2,1)} %get-tuple-element.19.own), channel_id=1, source_target_pairs={{8,0},{16,8},{24,16},{9,1},{17,9},{25,17},{10,2},{18,10},{26,18},{... | collective-permute-start | bytes 1769480 | tf_op jit(solution)/shard_map/ppermute | solution.py:554
  14.2 24.4 %collective-permute-start = (bf16[6,384,128]{2,1,0:T(8,128)(2,1)}, bf16[6,384,128]{2,1,0:T(8,128)(2,1)}, u32[]{:S(2)}, u32[]{:S(2)}) collective-permute-start(bf16[6,384,128]{2,1,0:T(8,128)(2,1)} %get-tuple-element.19.own), channel_id=1, source_target_pairs={{1,2},{3,4},{5,6},{2,1},{4,3},{6,5},{9,10},{11,12},{13,14},{10,9},... | collective-permute-start | bytes 1769480 | tf_op jit(solution)/shard_map/ppermute | solution.py:607
  20.0 21.8 %collective-permute-start.9 = (bf16[6,384,128]{2,1,0:T(8,128)(2,1)}, bf16[6,384,128]{2,1,0:T(8,128)(2,1)}, u32[]{:S(2)}, u32[]{:S(2)}) collective-permute-start(bf16[6,384,128]{2,1,0:T(8,128)(2,1)} %get-tuple-element.19.own), channel_id=1, source_target_pairs={{0,1},{1,0},{2,3},{3,2},{4,5},{5,4},{6,7},{7,6},{8,9},{9,8},{10,11... | collective-permute-start | bytes 1769480 | tf_op jit(solution)/shard_map/ppermute | solution.py:558
  20.1 2.4 %collective-permute-start.4 = (f32[64,128]{1,0:T(8,128)}, f32[64,128]{1,0:T(8,128)}, u32[]{:S(2)}, u32[]{:S(2)}) collective-permute-start(f32[64,128]{1,0:T(8,128)} %get-tuple-element.24), channel_id=1, source_target_pairs={{0,1},{1,0},{2,3},{3,2},{4,5},{5,4},{6,7},{7,6},{8,9},{9,8},{10,11... | collective-permute-start | bytes 98312 | tf_op jit(solution)/shard_map/ppermute | solution.py:558
  22.5 2.1 %collective-permute-start.3 = (f32[64,1536]{1,0:T(8,128)}, f32[64,1536]{1,0:T(8,128)}, u32[]{:S(2)}, u32[]{:S(2)}) collective-permute-start(f32[64,1536]{1,0:T(8,128)} %get-tuple-element.23), channel_id=1, source_target_pairs={{0,1},{1,0},{2,3},{3,2},{4,5},{5,4},{6,7},{7,6},{8,9},{9,8},{10,11... | collective-permute-start | bytes 1179656 | tf_op jit(solution)/shard_map/ppermute | solution.py:558
  32.6 10.5 %collective-permute-start.7 = (bf16[3,128,384]{2,1,0:T(8,128)(2,1)}, bf16[3,128,384]{2,1,0:T(8,128)(2,1)}, u32[]{:S(2)}, u32[]{:S(2)}) collective-permute-start(bf16[3,128,384]{2,1,0:T(8,128)(2,1)} %shard_map.142.queries), channel_id=1, source_target_pairs={{0,32},{32,64},{64,96},{1,33},{33,65},{65,97},{2,34},{34,66},{66,9... | collective-permute-start | bytes 884744 | tf_op jit(solution)/shard_map/ppermute | solution.py:554
  36.5 23.2 %collective-permute-start.10 = (bf16[6,384,128]{2,1,0:T(8,128)(2,1)}, bf16[6,384,128]{2,1,0:T(8,128)(2,1)}, u32[]{:S(2)}, u32[]{:S(2)}) collective-permute-start(bf16[6,384,128]{2,1,0:T(8,128)(2,1)} %collective-permute-done.5.rest_0_.left), channel_id=1, source_target_pairs={{0,1},{1,0},{2,3},{3,2},{4,5},{5,4},{6,7},{7,6},{8,9},{9,8},{10,11... | collective-permute-start | bytes 1769480 | tf_op jit(solution)/shard_map/ppermute | solution.py:558
  38.7 21.1 %collective-permute-start.11 = (bf16[6,384,128]{2,1,0:T(8,128)(2,1)}, bf16[6,384,128]{2,1,0:T(8,128)(2,1)}, u32[]{:S(2)}, u32[]{:S(2)}) collective-permute-start(bf16[6,384,128]{2,1,0:T(8,128)(2,1)} %collective-permute-done.6.rest_1_.right), channel_id=1, source_target_pairs={{0,1},{1,0},{2,3},{3,2},{4,5},{5,4},{6,7},{7,6},{8,9},{9,8},{10,11... | collective-permute-start | bytes 1769480 | tf_op jit(solution)/shard_map/ppermute | solution.py:558
  38.7 34.1 %collective-permute-start.1 = (bf16[6,384,128]{2,1,0:T(8,128)(2,1)}, bf16[6,384,128]{2,1,0:T(8,128)(2,1)}, u32[]{:S(2)}, u32[]{:S(2)}) collective-permute-start(bf16[6,384,128]{2,1,0:T(8,128)(2,1)} %collective-permute-done.own.refs_1_), channel_id=1, source_target_pairs={{0,8},{8,16},{16,24},{1,9},{9,17},{17,25},{2,10},{10,18},{18,26},{... | collective-permute-start | bytes 1769480 | tf_op jit(solution)/shard_map/ppermute | solution.py:554
  41.8 31.0 %collective-permute-start.2 = (bf16[6,384,128]{2,1,0:T(8,128)(2,1)}, bf16[6,384,128]{2,1,0:T(8,128)(2,1)}, u32[]{:S(2)}, u32[]{:S(2)}) collective-permute-start(bf16[6,384,128]{2,1,0:T(8,128)(2,1)} %collective-permute-done.own.refs_1_), channel_id=1, source_target_pairs={{8,0},{16,8},{24,16},{9,1},{17,9},{25,17},{10,2},{18,10},{26,18},{... | collective-permute-start | bytes 1769480 | tf_op jit(solution)/shard_map/ppermute | solution.py:554
  43.1 16.6 %collective-permute-start.8 = (bf16[3,128,384]{2,1,0:T(8,128)(2,1)}, bf16[3,128,384]{2,1,0:T(8,128)(2,1)}, u32[]{:S(2)}, u32[]{:S(2)}) collective-permute-start(bf16[3,128,384]{2,1,0:T(8,128)(2,1)} %shard_map.142.queries), channel_id=1, source_target_pairs={{32,0},{64,32},{96,64},{33,1},{65,33},{97,65},{34,2},{66,34},{98,6... | collective-permute-start | bytes 884744 | tf_op jit(solution)/shard_map/ppermute | solution.py:554
  44.4 40.7 %all-to-all-start = ((bf16[64,56,128]{2,1,0:T(8,128)(2,1)}), bf16[64,56,128]{2,1,0:T(8,128)(2,1)}, u32[]{:S(2)}, u32[]{:S(2)}) async-start(bf16[64,56,128]{2,1,0:T(8,128)(2,1)} %bitcast.18), calls=%async_computation | async-start | bytes 1835008 | tf_op jit(solution)/shard_map/all_to_all | solution.py:638
  70.0 37.8 %collective-permute-start.15 = (bf16[384,3072]{1,0:T(8,128)(2,1)}, bf16[384,3072]{1,0:T(8,128)(2,1)}, u32[]{:S(2)}, u32[]{:S(2)}) collective-permute-start(bf16[384,3072]{1,0:T(8,128)(2,1)} %shard_map.148), channel_id=1, source_target_pairs={{0,128},{3,129},{2,130},{5,131},{4,132},{7,133},{6,134},{1,135},{1... | collective-permute-start | bytes 7077896 | tf_op jit(solution)/shard_map/ppermute | solution.py:670
  85.1 7.7 %collective-permute-start.12 = (bf16[3584,128]{1,0:T(8,128)(2,1)}, bf16[3584,128]{1,0:T(8,128)(2,1)}, u32[]{:S(2)}, u32[]{:S(2)}) collective-permute-start(bf16[3584,128]{1,0:T(8,128)(2,1)} %shard_map.146.got_low), channel_id=1, source_target_pairs={{0,1},{1,0},{2,3},{3,2},{4,5},{5,4},{6,7},{7,6},{8,9},{9,8},{10,11... | collective-permute-start | bytes 2752520 | tf_op jit(solution)/shard_map/ppermute | solution.py:558
  88.8 14.5 %collective-permute-start.13 = (bf16[3,144,384]{2,1,0:T(8,128)(2,1)}, bf16[3,144,384]{2,1,0:T(8,128)(2,1)}, u32[]{:S(2)}, u32[]{:S(2)}) collective-permute-start(bf16[3,144,384]{2,1,0:T(8,128)(2,1)} %get-tuple-element.32), channel_id=1, source_target_pairs={{0,32},{32,64},{64,96},{1,33},{33,65},{65,97},{2,34},{34,66},{66,9... | collective-permute-start | bytes 995336 | tf_op jit(solution)/shard_map/ppermute | solution.py:554
  90.8 12.5 %collective-permute-start.14 = (bf16[3,144,384]{2,1,0:T(8,128)(2,1)}, bf16[3,144,384]{2,1,0:T(8,128)(2,1)}, u32[]{:S(2)}, u32[]{:S(2)}) collective-permute-start(bf16[3,144,384]{2,1,0:T(8,128)(2,1)} %get-tuple-element.29.refs_1_.after), channel_id=1, source_target_pairs={{32,0},{64,32},{96,64},{33,1},{65,33},{97,65},{34,2},{66,34},{98,6... | collective-permute-start | bytes 995336 | tf_op jit(solution)/shard_map/ppermute | solution.py:554
  107.8 11.0 %collective-permute-start.16 = (bf16[384,3072]{1,0:T(8,128)(2,1)}, bf16[384,3072]{1,0:T(8,128)(2,1)}, u32[]{:S(2)}, u32[]{:S(2)}) collective-permute-start(bf16[384,3072]{1,0:T(8,128)(2,1)} %shard_map.150.w_mine), channel_id=1, source_target_pairs={{0,1},{1,0},{2,3},{3,2},{4,5},{5,4},{6,7},{7,6},{8,9},{9,8},{10,11... | collective-permute-start | bytes 7077896 | tf_op jit(solution)/shard_map/ppermute | solution.py:558
  107.8 30.1 %all-to-all-start.1 = ((f32[64,16,128]{2,1,0:T(8,128)}), f32[64,16,128]{2,1,0:T(8,128)}, u32[]{:S(2)}, u32[]{:S(2)}) async-start(f32[64,16,128]{2,1,0:T(8,128)} %bitcast.13), calls=%async_computation.1 | async-start | bytes 1048576 | tf_op jit(solution)/shard_map/all_to_all | solution.py:696
  137.9 5.2 %collective-permute-start.18 = (f32[1024,128]{1,0:T(8,128)}, f32[1024,128]{1,0:T(8,128)}, u32[]{:S(2)}, u32[]{:S(2)}) collective-permute-start(f32[1024,128]{1,0:T(8,128)} %shard_map.152.mine), channel_id=1, source_target_pairs={{0,1},{1,0},{2,3},{3,2},{4,5},{5,4},{6,7},{7,6},{8,9},{9,8},{10,11... | collective-permute-start | bytes 1572872 | tf_op jit(solution)/shard_map/ppermute | solution.py:558
  141.6 3.7 %collective-permute-start.17 = (f32[6,4,512]{2,1,0:T(4,128)}, f32[6,4,512]{2,1,0:T(4,128)}, u32[]{:S(2)}, u32[]{:S(2)}) collective-permute-start(f32[6,4,512]{2,1,0:T(4,128)} %constant_dynamic-slice_fusion), channel_id=1, source_target_pairs={{0,128},{128,0},{1,129},{129,1},{2,130},{130,2},{3,131},{131,3},{4... | collective-permute-start | bytes 147464 | tf_op jit(solution)/shard_map/ppermute | solution.py:725

commit v4 on v3

--- a/solution.py
+++ b/solution.py
@@ -445,25 +445,27 @@
         )
         blocks.append(mixed / whole)
     blocks.append(jnp.zeros((ENDS - heads, DEPTH), jnp.float32))
-    chunk = jnp.concatenate(blocks, axis=0)
+    chunk = low(jnp.concatenate(blocks, axis=0))
     for source in range(sources):
         out[source * ENDS : (source + 1) * ENDS] = chunk
 
 
-def text_out_body(mine, other, out):
+def text_out_body(mine, other, out, held):
     half = mine.shape[0] // ENDS
+    held[0] = high(mine[...])
+    held[1] = high(other[...])
     heads = out.shape[1] // DEPTH
     core = lax.axis_index("co")
-    for source, place in ((mine, core), (other, 1 - core)):
+    for source, place in ((0, core), (1, 1 - core)):
         rows = pl.ds(pl.multiple_of(place * half, half), half)
         for head in range(heads):
-            picked = source[pl.ds(head, half, stride=ENDS), :]
+            picked = held[source, pl.ds(head, half, stride=ENDS), :]
             out[rows, head * DEPTH : (head + 1) * DEPTH] = low(picked)
 
 
 def final_body(
     windows, sums, stats, text_sums, text_stats, back0, back1, narrow, w_own, w_mine, w_other,
-    hidden, modulation, final, out, attended, weight, updated, residual,
+    hidden, modulation, final, kept, sent, attended, weight, updated, residual,
     spread, sems, *, parts,
 ):
     ids = wide_heads(windows)
@@ -542,11 +544,15 @@
         normed = normed + modulation[1, :, cols]
         result = result + outer(low(normed), final[:, cols])
     spread[:, :channels] = result
-    columns = out.shape[1] // channels
-    for column in range(columns):
-        out[:, column * channels : (column + 1) * channels] = spread[
-            pl.ds(column, tokens // columns, stride=columns), :
-        ][:, :channels]
+    frames, half_rows = kept.shape[:2]
+    columns = kept.shape[2] // channels
+    for out, place in ((kept, branch), (sent, 1 - branch)):
+        for frame in range(frames):
+            for column in range(columns):
+                first = ((frame * 2 + place) * half_rows) * columns + column
+                out[frame, :, column * channels : (column + 1) * channels] = spread[
+                    pl.ds(first, half_rows, stride=columns), :
+                ][:, :channels]
 
 
 def shift(x, axis, step):
@@ -579,6 +585,7 @@
     core = lax.axis_index("co")
     branch = lax.axis_index("cfg")
     zones = lax.axis_size("zh")
+    branches = lax.axis_size("cfg")
 
     part_shape = shape((half_text, width), f32)
     stat_shape = shape((half_text, DEPTH), f32)
@@ -676,7 +683,7 @@
     finished, narrow, beside_sums, beside_stats = call(
         back_body,
         (
-            shape((ENDS * half_text, DEPTH), f32), shape((tokens, width), bf16), wide_sums,
+            shape((ENDS * half_text, DEPTH), bf16), shape((tokens, width), bf16), wide_sums,
             wide_stats,
         ),
         [SMEM, SMEM] + [VMEM] * 7 + [HBM], (VMEM,) * 4,
@@ -696,10 +703,12 @@
     text_mine = lax.all_to_all(finished, CHIPS, 0, 0, tiled=True)
 
     parts = 6
-    branch_out = call(
+    half_rows = rows // branches
+    half_out = shape((frames, half_rows, cols * final_weight.shape[1]), f32)
+    kept, sent = call(
         functools.partial(final_body, parts=parts),
-        shape((frames * rows, cols * final_weight.shape[1]), f32),
-        [SMEM] + [VMEM] * 6 + [HBM] * 5 + [VMEM] * 2, VMEM,
+        (half_out, half_out),
+        [SMEM] + [VMEM] * 6 + [HBM] * 5 + [VMEM] * 2, (VMEM, VMEM),
         [
             pltpu.VMEM((tokens, width), bf16),
             pltpu.VMEM((width, model), bf16),
@@ -713,15 +722,12 @@
         out_weight, w_mine, w_other,
         hidden_state.reshape(tokens, model), modulation.transpose(1, 0, 2), final_weight.T,
     )
-    text_mine = after(text_mine, branch_out)
+    text_mine = after(text_mine, kept)
     text_out = call(
-        text_out_body, shape((text_len, width), bf16), [VMEM, VMEM], VMEM, [], 8, 0, MIB,
+        text_out_body, shape((text_len, width), bf16), [VMEM, VMEM], VMEM,
+        [pltpu.VMEM((2, ENDS * half_text, DEPTH), f32)], 8, 0, MIB,
         text_mine, swap_core(text_mine),
     )
-    half_rows = rows // 2
-    grid = branch_out.reshape(frames, rows, cols * final_weight.shape[1])
-    kept = lax.dynamic_slice_in_dim(grid, branch * half_rows, half_rows, 1)
-    sent = lax.dynamic_slice_in_dim(grid, (1 - branch) * half_rows, half_rows, 1)
     received = after(lax.ppermute(sent, "cfg", [(0, 1), (1, 0)]), text_out)
     conditional = jnp.where(branch == 0, kept, received)
     unconditional = jnp.where(branch == 0, received, kept)

time: 148 us -> 141 us (0.953)
  waiting for transfers between devices: 25.6 us -> 14.8 us
  Pallas kernels: 52.7 us -> 57.8 us
  local copies, waits for them, and re-layouts: 1.52 us -> 0 us
    all_to_all x1, waiting for transfers between devices: 7.36 us -> 2.1 us  [local(): text_mine = lax.all_to_all(finished, CHIPS, 0, 0, tiled=True)]
    all_to_all x1, waiting for transfers between devices: 5.5 us -> 0.29 us  [local(): got = lax.all_to_all(parcel, CHIPS, 0, 0, tiled=True)]
    pallas_call x7, Pallas kernels: 52.7 us -> 57.8 us  [call(): pl.pallas_call(body, grid=(1,), out_shape=out_shape, in_specs=in_specs, o...]
    dynamic_slice x1 -> x0, local copies, waits for them, and re-layouts: 1.52 us -> none  [local(): lax.dynamic_slice_in_dim(grid, (1 - branch) * half_rows, half_rows, 1)]
  transfers between devices with their start and end apart: 21 -> 21, of which waited for: 6 -> 7; matrix products, arithmetic and copies ran while one was open for 1% -> 0% of each run, Pallas kernels for 31% -> 36%
where the time goes in v4:
time: 141 us
  starting transfers between devices  64.4 us (46%)
  Pallas kernels  57.8 us (41%)
  waiting for transfers between devices  14.8 us (10%)
  between operations  2.12 us (2%)
  other arithmetic  1.45 us (1%)
    pallas_call x7, Pallas kernels, call(): pl.pallas_call(body, grid=(1,), out_shape=out_shape, in_specs=in_specs, o...  57.8 us
    ppermute x8, starting transfers between devices, shift(): lax.ppermute(x, axis, [(i, i + step) for i in range(size) if 0 <= i + ste...  18.9 us
    all_to_all x1, starting transfers between devices, local(): got = lax.all_to_all(parcel, CHIPS, 0, 0, tiled=True)  15.3 us
    all_to_all x1, starting transfers between devices, local(): text_mine = lax.all_to_all(finished, CHIPS, 0, 0, tiled=True)  11.8 us
    ppermute x8, starting transfers between devices, swap_core(): return lax.ppermute(x, 'co', [(0, 1), (1, 0)])  9.11 us
    ppermute x1, starting transfers between devices, local(): next_pairs = lax.ppermute(pairs, ('zh', 'co'), beside)  5.74 us
    ppermute x8, waiting for transfers between devices, shift(): lax.ppermute(x, axis, [(i, i + step) for i in range(size) if 0 <= i + ste...  4.5 us
    ppermute x1, waiting for transfers between devices, local(): lax.ppermute(after(quarter, near_stats), ('cfg', 'zh', 'co'), weight_pairs)  3.92 us
  transfers between devices with their start and end apart: 21, of which 7 were waited for; matrix products, arithmetic and copies ran while one was open for 0% of the time, Pallas kernels for 36%

profile of v4, /device:TPU:1, one launch (start us, length us, event | category | flops | bytes accessed | tf_op | source)
XLA Modules:
  0.0 140.6 jit_solution(8584139446731426197)
XLA Ops:
  0.6 7.6 %shard_map.140 = (bf16[6,384,128]{2,1,0:T(8,128)(2,1)}, bf16[3,128,384]{2,1,0:T(8,128)(2,1)}, bf16[384,3072]{1,0:T(8,128)(2,1)}, f32[64,1536]{1,0:T(8,128)}, f32...) custom-call(s32[3,12]{1,0:T(4,128)} %bitcast.35, bf16[128,1536]{1,0:T(8,128)(2,1)} %bitcast.28, ...), custom_call_target="tpu_custom_call" | custom-call | tf_op jit(solution)/shard_map/pallas_call | solution.py:28
  8.2 4.8 %collective-permute-start.5 = (bf16[6,384,128]{2,1,0:T(8,128)(2,1)}, bf16[6,384,128]{2,1,0:T(8,128)(2,1)}, u32[]{:S(2)}, u32[]{:S(2)}) collective-permute-start(bf16[6,384,128]{2,1,0:T(8,128)(2,1)} %get-tuple-element.21.own), channel_id=1, source_target_pairs={{0,8},{8,16},{16,24},{1,9},{9,17},{17,25},{2,10},{10,18},{18,26},{... | collective-permute-start | bytes 1769480 | tf_op jit(solution)/shard_map/ppermute | solution.py:560
  14.2 5.7 %collective-permute-start = (bf16[6,384,128]{2,1,0:T(8,128)(2,1)}, bf16[6,384,128]{2,1,0:T(8,128)(2,1)}, u32[]{:S(2)}, u32[]{:S(2)}) collective-permute-start(bf16[6,384,128]{2,1,0:T(8,128)(2,1)} %get-tuple-element.21.own), channel_id=1, source_target_pairs={{1,2},{3,4},{5,6},{2,1},{4,3},{6,5},{9,10},{11,12},{13,14},{10,9},... | collective-permute-start | bytes 1769480 | tf_op jit(solution)/shard_map/ppermute | solution.py:614
  20.6 1.9 %collective-permute-done.4.far_stats = f32[64,128]{1,0:T(8,128)} collective-permute-done((f32[64,128]{1,0:T(8,128)}, f32[64,128]{1,0:T(8,128)}, u32[]{:S(2)}, u32[]{:S(2)}) %collective-permute-start.4) | collective-permute-done | bytes 32800 | tf_op jit(solution)/shard_map/ppermute | solution.py:564
  22.6 1.9 %collective-permute-done.3.far_sums = f32[64,1536]{1,0:T(8,128)} collective-permute-done((f32[64,1536]{1,0:T(8,128)}, f32[64,1536]{1,0:T(8,128)}, u32[]{:S(2)}, u32[]{:S(2)}) %collective-permute-start.3) | collective-permute-done | bytes 393248 | tf_op jit(solution)/shard_map/ppermute | solution.py:564
  24.5 4.5 %collective-permute-done.6.rest_1_.right = bf16[6,384,128]{2,1,0:T(8,128)(2,1)} collective-permute-done((bf16[6,384,128]{2,1,0:T(8,128)(2,1)}, bf16[6,384,128]{2,1,0:T(8,128)(2,1)}, u32[]{:S(2)}, u32[]{:S(2)}) %collective-permute-start.6) | collective-permute-done | bytes 589856 | tf_op jit(solution)/shard_map/ppermute | solution.py:560
  29.0 3.6 %shard_map.141.refs_1_.refs_0_ = bf16[3584,128]{1,0:T(8,128)(2,1)} custom-call(f32[64,1536]{1,0:T(8,128)} %get-tuple-element.23.sums, f32[64,128]{1,0:T(8,128)} %get-tuple-element.24.stats, f32[64,1536]{1,0:T(8,128)} %collective-permute-done.3.far_sums, f32[64,128]{1,0:T(8,128)} %collective-permute-done.4.far_stats, bf16[1,1536]{1,0:T(2,128)(2,1)} %bitcast.40, ...), custom_call_target="tpu_custom_call" | custom-call | bytes 2097152 | tf_op jit(solution)/shard_map/pallas_call | solution.py:28
  32.6 3.9 %collective-permute-start.7 = (bf16[3,128,384]{2,1,0:T(8,128)(2,1)}, bf16[3,128,384]{2,1,0:T(8,128)(2,1)}, u32[]{:S(2)}, u32[]{:S(2)}) collective-permute-start(bf16[3,128,384]{2,1,0:T(8,128)(2,1)} %shard_map.142.queries), channel_id=1, source_target_pairs={{0,32},{32,64},{64,96},{1,33},{33,65},{65,97},{2,34},{34,66},{66,9... | collective-permute-start | bytes 884744 | tf_op jit(solution)/shard_map/ppermute | solution.py:560
  36.5 2.2 %collective-permute-start.10 = (bf16[6,384,128]{2,1,0:T(8,128)(2,1)}, bf16[6,384,128]{2,1,0:T(8,128)(2,1)}, u32[]{:S(2)}, u32[]{:S(2)}) collective-permute-start(bf16[6,384,128]{2,1,0:T(8,128)(2,1)} %collective-permute-done.5.rest_0_.left), channel_id=1, source_target_pairs={{0,1},{1,0},{2,3},{3,2},{4,5},{5,4},{6,7},{7,6},{8,9},{9,8},{10,11... | collective-permute-start | bytes 1769480 | tf_op jit(solution)/shard_map/ppermute | solution.py:564
  38.7 3.1 %collective-permute-start.1 = (bf16[6,384,128]{2,1,0:T(8,128)(2,1)}, bf16[6,384,128]{2,1,0:T(8,128)(2,1)}, u32[]{:S(2)}, u32[]{:S(2)}) collective-permute-start(bf16[6,384,128]{2,1,0:T(8,128)(2,1)} %collective-permute-done.own.refs_1_), channel_id=1, source_target_pairs={{0,8},{8,16},{16,24},{1,9},{9,17},{17,25},{2,10},{10,18},{18,26},{... | collective-permute-start | bytes 1769480 | tf_op jit(solution)/shard_map/ppermute | solution.py:560
  44.4 15.3 %all-to-all-start = ((bf16[64,56,128]{2,1,0:T(8,128)(2,1)}), bf16[64,56,128]{2,1,0:T(8,128)(2,1)}, u32[]{:S(2)}, u32[]{:S(2)}) async-start(bf16[64,56,128]{2,1,0:T(8,128)(2,1)} %bitcast.20), calls=%async_computation | async-start | bytes 1835008 | tf_op jit(solution)/shard_map/all_to_all | solution.py:645
  59.7 13.1 %shard_map.143 = (f32[3,128,1152]{2,1,0:T(8,128)}, f32[3,8,1152]{2,1,0:T(8,128)}) custom-call(s32[3,12]{1,0:T(4,128)} %bitcast.36, bf16[6,384,128]{2,1,0:T(8,128)(2,1)} %get-tuple-element.21.own, bf16[6,384,128]{2,1,0:T(8,128)(2,1)} %collective-permute-done.5.rest_0_.left, bf16[6,384,128]{2,1,0:T(8,128)(2,1)} %collective-permute-done.6.rest_1_.right, ...), custom_call_target="tpu_custom_call" | custom-call | tf_op jit(solution)/shard_map/pallas_call | solution.py:28
  72.8 2.7 %collective-permute-start.15 = (bf16[384,3072]{1,0:T(8,128)(2,1)}, bf16[384,3072]{1,0:T(8,128)(2,1)}, u32[]{:S(2)}, u32[]{:S(2)}) collective-permute-start(bf16[384,3072]{1,0:T(8,128)(2,1)} %shard_map.148), channel_id=1, source_target_pairs={{0,128},{3,129},{2,130},{5,131},{4,132},{7,133},{6,134},{1,135},{1... | collective-permute-start | bytes 7077896 | tf_op jit(solution)/shard_map/ppermute | solution.py:677
  75.6 9.2 %shard_map.144 = (f32[3,128,384]{2,1,0:T(8,128)}, f32[3,8,384]{2,1,0:T(8,128)}, bf16[3,144,384]{2,1,0:T(8,128)(2,1)}, bf16[3,144,384]{2,1,0:T(8,128)(2,1)}) custom-call(s32[3,12]{1,0:T(4,128)} %bitcast.37, bf16[6,384,128]{2,1,0:T(8,128)(2,1)} %collective-permute-done.own.refs_1_, bf16[6,384,128]{2,1,0:T(8,128)(2,1)} %collective-permute-done.1.left, ...), custom_call_target="tpu_custom_call" | custom-call | flops 999999995904 | tf_op jit(solution)/shard_map/pallas_call | solution.py:28
  85.1 4.3 %collective-permute-start.12 = (bf16[3584,128]{1,0:T(8,128)(2,1)}, bf16[3584,128]{1,0:T(8,128)(2,1)}, u32[]{:S(2)}, u32[]{:S(2)}) collective-permute-start(bf16[3584,128]{1,0:T(8,128)(2,1)} %shard_map.146.got_low), channel_id=1, source_target_pairs={{0,1},{1,0},{2,3},{3,2},{4,5},{5,4},{6,7},{7,6},{8,9},{9,8},{10,11... | collective-permute-start | bytes 2752520 | tf_op jit(solution)/shard_map/ppermute | solution.py:564
  89.4 2.0 %collective-permute-start.13 = (bf16[3,144,384]{2,1,0:T(8,128)(2,1)}, bf16[3,144,384]{2,1,0:T(8,128)(2,1)}, u32[]{:S(2)}, u32[]{:S(2)}) collective-permute-start(bf16[3,144,384]{2,1,0:T(8,128)(2,1)} %get-tuple-element.34), channel_id=1, source_target_pairs={{0,32},{32,64},{64,96},{1,33},{33,65},{65,97},{2,34},{34,66},{66,9... | collective-permute-start | bytes 995336 | tf_op jit(solution)/shard_map/ppermute | solution.py:560
  93.3 10.5 %shard_map.147 = (bf16[1024,128]{1,0:T(8,128)(2,1)}, bf16[384,1536]{1,0:T(8,128)(2,1)}, f32[3,128,384]{2,1,0:T(8,128)}, f32[3,8,384]{2,1,0:T(8,128)}) custom-call(s32[3,12]{1,0:T(4,128)} %bitcast.38, s32[1]{0:T(128)S(6)} %copy.31.count, bf16[128,1536]{1,0:T(8,128)(2,1)} %bitcast.29, bf16[384,1536]{1,0:T(8,128)(2,1)} %bitcast.22, bf16[384,1536]{1,0:T(8,128)(2,1)} %bitcast.24, ...), custom_call_target="tpu_custom_call" | custom-call | flops 905969664 | bytes 5898240 | tf_op jit(solution)/shard_map/pallas_call | solution.py:28
  103.9 3.9 %collective-permute-done.15.refs_0_ = bf16[384,3072]{1,0:T(8,128)(2,1)} collective-permute-done((bf16[384,3072]{1,0:T(8,128)(2,1)}, bf16[384,3072]{1,0:T(8,128)(2,1)}, u32[]{:S(2)}, u32[]{:S(2)}) %collective-permute-start.15) | collective-permute-done | bytes 2359328 | tf_op jit(solution)/shard_map/ppermute | solution.py:677
  107.8 11.8 %all-to-all-start.1 = ((bf16[64,16,128]{2,1,0:T(8,128)(2,1)}), bf16[64,16,128]{2,1,0:T(8,128)(2,1)}, u32[]{:S(2)}, u32[]{:S(2)}) async-start(bf16[64,16,128]{2,1,0:T(8,128)(2,1)} %bitcast.12), calls=%async_computation.1 | async-start | bytes 524288 | tf_op jit(solution)/shard_map/all_to_all | solution.py:703
  119.6 11.7 %shard_map.151 = (f32[6,4,512]{2,1,0:T(4,128)}, f32[6,4,512]{2,1,0:T(4,128)}) custom-call(s32[3,12]{1,0:T(4,128)} %bitcast.39, f32[3,128,384]{2,1,0:T(8,128)} %get-tuple-element.29.sums, f32[3,8,384]{2,1,0:T(8,128)} %get-tuple-element.30.stats, f32[3,128,384]{2,1,0:T(8,128)} %get-tuple-element.32.text_sums, f32[3,8,384]{2,1,0:T(8,128)} %get-tuple-element.33.text_stats, ...), custom_call_target="tpu_custom_call" | custom-call | flops 3623878656 | bytes 16777216 | tf_op jit(solution)/shard_map/pallas_call | solution.py:28
  131.3 2.1 %all-to-all-done.1 = bf16[64,16,128]{2,1,0:T(8,128)(2,1)} async-done(((bf16[64,16,128]{2,1,0:T(8,128)(2,1)}), bf16[64,16,128]{2,1,0:T(8,128)(2,1)}, u32[]{:S(2)}, u32[]{:S(2)}) %all-to-all-start.1) | async-done | bytes 262176 | tf_op jit(solution)/shard_map/all_to_all | solution.py:703
  133.4 2.0 %collective-permute-start.18 = (bf16[1024,128]{1,0:T(8,128)(2,1)}, bf16[1024,128]{1,0:T(8,128)(2,1)}, u32[]{:S(2)}, u32[]{:S(2)}) collective-permute-start(bf16[1024,128]{1,0:T(8,128)(2,1)} %shard_map.152.mine), channel_id=1, source_target_pairs={{0,1},{1,0},{2,3},{3,2},{4,5},{5,4},{6,7},{7,6},{8,9},{9,8},{10,11... | collective-permute-start | bytes 786440 | tf_op jit(solution)/shard_map/ppermute | solution.py:564
  136.9 2.1 %shard_map.153.refs_1_ = bf16[128,1536]{1,0:T(8,128)(2,1)} custom-call(bf16[1024,128]{1,0:T(8,128)(2,1)} %shard_map.152.mine, bf16[1024,128]{1,0:T(8,128)(2,1)} %collective-permute-done.18.other), custom_call_target="tpu_custom_call" | custom-call | bytes 1048576 | tf_op jit(solution)/shard_map/pallas_call | solution.py:28
  139.1 1.5 %multiply_add_fusion = f32[3,8,512]{2,1,0:T(8,128)} fusion(f32[3,8,512]{2,1,0:T(8,128)} %bitcast.32, f32[3,8,512]{2,1,0:T(8,128)} %bitcast.17, f32[]{:T(128)} %bitcast.19, pred[]{:T(512)S(6)} %eq.4), kind=kLoop, calls=%fused_computation | loop fusion | flops 61440 | bytes 147461 | tf_op jit(solution)/shard_map/add | solution.py:734
  (34 shorter events, 7.1 us)
Async XLA Ops:
  8.2 16.4 %collective-permute-start.5 = (bf16[6,384,128]{2,1,0:T(8,128)(2,1)}, bf16[6,384,128]{2,1,0:T(8,128)(2,1)}, u32[]{:S(2)}, u32[]{:S(2)}) collective-permute-start(bf16[6,384,128]{2,1,0:T(8,128)(2,1)} %get-tuple-element.21.own), channel_id=1, source_target_pairs={{0,8},{8,16},{16,24},{1,9},{9,17},{17,25},{2,10},{10,18},{18,26},{... | collective-permute-start | bytes 1769480 | tf_op jit(solution)/shard_map/ppermute | solution.py:560
  13.0 16.1 %collective-permute-start.6 = (bf16[6,384,128]{2,1,0:T(8,128)(2,1)}, bf16[6,384,128]{2,1,0:T(8,128)(2,1)}, u32[]{:S(2)}, u32[]{:S(2)}) collective-permute-start(bf16[6,384,128]{2,1,0:T(8,128)(2,1)} %get-tuple-element.21.own), channel_id=1, source_target_pairs={{8,0},{16,8},{24,16},{9,1},{17,9},{25,17},{10,2},{18,10},{26,18},{... | collective-permute-start | bytes 1769480 | tf_op jit(solution)/shard_map/ppermute | solution.py:560
  14.2 24.4 %collective-permute-start = (bf16[6,384,128]{2,1,0:T(8,128)(2,1)}, bf16[6,384,128]{2,1,0:T(8,128)(2,1)}, u32[]{:S(2)}, u32[]{:S(2)}) collective-permute-start(bf16[6,384,128]{2,1,0:T(8,128)(2,1)} %get-tuple-element.21.own), channel_id=1, source_target_pairs={{1,2},{3,4},{5,6},{2,1},{4,3},{6,5},{9,10},{11,12},{13,14},{10,9},... | collective-permute-start | bytes 1769480 | tf_op jit(solution)/shard_map/ppermute | solution.py:614
  20.0 21.8 %collective-permute-start.9 = (bf16[6,384,128]{2,1,0:T(8,128)(2,1)}, bf16[6,384,128]{2,1,0:T(8,128)(2,1)}, u32[]{:S(2)}, u32[]{:S(2)}) collective-permute-start(bf16[6,384,128]{2,1,0:T(8,128)(2,1)} %get-tuple-element.21.own), channel_id=1, source_target_pairs={{0,1},{1,0},{2,3},{3,2},{4,5},{5,4},{6,7},{7,6},{8,9},{9,8},{10,11... | collective-permute-start | bytes 1769480 | tf_op jit(solution)/shard_map/ppermute | solution.py:564
  20.1 2.4 %collective-permute-start.4 = (f32[64,128]{1,0:T(8,128)}, f32[64,128]{1,0:T(8,128)}, u32[]{:S(2)}, u32[]{:S(2)}) collective-permute-start(f32[64,128]{1,0:T(8,128)} %get-tuple-element.26), channel_id=1, source_target_pairs={{0,1},{1,0},{2,3},{3,2},{4,5},{5,4},{6,7},{7,6},{8,9},{9,8},{10,11... | collective-permute-start | bytes 98312 | tf_op jit(solution)/shard_map/ppermute | solution.py:564
  22.5 2.1 %collective-permute-start.3 = (f32[64,1536]{1,0:T(8,128)}, f32[64,1536]{1,0:T(8,128)}, u32[]{:S(2)}, u32[]{:S(2)}) collective-permute-start(f32[64,1536]{1,0:T(8,128)} %get-tuple-element.25), channel_id=1, source_target_pairs={{0,1},{1,0},{2,3},{3,2},{4,5},{5,4},{6,7},{7,6},{8,9},{9,8},{10,11... | collective-permute-start | bytes 1179656 | tf_op jit(solution)/shard_map/ppermute | solution.py:564
  32.6 10.5 %collective-permute-start.7 = (bf16[3,128,384]{2,1,0:T(8,128)(2,1)}, bf16[3,128,384]{2,1,0:T(8,128)(2,1)}, u32[]{:S(2)}, u32[]{:S(2)}) collective-permute-start(bf16[3,128,384]{2,1,0:T(8,128)(2,1)} %shard_map.142.queries), channel_id=1, source_target_pairs={{0,32},{32,64},{64,96},{1,33},{33,65},{65,97},{2,34},{34,66},{66,9... | collective-permute-start | bytes 884744 | tf_op jit(solution)/shard_map/ppermute | solution.py:560
  36.5 23.2 %collective-permute-start.10 = (bf16[6,384,128]{2,1,0:T(8,128)(2,1)}, bf16[6,384,128]{2,1,0:T(8,128)(2,1)}, u32[]{:S(2)}, u32[]{:S(2)}) collective-permute-start(bf16[6,384,128]{2,1,0:T(8,128)(2,1)} %collective-permute-done.5.rest_0_.left), channel_id=1, source_target_pairs={{0,1},{1,0},{2,3},{3,2},{4,5},{5,4},{6,7},{7,6},{8,9},{9,8},{10,11... | collective-permute-start | bytes 1769480 | tf_op jit(solution)/shard_map/ppermute | solution.py:564
  38.7 21.1 %collective-permute-start.11 = (bf16[6,384,128]{2,1,0:T(8,128)(2,1)}, bf16[6,384,128]{2,1,0:T(8,128)(2,1)}, u32[]{:S(2)}, u32[]{:S(2)}) collective-permute-start(bf16[6,384,128]{2,1,0:T(8,128)(2,1)} %collective-permute-done.6.rest_1_.right), channel_id=1, source_target_pairs={{0,1},{1,0},{2,3},{3,2},{4,5},{5,4},{6,7},{7,6},{8,9},{9,8},{10,11... | collective-permute-start | bytes 1769480 | tf_op jit(solution)/shard_map/ppermute | solution.py:564
  38.7 36.9 %collective-permute-start.1 = (bf16[6,384,128]{2,1,0:T(8,128)(2,1)}, bf16[6,384,128]{2,1,0:T(8,128)(2,1)}, u32[]{:S(2)}, u32[]{:S(2)}) collective-permute-start(bf16[6,384,128]{2,1,0:T(8,128)(2,1)} %collective-permute-done.own.refs_1_), channel_id=1, source_target_pairs={{0,8},{8,16},{16,24},{1,9},{9,17},{17,25},{2,10},{10,18},{18,26},{... | collective-permute-start | bytes 1769480 | tf_op jit(solution)/shard_map/ppermute | solution.py:560
  41.8 33.8 %collective-permute-start.2 = (bf16[6,384,128]{2,1,0:T(8,128)(2,1)}, bf16[6,384,128]{2,1,0:T(8,128)(2,1)}, u32[]{:S(2)}, u32[]{:S(2)}) collective-permute-start(bf16[6,384,128]{2,1,0:T(8,128)(2,1)} %collective-permute-done.own.refs_1_), channel_id=1, source_target_pairs={{8,0},{16,8},{24,16},{9,1},{17,9},{25,17},{10,2},{18,10},{26,18},{... | collective-permute-start | bytes 1769480 | tf_op jit(solution)/shard_map/ppermute | solution.py:560
  43.1 16.6 %collective-permute-start.8 = (bf16[3,128,384]{2,1,0:T(8,128)(2,1)}, bf16[3,128,384]{2,1,0:T(8,128)(2,1)}, u32[]{:S(2)}, u32[]{:S(2)}) collective-permute-start(bf16[3,128,384]{2,1,0:T(8,128)(2,1)} %shard_map.142.queries), channel_id=1, source_target_pairs={{32,0},{64,32},{96,64},{33,1},{65,33},{97,65},{34,2},{66,34},{98,6... | collective-permute-start | bytes 884744 | tf_op jit(solution)/shard_map/ppermute | solution.py:560
  44.4 40.7 %all-to-all-start = ((bf16[64,56,128]{2,1,0:T(8,128)(2,1)}), bf16[64,56,128]{2,1,0:T(8,128)(2,1)}, u32[]{:S(2)}, u32[]{:S(2)}) async-start(bf16[64,56,128]{2,1,0:T(8,128)(2,1)} %bitcast.20), calls=%async_computation | async-start | bytes 1835008 | tf_op jit(solution)/shard_map/all_to_all | solution.py:645
  72.8 34.9 %collective-permute-start.15 = (bf16[384,3072]{1,0:T(8,128)(2,1)}, bf16[384,3072]{1,0:T(8,128)(2,1)}, u32[]{:S(2)}, u32[]{:S(2)}) collective-permute-start(bf16[384,3072]{1,0:T(8,128)(2,1)} %shard_map.148), channel_id=1, source_target_pairs={{0,128},{3,129},{2,130},{5,131},{4,132},{7,133},{6,134},{1,135},{1... | collective-permute-start | bytes 7077896 | tf_op jit(solution)/shard_map/ppermute | solution.py:677
  85.1 8.2 %collective-permute-start.12 = (bf16[3584,128]{1,0:T(8,128)(2,1)}, bf16[3584,128]{1,0:T(8,128)(2,1)}, u32[]{:S(2)}, u32[]{:S(2)}) collective-permute-start(bf16[3584,128]{1,0:T(8,128)(2,1)} %shard_map.146.got_low), channel_id=1, source_target_pairs={{0,1},{1,0},{2,3},{3,2},{4,5},{5,4},{6,7},{7,6},{8,9},{9,8},{10,11... | collective-permute-start | bytes 2752520 | tf_op jit(solution)/shard_map/ppermute | solution.py:564
  89.4 14.5 %collective-permute-start.13 = (bf16[3,144,384]{2,1,0:T(8,128)(2,1)}, bf16[3,144,384]{2,1,0:T(8,128)(2,1)}, u32[]{:S(2)}, u32[]{:S(2)}) collective-permute-start(bf16[3,144,384]{2,1,0:T(8,128)(2,1)} %get-tuple-element.34), channel_id=1, source_target_pairs={{0,32},{32,64},{64,96},{1,33},{33,65},{65,97},{2,34},{34,66},{66,9... | collective-permute-start | bytes 995336 | tf_op jit(solution)/shard_map/ppermute | solution.py:560
  91.4 12.5 %collective-permute-start.14 = (bf16[3,144,384]{2,1,0:T(8,128)(2,1)}, bf16[3,144,384]{2,1,0:T(8,128)(2,1)}, u32[]{:S(2)}, u32[]{:S(2)}) collective-permute-start(bf16[3,144,384]{2,1,0:T(8,128)(2,1)} %get-tuple-element.31.refs_1_.after), channel_id=1, source_target_pairs={{32,0},{64,32},{96,64},{33,1},{65,33},{97,65},{34,2},{66,34},{98,6... | collective-permute-start | bytes 995336 | tf_op jit(solution)/shard_map/ppermute | solution.py:560
  107.8 11.8 %collective-permute-start.16 = (bf16[384,3072]{1,0:T(8,128)(2,1)}, bf16[384,3072]{1,0:T(8,128)(2,1)}, u32[]{:S(2)}, u32[]{:S(2)}) collective-permute-start(bf16[384,3072]{1,0:T(8,128)(2,1)} %shard_map.150.w_mine), channel_id=1, source_target_pairs={{0,1},{1,0},{2,3},{3,2},{4,5},{5,4},{6,7},{7,6},{8,9},{9,8},{10,11... | collective-permute-start | bytes 7077896 | tf_op jit(solution)/shard_map/ppermute | solution.py:564
  107.8 25.7 %all-to-all-start.1 = ((bf16[64,16,128]{2,1,0:T(8,128)(2,1)}), bf16[64,16,128]{2,1,0:T(8,128)(2,1)}, u32[]{:S(2)}, u32[]{:S(2)}) async-start(bf16[64,16,128]{2,1,0:T(8,128)(2,1)} %bitcast.12), calls=%async_computation.1 | async-start | bytes 524288 | tf_op jit(solution)/shard_map/all_to_all | solution.py:703
  133.4 3.5 %collective-permute-start.18 = (bf16[1024,128]{1,0:T(8,128)(2,1)}, bf16[1024,128]{1,0:T(8,128)(2,1)}, u32[]{:S(2)}, u32[]{:S(2)}) collective-permute-start(bf16[1024,128]{1,0:T(8,128)(2,1)} %shard_map.152.mine), channel_id=1, source_target_pairs={{0,1},{1,0},{2,3},{3,2},{4,5},{5,4},{6,7},{7,6},{8,9},{9,8},{10,11... | collective-permute-start | bytes 786440 | tf_op jit(solution)/shard_map/ppermute | solution.py:564
  135.4 3.7 %collective-permute-start.17 = (f32[6,4,512]{2,1,0:T(4,128)}, f32[6,4,512]{2,1,0:T(4,128)}, u32[]{:S(2)}, u32[]{:S(2)}) collective-permute-start(f32[6,4,512]{2,1,0:T(4,128)} %get-tuple-element.38), channel_id=1, source_target_pairs={{0,128},{128,0},{1,129},{129,1},{2,130},{130,2},{3,131},{131,3},{4... | collective-permute-start | bytes 147464 | tf_op jit(solution)/shard_map/ppermute | solution.py:731

commit v5 on v4

--- a/solution.py
+++ b/solution.py
@@ -702,7 +702,7 @@
     w_other = swap_core(w_mine)
     text_mine = lax.all_to_all(finished, CHIPS, 0, 0, tiled=True)
 
-    parts = 6
+    parts = 12
     half_rows = rows // branches
     half_out = shape((frames, half_rows, cols * final_weight.shape[1]), f32)
     kept, sent = call(

time: 141 us -> 141 us (level)
  starting transfers between devices: 64.4 us -> 61.7 us
  waiting for transfers between devices: 14.8 us -> 17.3 us
    all_to_all x1, waiting for transfers between devices: 0.29 us -> 4.47 us  [local(): got = lax.all_to_all(parcel, CHIPS, 0, 0, tiled=True)]
    all_to_all x1, waiting for transfers between devices: 2.1 us -> 0.01 us  [local(): text_mine = lax.all_to_all(finished, CHIPS, 0, 0, tiled=True)]
    ppermute x8, starting transfers between devices: 9.11 us -> 7.15 us  [swap_core(): return lax.ppermute(x, 'co', [(0, 1), (1, 0)])]
  transfers between devices with their start and end apart: 21 -> 21, of which waited for: 7 -> 5; matrix products, arithmetic and copies ran while one was open for 0% -> 0% of each run, Pallas kernels for 36% -> 35%
where the time goes in v5:
time: 141 us; the launch traced here: 140 us
  starting transfers between devices  61.7 us (44%)
  Pallas kernels  57.1 us (40%)
  waiting for transfers between devices  17.3 us (12%)
  between operations  2.13 us (2%)
  other arithmetic  1.45 us (1%)
    pallas_call x7, Pallas kernels, call(): pl.pallas_call(body, grid=(1,), out_shape=out_shape, in_specs=in_specs, o...  57.1 us
    ppermute x8, starting transfers between devices, shift(): lax.ppermute(x, axis, [(i, i + step) for i in range(size) if 0 <= i + ste...  18.9 us
    all_to_all x1, starting transfers between devices, local(): got = lax.all_to_all(parcel, CHIPS, 0, 0, tiled=True)  15.3 us
    all_to_all x1, starting transfers between devices, local(): text_mine = lax.all_to_all(finished, CHIPS, 0, 0, tiled=True)  11 us
    ppermute x8, starting transfers between devices, swap_core(): return lax.ppermute(x, 'co', [(0, 1), (1, 0)])  7.15 us
    ppermute x1, starting transfers between devices, local(): next_pairs = lax.ppermute(pairs, ('zh', 'co'), beside)  5.74 us
    ppermute x8, waiting for transfers between devices, shift(): lax.ppermute(x, axis, [(i, i + step) for i in range(size) if 0 <= i + ste...  4.5 us
    ppermute x1, waiting for transfers between devices, local(): lax.ppermute(after(quarter, near_stats), ('cfg', 'zh', 'co'), weight_pairs)  4.47 us
  transfers between devices with their start and end apart: 21, of which 5 were waited for; matrix products, arithmetic and copies ran while one was open for 0% of the time, Pallas kernels for 35%

profile of v5, /device:TPU:1, one launch (start us, length us, event | category | flops | bytes accessed | tf_op | source)
XLA Modules:
  0.0 139.7 jit_solution(16771240837025980853)
XLA Ops:
  0.6 7.6 %shard_map.140 = (bf16[6,384,128]{2,1,0:T(8,128)(2,1)}, bf16[3,128,384]{2,1,0:T(8,128)(2,1)}, bf16[384,3072]{1,0:T(8,128)(2,1)}, f32[64,1536]{1,0:T(8,128)}, f32...) custom-call(s32[3,12]{1,0:T(4,128)} %bitcast.35, bf16[128,1536]{1,0:T(8,128)(2,1)} %bitcast.28, ...), custom_call_target="tpu_custom_call" | custom-call | tf_op jit(solution)/shard_map/pallas_call | solution.py:28
  8.2 4.8 %collective-permute-start.5 = (bf16[6,384,128]{2,1,0:T(8,128)(2,1)}, bf16[6,384,128]{2,1,0:T(8,128)(2,1)}, u32[]{:S(2)}, u32[]{:S(2)}) collective-permute-start(bf16[6,384,128]{2,1,0:T(8,128)(2,1)} %get-tuple-element.21.own), channel_id=1, source_target_pairs={{0,8},{8,16},{16,24},{1,9},{9,17},{17,25},{2,10},{10,18},{18,26},{... | collective-permute-start | bytes 1769480 | tf_op jit(solution)/shard_map/ppermute | solution.py:560
  14.2 5.7 %collective-permute-start = (bf16[6,384,128]{2,1,0:T(8,128)(2,1)}, bf16[6,384,128]{2,1,0:T(8,128)(2,1)}, u32[]{:S(2)}, u32[]{:S(2)}) collective-permute-start(bf16[6,384,128]{2,1,0:T(8,128)(2,1)} %get-tuple-element.21.own), channel_id=1, source_target_pairs={{1,2},{3,4},{5,6},{2,1},{4,3},{6,5},{9,10},{11,12},{13,14},{10,9},... | collective-permute-start | bytes 1769480 | tf_op jit(solution)/shard_map/ppermute | solution.py:614
  20.6 1.9 %collective-permute-done.4.far_stats = f32[64,128]{1,0:T(8,128)} collective-permute-done((f32[64,128]{1,0:T(8,128)}, f32[64,128]{1,0:T(8,128)}, u32[]{:S(2)}, u32[]{:S(2)}) %collective-permute-start.4) | collective-permute-done | bytes 32800 | tf_op jit(solution)/shard_map/ppermute | solution.py:564
  22.6 1.9 %collective-permute-done.3.far_sums = f32[64,1536]{1,0:T(8,128)} collective-permute-done((f32[64,1536]{1,0:T(8,128)}, f32[64,1536]{1,0:T(8,128)}, u32[]{:S(2)}, u32[]{:S(2)}) %collective-permute-start.3) | collective-permute-done | bytes 393248 | tf_op jit(solution)/shard_map/ppermute | solution.py:564
  24.5 4.5 %collective-permute-done.6.rest_1_.right = bf16[6,384,128]{2,1,0:T(8,128)(2,1)} collective-permute-done((bf16[6,384,128]{2,1,0:T(8,128)(2,1)}, bf16[6,384,128]{2,1,0:T(8,128)(2,1)}, u32[]{:S(2)}, u32[]{:S(2)}) %collective-permute-start.6) | collective-permute-done | bytes 589856 | tf_op jit(solution)/shard_map/ppermute | solution.py:560
  29.0 3.6 %shard_map.141.refs_1_.refs_0_ = bf16[3584,128]{1,0:T(8,128)(2,1)} custom-call(f32[64,1536]{1,0:T(8,128)} %get-tuple-element.23.sums, f32[64,128]{1,0:T(8,128)} %get-tuple-element.24.stats, f32[64,1536]{1,0:T(8,128)} %collective-permute-done.3.far_sums, f32[64,128]{1,0:T(8,128)} %collective-permute-done.4.far_stats, bf16[1,1536]{1,0:T(2,128)(2,1)} %bitcast.40, ...), custom_call_target="tpu_custom_call" | custom-call | bytes 2097152 | tf_op jit(solution)/shard_map/pallas_call | solution.py:28
  32.6 3.9 %collective-permute-start.7 = (bf16[3,128,384]{2,1,0:T(8,128)(2,1)}, bf16[3,128,384]{2,1,0:T(8,128)(2,1)}, u32[]{:S(2)}, u32[]{:S(2)}) collective-permute-start(bf16[3,128,384]{2,1,0:T(8,128)(2,1)} %shard_map.142.queries), channel_id=1, source_target_pairs={{0,32},{32,64},{64,96},{1,33},{33,65},{65,97},{2,34},{34,66},{66,9... | collective-permute-start | bytes 884744 | tf_op jit(solution)/shard_map/ppermute | solution.py:560
  36.5 2.2 %collective-permute-start.10 = (bf16[6,384,128]{2,1,0:T(8,128)(2,1)}, bf16[6,384,128]{2,1,0:T(8,128)(2,1)}, u32[]{:S(2)}, u32[]{:S(2)}) collective-permute-start(bf16[6,384,128]{2,1,0:T(8,128)(2,1)} %collective-permute-done.5.rest_0_.left), channel_id=1, source_target_pairs={{0,1},{1,0},{2,3},{3,2},{4,5},{5,4},{6,7},{7,6},{8,9},{9,8},{10,11... | collective-permute-start | bytes 1769480 | tf_op jit(solution)/shard_map/ppermute | solution.py:564
  38.7 3.1 %collective-permute-start.1 = (bf16[6,384,128]{2,1,0:T(8,128)(2,1)}, bf16[6,384,128]{2,1,0:T(8,128)(2,1)}, u32[]{:S(2)}, u32[]{:S(2)}) collective-permute-start(bf16[6,384,128]{2,1,0:T(8,128)(2,1)} %collective-permute-done.own.refs_1_), channel_id=1, source_target_pairs={{0,8},{8,16},{16,24},{1,9},{9,17},{17,25},{2,10},{10,18},{18,26},{... | collective-permute-start | bytes 1769480 | tf_op jit(solution)/shard_map/ppermute | solution.py:560
  43.1 1.3 collective-permute-start.8
  44.4 15.3 %all-to-all-start = ((bf16[64,56,128]{2,1,0:T(8,128)(2,1)}), bf16[64,56,128]{2,1,0:T(8,128)(2,1)}, u32[]{:S(2)}, u32[]{:S(2)}) async-start(bf16[64,56,128]{2,1,0:T(8,128)(2,1)} %bitcast.20), calls=%async_computation | async-start | bytes 1835008 | tf_op jit(solution)/shard_map/all_to_all | solution.py:645
  59.7 11.5 %shard_map.143 = (f32[3,128,1152]{2,1,0:T(8,128)}, f32[3,8,1152]{2,1,0:T(8,128)}) custom-call(s32[3,12]{1,0:T(4,128)} %bitcast.36, bf16[6,384,128]{2,1,0:T(8,128)(2,1)} %get-tuple-element.21.own, bf16[6,384,128]{2,1,0:T(8,128)(2,1)} %collective-permute-done.5.rest_0_.left, bf16[6,384,128]{2,1,0:T(8,128)(2,1)} %collective-permute-done.6.rest_1_.right, ...), custom_call_target="tpu_custom_call" | custom-call | tf_op jit(solution)/shard_map/pallas_call | solution.py:28
  71.3 2.7 %collective-permute-start.15 = (bf16[384,3072]{1,0:T(8,128)(2,1)}, bf16[384,3072]{1,0:T(8,128)(2,1)}, u32[]{:S(2)}, u32[]{:S(2)}) collective-permute-start(bf16[384,3072]{1,0:T(8,128)(2,1)} %shard_map.148), channel_id=1, source_target_pairs={{0,128},{3,129},{2,130},{5,131},{4,132},{7,133},{6,134},{1,135},{1... | collective-permute-start | bytes 7077896 | tf_op jit(solution)/shard_map/ppermute | solution.py:677
  74.0 6.6 %shard_map.144 = (f32[3,128,384]{2,1,0:T(8,128)}, f32[3,8,384]{2,1,0:T(8,128)}, bf16[3,144,384]{2,1,0:T(8,128)(2,1)}, bf16[3,144,384]{2,1,0:T(8,128)(2,1)}) custom-call(s32[3,12]{1,0:T(4,128)} %bitcast.37, bf16[6,384,128]{2,1,0:T(8,128)(2,1)} %collective-permute-done.own.refs_1_, bf16[6,384,128]{2,1,0:T(8,128)(2,1)} %collective-permute-done.1.left, ...), custom_call_target="tpu_custom_call" | custom-call | flops 999999995904 | tf_op jit(solution)/shard_map/pallas_call | solution.py:28
  80.6 4.5 %all-to-all-done = bf16[64,56,128]{2,1,0:T(8,128)(2,1)} async-done(((bf16[64,56,128]{2,1,0:T(8,128)(2,1)}), bf16[64,56,128]{2,1,0:T(8,128)(2,1)}, u32[]{:S(2)}, u32[]{:S(2)}) %all-to-all-start) | async-done | bytes 917536 | tf_op jit(solution)/shard_map/all_to_all | solution.py:645
  85.1 3.7 %collective-permute-start.12 = (bf16[3584,128]{1,0:T(8,128)(2,1)}, bf16[3584,128]{1,0:T(8,128)(2,1)}, u32[]{:S(2)}, u32[]{:S(2)}) collective-permute-start(bf16[3584,128]{1,0:T(8,128)(2,1)} %shard_map.146.got_low), channel_id=1, source_target_pairs={{0,1},{1,0},{2,3},{3,2},{4,5},{5,4},{6,7},{7,6},{8,9},{9,8},{10,11... | collective-permute-start | bytes 2752520 | tf_op jit(solution)/shard_map/ppermute | solution.py:564
  88.8 2.0 %collective-permute-start.13 = (bf16[3,144,384]{2,1,0:T(8,128)(2,1)}, bf16[3,144,384]{2,1,0:T(8,128)(2,1)}, u32[]{:S(2)}, u32[]{:S(2)}) collective-permute-start(bf16[3,144,384]{2,1,0:T(8,128)(2,1)} %get-tuple-element.34), channel_id=1, source_target_pairs={{0,32},{32,64},{64,96},{1,33},{33,65},{65,97},{2,34},{34,66},{66,9... | collective-permute-start | bytes 995336 | tf_op jit(solution)/shard_map/ppermute | solution.py:560
  92.8 10.5 %shard_map.147 = (bf16[1024,128]{1,0:T(8,128)(2,1)}, bf16[384,1536]{1,0:T(8,128)(2,1)}, f32[3,128,384]{2,1,0:T(8,128)}, f32[3,8,384]{2,1,0:T(8,128)}) custom-call(s32[3,12]{1,0:T(4,128)} %bitcast.38, s32[1]{0:T(128)S(6)} %copy.31.count, bf16[128,1536]{1,0:T(8,128)(2,1)} %bitcast.29, bf16[384,1536]{1,0:T(8,128)(2,1)} %bitcast.22, bf16[384,1536]{1,0:T(8,128)(2,1)} %bitcast.24, ...), custom_call_target="tpu_custom_call" | custom-call | flops 905969664 | bytes 5898240 | tf_op jit(solution)/shard_map/pallas_call | solution.py:28
  103.3 4.5 %collective-permute-done.15.refs_0_ = bf16[384,3072]{1,0:T(8,128)(2,1)} collective-permute-done((bf16[384,3072]{1,0:T(8,128)(2,1)}, bf16[384,3072]{1,0:T(8,128)(2,1)}, u32[]{:S(2)}, u32[]{:S(2)}) %collective-permute-start.15) | collective-permute-done | bytes 2359328 | tf_op jit(solution)/shard_map/ppermute | solution.py:677
  107.8 11.0 %all-to-all-start.1 = ((bf16[64,16,128]{2,1,0:T(8,128)(2,1)}), bf16[64,16,128]{2,1,0:T(8,128)(2,1)}, u32[]{:S(2)}, u32[]{:S(2)}) async-start(bf16[64,16,128]{2,1,0:T(8,128)(2,1)} %bitcast.12), calls=%async_computation.1 | async-start | bytes 524288 | tf_op jit(solution)/shard_map/all_to_all | solution.py:703
  118.8 15.2 %shard_map.151 = (f32[6,4,512]{2,1,0:T(4,128)}, f32[6,4,512]{2,1,0:T(4,128)}) custom-call(s32[3,12]{1,0:T(4,128)} %bitcast.39, f32[3,128,384]{2,1,0:T(8,128)} %get-tuple-element.29.sums, f32[3,8,384]{2,1,0:T(8,128)} %get-tuple-element.30.stats, f32[3,128,384]{2,1,0:T(8,128)} %get-tuple-element.32.text_sums, f32[3,8,384]{2,1,0:T(8,128)} %get-tuple-element.33.text_stats, ...), custom_call_target="tpu_custom_call" | custom-call | flops 3623878656 | bytes 16777216 | tf_op jit(solution)/shard_map/pallas_call | solution.py:28
  136.1 2.1 %shard_map.153.refs_1_ = bf16[128,1536]{1,0:T(8,128)(2,1)} custom-call(bf16[1024,128]{1,0:T(8,128)(2,1)} %shard_map.152.mine, bf16[1024,128]{1,0:T(8,128)(2,1)} %collective-permute-done.18.other), custom_call_target="tpu_custom_call" | custom-call | bytes 1048576 | tf_op jit(solution)/shard_map/pallas_call | solution.py:28
  138.2 1.5 %multiply_add_fusion = f32[3,8,512]{2,1,0:T(8,128)} fusion(f32[3,8,512]{2,1,0:T(8,128)} %bitcast.32, f32[3,8,512]{2,1,0:T(8,128)} %bitcast.17, f32[]{:T(128)} %bitcast.19, pred[]{:T(512)S(6)} %eq.4), kind=kLoop, calls=%fused_computation | loop fusion | flops 61440 | bytes 147461 | tf_op jit(solution)/shard_map/add | solution.py:734
  (34 shorter events, 6.1 us)
Async XLA Ops:
  8.2 16.4 %collective-permute-start.5 = (bf16[6,384,128]{2,1,0:T(8,128)(2,1)}, bf16[6,384,128]{2,1,0:T(8,128)(2,1)}, u32[]{:S(2)}, u32[]{:S(2)}) collective-permute-start(bf16[6,384,128]{2,1,0:T(8,128)(2,1)} %get-tuple-element.21.own), channel_id=1, source_target_pairs={{0,8},{8,16},{16,24},{1,9},{9,17},{17,25},{2,10},{10,18},{18,26},{... | collective-permute-start | bytes 1769480 | tf_op jit(solution)/shard_map/ppermute | solution.py:560
  13.0 16.1 %collective-permute-start.6 = (bf16[6,384,128]{2,1,0:T(8,128)(2,1)}, bf16[6,384,128]{2,1,0:T(8,128)(2,1)}, u32[]{:S(2)}, u32[]{:S(2)}) collective-permute-start(bf16[6,384,128]{2,1,0:T(8,128)(2,1)} %get-tuple-element.21.own), channel_id=1, source_target_pairs={{8,0},{16,8},{24,16},{9,1},{17,9},{25,17},{10,2},{18,10},{26,18},{... | collective-permute-start | bytes 1769480 | tf_op jit(solution)/shard_map/ppermute | solution.py:560
  14.2 24.4 %collective-permute-start = (bf16[6,384,128]{2,1,0:T(8,128)(2,1)}, bf16[6,384,128]{2,1,0:T(8,128)(2,1)}, u32[]{:S(2)}, u32[]{:S(2)}) collective-permute-start(bf16[6,384,128]{2,1,0:T(8,128)(2,1)} %get-tuple-element.21.own), channel_id=1, source_target_pairs={{1,2},{3,4},{5,6},{2,1},{4,3},{6,5},{9,10},{11,12},{13,14},{10,9},... | collective-permute-start | bytes 1769480 | tf_op jit(solution)/shard_map/ppermute | solution.py:614
  20.0 21.8 %collective-permute-start.9 = (bf16[6,384,128]{2,1,0:T(8,128)(2,1)}, bf16[6,384,128]{2,1,0:T(8,128)(2,1)}, u32[]{:S(2)}, u32[]{:S(2)}) collective-permute-start(bf16[6,384,128]{2,1,0:T(8,128)(2,1)} %get-tuple-element.21.own), channel_id=1, source_target_pairs={{0,1},{1,0},{2,3},{3,2},{4,5},{5,4},{6,7},{7,6},{8,9},{9,8},{10,11... | collective-permute-start | bytes 1769480 | tf_op jit(solution)/shard_map/ppermute | solution.py:564
  20.1 2.4 %collective-permute-start.4 = (f32[64,128]{1,0:T(8,128)}, f32[64,128]{1,0:T(8,128)}, u32[]{:S(2)}, u32[]{:S(2)}) collective-permute-start(f32[64,128]{1,0:T(8,128)} %get-tuple-element.26), channel_id=1, source_target_pairs={{0,1},{1,0},{2,3},{3,2},{4,5},{5,4},{6,7},{7,6},{8,9},{9,8},{10,11... | collective-permute-start | bytes 98312 | tf_op jit(solution)/shard_map/ppermute | solution.py:564
  22.5 2.1 %collective-permute-start.3 = (f32[64,1536]{1,0:T(8,128)}, f32[64,1536]{1,0:T(8,128)}, u32[]{:S(2)}, u32[]{:S(2)}) collective-permute-start(f32[64,1536]{1,0:T(8,128)} %get-tuple-element.25), channel_id=1, source_target_pairs={{0,1},{1,0},{2,3},{3,2},{4,5},{5,4},{6,7},{7,6},{8,9},{9,8},{10,11... | collective-permute-start | bytes 1179656 | tf_op jit(solution)/shard_map/ppermute | solution.py:564
  32.6 10.5 %collective-permute-start.7 = (bf16[3,128,384]{2,1,0:T(8,128)(2,1)}, bf16[3,128,384]{2,1,0:T(8,128)(2,1)}, u32[]{:S(2)}, u32[]{:S(2)}) collective-permute-start(bf16[3,128,384]{2,1,0:T(8,128)(2,1)} %shard_map.142.queries), channel_id=1, source_target_pairs={{0,32},{32,64},{64,96},{1,33},{33,65},{65,97},{2,34},{34,66},{66,9... | collective-permute-start | bytes 884744 | tf_op jit(solution)/shard_map/ppermute | solution.py:560
  36.5 23.2 %collective-permute-start.10 = (bf16[6,384,128]{2,1,0:T(8,128)(2,1)}, bf16[6,384,128]{2,1,0:T(8,128)(2,1)}, u32[]{:S(2)}, u32[]{:S(2)}) collective-permute-start(bf16[6,384,128]{2,1,0:T(8,128)(2,1)} %collective-permute-done.5.rest_0_.left), channel_id=1, source_target_pairs={{0,1},{1,0},{2,3},{3,2},{4,5},{5,4},{6,7},{7,6},{8,9},{9,8},{10,11... | collective-permute-start | bytes 1769480 | tf_op jit(solution)/shard_map/ppermute | solution.py:564
  38.7 21.1 %collective-permute-start.11 = (bf16[6,384,128]{2,1,0:T(8,128)(2,1)}, bf16[6,384,128]{2,1,0:T(8,128)(2,1)}, u32[]{:S(2)}, u32[]{:S(2)}) collective-permute-start(bf16[6,384,128]{2,1,0:T(8,128)(2,1)} %collective-permute-done.6.rest_1_.right), channel_id=1, source_target_pairs={{0,1},{1,0},{2,3},{3,2},{4,5},{5,4},{6,7},{7,6},{8,9},{9,8},{10,11... | collective-permute-start | bytes 1769480 | tf_op jit(solution)/shard_map/ppermute | solution.py:564
  38.7 35.4 %collective-permute-start.1 = (bf16[6,384,128]{2,1,0:T(8,128)(2,1)}, bf16[6,384,128]{2,1,0:T(8,128)(2,1)}, u32[]{:S(2)}, u32[]{:S(2)}) collective-permute-start(bf16[6,384,128]{2,1,0:T(8,128)(2,1)} %collective-permute-done.own.refs_1_), channel_id=1, source_target_pairs={{0,8},{8,16},{16,24},{1,9},{9,17},{17,25},{2,10},{10,18},{18,26},{... | collective-permute-start | bytes 1769480 | tf_op jit(solution)/shard_map/ppermute | solution.py:560
  41.8 32.2 %collective-permute-start.2 = (bf16[6,384,128]{2,1,0:T(8,128)(2,1)}, bf16[6,384,128]{2,1,0:T(8,128)(2,1)}, u32[]{:S(2)}, u32[]{:S(2)}) collective-permute-start(bf16[6,384,128]{2,1,0:T(8,128)(2,1)} %collective-permute-done.own.refs_1_), channel_id=1, source_target_pairs={{8,0},{16,8},{24,16},{9,1},{17,9},{25,17},{10,2},{18,10},{26,18},{... | collective-permute-start | bytes 1769480 | tf_op jit(solution)/shard_map/ppermute | solution.py:560
  43.1 16.6 %collective-permute-start.8 = (bf16[3,128,384]{2,1,0:T(8,128)(2,1)}, bf16[3,128,384]{2,1,0:T(8,128)(2,1)}, u32[]{:S(2)}, u32[]{:S(2)}) collective-permute-start(bf16[3,128,384]{2,1,0:T(8,128)(2,1)} %shard_map.142.queries), channel_id=1, source_target_pairs={{32,0},{64,32},{96,64},{33,1},{65,33},{97,65},{34,2},{66,34},{98,6... | collective-permute-start | bytes 884744 | tf_op jit(solution)/shard_map/ppermute | solution.py:560
  44.4 40.7 %all-to-all-start = ((bf16[64,56,128]{2,1,0:T(8,128)(2,1)}), bf16[64,56,128]{2,1,0:T(8,128)(2,1)}, u32[]{:S(2)}, u32[]{:S(2)}) async-start(bf16[64,56,128]{2,1,0:T(8,128)(2,1)} %bitcast.20), calls=%async_computation | async-start | bytes 1835008 | tf_op jit(solution)/shard_map/all_to_all | solution.py:645
  71.3 36.5 %collective-permute-start.15 = (bf16[384,3072]{1,0:T(8,128)(2,1)}, bf16[384,3072]{1,0:T(8,128)(2,1)}, u32[]{:S(2)}, u32[]{:S(2)}) collective-permute-start(bf16[384,3072]{1,0:T(8,128)(2,1)} %shard_map.148), channel_id=1, source_target_pairs={{0,128},{3,129},{2,130},{5,131},{4,132},{7,133},{6,134},{1,135},{1... | collective-permute-start | bytes 7077896 | tf_op jit(solution)/shard_map/ppermute | solution.py:677
  85.1 7.7 %collective-permute-start.12 = (bf16[3584,128]{1,0:T(8,128)(2,1)}, bf16[3584,128]{1,0:T(8,128)(2,1)}, u32[]{:S(2)}, u32[]{:S(2)}) collective-permute-start(bf16[3584,128]{1,0:T(8,128)(2,1)} %shard_map.146.got_low), channel_id=1, source_target_pairs={{0,1},{1,0},{2,3},{3,2},{4,5},{5,4},{6,7},{7,6},{8,9},{9,8},{10,11... | collective-permute-start | bytes 2752520 | tf_op jit(solution)/shard_map/ppermute | solution.py:564
  88.8 14.5 %collective-permute-start.13 = (bf16[3,144,384]{2,1,0:T(8,128)(2,1)}, bf16[3,144,384]{2,1,0:T(8,128)(2,1)}, u32[]{:S(2)}, u32[]{:S(2)}) collective-permute-start(bf16[3,144,384]{2,1,0:T(8,128)(2,1)} %get-tuple-element.34), channel_id=1, source_target_pairs={{0,32},{32,64},{64,96},{1,33},{33,65},{65,97},{2,34},{34,66},{66,9... | collective-permute-start | bytes 995336 | tf_op jit(solution)/shard_map/ppermute | solution.py:560
  90.9 12.4 %collective-permute-start.14 = (bf16[3,144,384]{2,1,0:T(8,128)(2,1)}, bf16[3,144,384]{2,1,0:T(8,128)(2,1)}, u32[]{:S(2)}, u32[]{:S(2)}) collective-permute-start(bf16[3,144,384]{2,1,0:T(8,128)(2,1)} %get-tuple-element.31.refs_1_.after), channel_id=1, source_target_pairs={{32,0},{64,32},{96,64},{33,1},{65,33},{97,65},{34,2},{66,34},{98,6... | collective-permute-start | bytes 995336 | tf_op jit(solution)/shard_map/ppermute | solution.py:560
  107.8 11.0 %collective-permute-start.16 = (bf16[384,3072]{1,0:T(8,128)(2,1)}, bf16[384,3072]{1,0:T(8,128)(2,1)}, u32[]{:S(2)}, u32[]{:S(2)}) collective-permute-start(bf16[384,3072]{1,0:T(8,128)(2,1)} %shard_map.150.w_mine), channel_id=1, source_target_pairs={{0,1},{1,0},{2,3},{3,2},{4,5},{5,4},{6,7},{7,6},{8,9},{9,8},{10,11... | collective-permute-start | bytes 7077896 | tf_op jit(solution)/shard_map/ppermute | solution.py:564
  107.8 26.3 %all-to-all-start.1 = ((bf16[64,16,128]{2,1,0:T(8,128)(2,1)}), bf16[64,16,128]{2,1,0:T(8,128)(2,1)}, u32[]{:S(2)}, u32[]{:S(2)}) async-start(bf16[64,16,128]{2,1,0:T(8,128)(2,1)} %bitcast.12), calls=%async_computation.1 | async-start | bytes 524288 | tf_op jit(solution)/shard_map/all_to_all | solution.py:703
  134.1 2.1 %collective-permute-start.18 = (bf16[1024,128]{1,0:T(8,128)(2,1)}, bf16[1024,128]{1,0:T(8,128)(2,1)}, u32[]{:S(2)}, u32[]{:S(2)}) collective-permute-start(bf16[1024,128]{1,0:T(8,128)(2,1)} %shard_map.152.mine), channel_id=1, source_target_pairs={{0,1},{1,0},{2,3},{3,2},{4,5},{5,4},{6,7},{7,6},{8,9},{9,8},{10,11... | collective-permute-start | bytes 786440 | tf_op jit(solution)/shard_map/ppermute | solution.py:564
  134.6 3.6 %collective-permute-start.17 = (f32[6,4,512]{2,1,0:T(4,128)}, f32[6,4,512]{2,1,0:T(4,128)}, u32[]{:S(2)}, u32[]{:S(2)}) collective-permute-start(f32[6,4,512]{2,1,0:T(4,128)} %get-tuple-element.38), channel_id=1, source_target_pairs={{0,128},{128,0},{1,129},{129,1},{2,130},{130,2},{3,131},{131,3},{4... | collective-permute-start | bytes 147464 | tf_op jit(solution)/shard_map/ppermute | solution.py:731
